TPU v7x, 32 devices: a whole 2x2x4 slice. The times are simulated.
32 devices in a mesh: groups: 2 (over y), section: 4 (over x, core), tp: 4 (over z).
Axes of the slice: x: 2, y: 2, z: 4, core: 2. Of those that a mesh axis runs over, the one named last changes fastest.
Arguments:
- step_token_states: bfloat16 [4, 64, 8192], P(None, ('groups', 'section')), parts along dimension 1, may hold values from -6 to 6
- input_norm_gain: bfloat16 [8192], replicated, may hold values from 0.099609375 to 1.8984375
- wq: bfloat16 [8192, 8192], P(None, 'tp'), may hold values from -0.0625 to 0.0625
- wkv: bfloat16 [8192, 2048], P(None, 'tp'), may hold values from -0.25 to 0.25
- wo: bfloat16 [8192, 8192], P('tp'), may hold values from -0.0625 to 0.0625
- adapter_down: bfloat16 [32, 8192, 128], P(('groups', 'section'), 'tp'), parts along dimension 0, may hold values from -0.0625 to 0.0625
- adapter_up: bfloat16 [32, 128, 8192], P(('groups', 'section'), None, 'tp'), parts along dimension 0, may hold values from -0.375 to 0.375
- prompt_cache_pool: bfloat16 [64, 2, 2048, 1024], P('groups', None, 'section', 'tp'), parts along dimension 0, may hold values from -1100 to 1100
- prompt_slot: int32 [64], P('groups'), parts along dimension 0, may hold values from 0 to 31, each once
- prompt_cache_length: int32 [64], P('groups'), parts along dimension 0, may hold values from 512 to 2044, as said below
- slot_adapter: int32 [64], P('groups'), parts along dimension 0, may hold values from 0 to 15
- adapter_ranks: int32 [32], P('groups'), parts along dimension 0, may hold values from 8 to 128, as said below
Outputs:
- block_output: bfloat16 [4, 64, 8192], P(None, ('groups', 'section')), parts along dimension 1
There are 2 independent parts, one for each index of `groups`. A program takes and returns all parts, laid end to end along the dimension named above; an argument that names none is the same for every part. Nothing has to cross between parts.
Inputs may be any that keep to these rules, and one draw needn't show every extreme that they name: `prompt_cache_length`: some prompt has 2044 cached tokens. `adapter_ranks`: some adapter has rank 128 and some rank 8.
All inputs are finite; a program needn't handle non-finite values.
Results may differ from a plain program's by a relative error of at most 0.013.
The roundings to bfloat16 on the way count: a program that leaves them out, or rounds other values in their place, can miss the bound.
Values may be sent and summed in bfloat16 or wider, within the bound.
No kernel may reach another device: no remote copies, remote signals or barrier semaphores. Data moves between devices by JAX's collectives and lax.ppermute only.
A program may use at most 320 MiB of HBM per device.

v0:
```python
import math

import jax
import jax.numpy as jnp
from jax import lax
from jax.sharding import PartitionSpec as P

QUERY_HEADS = 64
KVH = 8
HEAD_DIM = 128


EPSILON = 1e-05
ROPE_BASE = 500000.0
ADAPTER_ALPHA = 16.0
NEGATIVE = -1e30


def merged(part, axis, combine):
    gathered = jax.tree.map(lambda a: lax.all_gather(a, axis), part)

    def take(source):
        return jax.tree.map(lambda a: lax.dynamic_index_in_dim(a, source, 0, False), gathered)

    return lax.fori_loop(
        1, lax.axis_size(axis), lambda source, state: combine(state, take(source)), take(0)
    )


def apply_rotary(vectors, positions):
    half_dim = vectors.shape[-1] // 2
    exponents = jnp.arange(half_dim, dtype=jnp.float32) * (2.0 / vectors.shape[-1])
    frequency = ROPE_BASE ** (-exponents)
    angles = positions.astype(jnp.float32)[:, None] * frequency[None, :]
    cosine = jnp.cos(angles)[:, None, :]
    sine = jnp.sin(angles)[:, None, :]
    first_half = vectors[..., :half_dim]
    second_half = vectors[..., half_dim:]
    return jnp.concatenate(
        [first_half * cosine - second_half * sine, second_half * cosine + first_half * sine],
        axis=-1,
    )


def normalize(hidden_rows, input_norm_gain):
    values_f32 = hidden_rows.astype(jnp.float32)
    inverse = lax.rsqrt(jnp.mean(values_f32 * values_f32, axis=-1, keepdims=True) + EPSILON)
    return (values_f32 * inverse * input_norm_gain.astype(jnp.float32)).astype(jnp.bfloat16)


def attend(grouped, kv_cache, positions, lengths, stacked_keys, stacked_values, fresh_valid):
    root_dim = math.sqrt(grouped.shape[-1])
    is_valid = (positions[None, :] < lengths[:, None])[:, None, None, :]
    old_scores = (
        jnp.einsum("rkgd,rtkd->rkgt", grouped, kv_cache[:, 0], preferred_element_type=jnp.float32)
        / root_dim
    )
    new_scores = (
        jnp.einsum("rkgd,srkd->rkgs", grouped, stacked_keys, preferred_element_type=jnp.float32)
        / root_dim
    )
    old_top = jnp.max(jnp.where(is_valid, old_scores, NEGATIVE), axis=-1)
    new_top = jnp.max(jnp.where(fresh_valid, new_scores, NEGATIVE), axis=-1)
    row_top = jnp.maximum(old_top, new_top)
    old_weights = jnp.where(is_valid, jnp.exp(old_scores - row_top[..., None]), 0.0)
    new_weights = jnp.where(fresh_valid, jnp.exp(new_scores - row_top[..., None]), 0.0)
    row_total = jnp.sum(old_weights, axis=-1) + jnp.sum(new_weights, axis=-1)
    weighted = jnp.einsum(
        "rkgt,rtkd->rkgd",
        old_weights.astype(jnp.bfloat16),
        kv_cache[:, 1],
        preferred_element_type=jnp.float32,
    )
    weighted = weighted + jnp.einsum(
        "rkgs,srkd->rkgd",
        new_weights.astype(jnp.bfloat16),
        stacked_values,
        preferred_element_type=jnp.float32,
    )
    return (row_top, row_total, weighted)


def combine(earlier, later):
    row_top = jnp.maximum(earlier[0], later[0])
    scale_one = jnp.exp(earlier[0] - row_top)
    scale_two = jnp.exp(later[0] - row_top)
    row_total = earlier[1] * scale_one + later[1] * scale_two
    weighted = earlier[2] * scale_one[..., None] + later[2] * scale_two[..., None]
    return (row_top, row_total, weighted)


def per_device(
    step_token_states,
    input_norm_gain,
    wq,
    wkv,
    wo,
    adapter_down,
    adapter_up,
    prompt_cache_pool,
    prompt_slot,
    prompt_cache_length,
    slot_adapter,
    adapter_ranks,
):
    sections = lax.axis_size("section")
    tp_width = lax.axis_size("tp")
    section_id = lax.axis_index("section")
    tp_id = lax.axis_index("tp")
    step_count, slot_row_index, model_width = step_token_states.shape
    request_list = prompt_slot.shape[0]
    section_tokens = prompt_cache_pool.shape[2]
    cols_dev = prompt_cache_pool.shape[3]
    sub_len = section_tokens // tp_width
    local_heads = QUERY_HEADS // tp_width
    per_kv = QUERY_HEADS // KVH
    kv_cols = KVH * HEAD_DIM
    owners = (
        jnp.zeros((request_list,), jnp.int32)
        .at[prompt_slot]
        .set(jnp.arange(request_list, dtype=jnp.int32))
    )
    own_owners = lax.dynamic_slice_in_dim(owners, section_id * slot_row_index, slot_row_index)
    lengths = prompt_cache_length[own_owners]
    own_ids = lax.dynamic_slice_in_dim(slot_adapter, section_id * slot_row_index, slot_row_index)
    all_a, all_b = (
        lax.all_gather(adapter_down, "section", axis=0, tiled=True),
        lax.all_gather(adapter_up, "section", axis=0, tiled=True),
    )
    chosen_down = all_a[own_ids]
    chosen_up = all_b[own_ids]
    rank_entries = adapter_ranks[own_ids]
    valid_rank_mask = jnp.arange(chosen_down.shape[2])[None, :] < rank_entries[:, None]
    adapter_scale = ADAPTER_ALPHA / rank_entries.astype(jnp.float32)
    by_slot = prompt_cache_pool[owners].reshape(
        sections, slot_row_index, 2, tp_width, sub_len, cols_dev
    )
    outgoing = by_slot.transpose(0, 3, 1, 2, 4, 5)
    flat_out = outgoing.reshape(sections * tp_width, slot_row_index, 2, sub_len, cols_dev)
    arrived = lax.all_to_all(flat_out, ("section", "tp"), split_axis=0, concat_axis=0, tiled=True)
    arrived = arrived.reshape(sections, tp_width, slot_row_index, 2, sub_len, cols_dev)
    kv_cache = arrived.transpose(2, 3, 0, 4, 1, 5).reshape(
        slot_row_index, 2, sections * sub_len, KVH, HEAD_DIM
    )
    token_order = jnp.arange(sections * sub_len, dtype=jnp.int32)
    positions = token_order // sub_len * section_tokens + tp_id * sub_len + token_order % sub_len
    slice_cols = model_width // tp_width
    fresh_keys = []
    fresh_values = []
    results = []
    for step_index in range(step_count):
        normed = normalize(step_token_states[step_index], input_norm_gain)
        plain_query = jnp.dot(normed, wq, preferred_element_type=jnp.float32)
        kv_part = jnp.dot(normed, wkv, preferred_element_type=jnp.float32)
        local_rows = lax.dynamic_slice_in_dim(normed, tp_id * slice_cols, slice_cols, 1)
        rank_part = jnp.einsum(
            "rd,rdk->rk", local_rows, chosen_down, preferred_element_type=jnp.float32
        )
        widened = jnp.zeros((slot_row_index, 2 * kv_cols), jnp.float32)
        widened = lax.dynamic_update_slice_in_dim(widened, kv_part, tp_id * kv_part.shape[1], 1)
        rank_products_sum, kv_full = lax.psum((rank_part, widened), "tp")
        reduced_rank_state = jnp.where(
            valid_rank_mask, rank_products_sum * adapter_scale[:, None], 0.0
        ).astype(jnp.bfloat16)
        adapter_change = jnp.einsum(
            "vf,vfs->vs", reduced_rank_state, chosen_up, preferred_element_type=jnp.float32
        )
        current_position = lengths + step_index
        query_rows = apply_rotary(
            (plain_query + adapter_change).reshape(slot_row_index, local_heads, HEAD_DIM),
            current_position,
        ).astype(jnp.bfloat16)
        new_key = apply_rotary(
            kv_full[:, :kv_cols].reshape(slot_row_index, KVH, HEAD_DIM), current_position
        ).astype(jnp.bfloat16)
        new_value = kv_full[:, kv_cols:].reshape(slot_row_index, KVH, HEAD_DIM).astype(jnp.bfloat16)
        fresh_keys.append(new_key)
        fresh_values.append(new_value)
        stacked_keys = jnp.stack(fresh_keys)
        stacked_values = jnp.stack(fresh_values)
        gathered = lax.all_gather(
            query_rows.reshape(slot_row_index, local_heads * HEAD_DIM), "tp", axis=1, tiled=True
        )
        grouped = gathered.reshape(slot_row_index, KVH, per_kv, HEAD_DIM)
        row_top, row_total, weighted = attend(
            grouped, kv_cache, positions, lengths, stacked_keys, stacked_values, tp_id == 0
        )
        top_all = row_top.reshape(slot_row_index, QUERY_HEADS)
        total_all = row_total.reshape(slot_row_index, QUERY_HEADS)
        weighted_all = weighted.reshape(slot_row_index, QUERY_HEADS, HEAD_DIM)
        top_all, total_all, weighted_all = merged((top_all, total_all, weighted_all), "tp", combine)
        my_heads = tp_id * local_heads
        heads_out = (
            lax.dynamic_slice_in_dim(weighted_all, my_heads, local_heads, 1)
            / lax.dynamic_slice_in_dim(total_all, my_heads, local_heads, 1)[..., None]
        )
        attended = heads_out.reshape(slot_row_index, local_heads * HEAD_DIM).astype(jnp.bfloat16)
        partial_out = jnp.dot(attended, wo, preferred_element_type=jnp.float32)
        results.append(lax.psum(partial_out.astype(jnp.bfloat16), "tp"))
    return jnp.stack(results)


def solution(mesh):
    return jax.shard_map(
        per_device,
        mesh=mesh,
        in_specs=(
            P(None, ("groups", "section"), None),
            P(),
            P(None, "tp"),
            P(None, "tp"),
            P("tp", None),
            P(("groups", "section"), "tp", None),
            P(("groups", "section"), None, "tp"),
            P("groups", None, "section", "tp"),
            P("groups"),
            P("groups"),
            P("groups"),
            P("groups"),
        ),
        out_specs=P(None, ("groups", "section"), None),
        check_vma=False,
    )
```

profile of v0, /device:TPU:0, one launch (start us, length us, event | category | flops | bytes accessed | tf_op | source)
XLA Modules:
  0.0 876.5 jit_solution(1596579600646713615)
XLA Ops:
  22.2 14.8 %gather_fusion.4 = bf16[32,2,512,256]{3,2,1,0:T(8,128)(2,1)} fusion(bf16[32,2,512,256]{3,2,1,0:T(8,128)(2,1)} %param.27, s32[1024]{0:T(1024)S(1)} %pad_clamp_fusion), kind=kCustom, calls=%fused_computation.4 | custom fusion | bytes 33554560 | tf_op jit(solution)/shard_map/gather | solution.py:135
  37.0 14.6 %copy.57 = bf16[4,4,8,2,128,256]{5,4,3,2,1,0:T(8,128)(2,1)} copy(bf16[4,4,8,2,128,256]{5,4,1,3,2,0:T(8,128)(2,1)} %bitcast.346) | data formatting | bytes 33554432 | tf_op jit(solution)/shard_map/transpose | solution.py:138
  51.6 7.5 all-to-all-start
  71.6 137.4 %all-gather.9.cloned.1.call-done = bf16[16,128,2048]{2,1,0:T(8,128)(2,1)} async-done(((bf16[4,128,2048]{2,1,0:T(8,128)(2,1)}), bf16[16,128,2048]{2,1,0:T(8,128)(2,1)}) %all-gather.9.cloned.1.call-update) | async-done | bytes 8388624 | tf_op jit(solution)/shard_map/all_gather | solution.py:128
  208.9 6.3 gather_fusion.3
  215.2 82.1 %all-gather.7.cloned.1.call-done = bf16[16,2048,128]{2,1,0:T(8,128)(2,1)} async-done(((bf16[4,2048,128]{2,1,0:T(8,128)(2,1)}), bf16[16,2048,128]{2,1,0:T(8,128)(2,1)}) %all-gather.7.cloned.1.call-update) | async-done | bytes 8388624 | tf_op jit(solution)/shard_map/all_gather | solution.py:127
  297.3 6.5 gather_fusion.2
  311.1 120.1 %all-reduce = (f32[8,128]{1,0:T(8,128)S(1)}, f32[8,128]{1,0:T(8,128)S(1)}, f32[8,128]{1,0:T(8,128)S(1)}, f32[8,128]{1,0:T(8,128)S(1)}) all-reduce(f32[8,128]{1,0:T(8,128)S(1)} %bitcast.364, f32[8,128]{1,0:T(8,128)S(1)} %bitcast.365, f32[8,128]{1,0:T(8,128)S(1)} %bitcast.366, ...), channel_id=1, replica_groups=mesh['groups'=2,'section'=4,'tp'=4] {'tp'}, use_global_device_ids=true, to_apply=%region_2.3 | all-reduce | flops 4096 | bytes 32768 | tf_op jit(solution)/shard_map/psum | solution.py:161
  434.1 13.0 %fusion.33 = f32[8,16,128]{2,0,1:T(8,128)S(1)} fusion(bf16[8,8192]{1,0:T(8,128)(2,1)S(1)} %get-tuple-element.823, bf16[8192,2048]{1,0:T(8,128)(2,1)} %param.22, f32[8,1,2048]{2,1,0:T(1,128)S(1)} %fusion.185), kind=kOutput, calls=%fused_computation.75 | convolution fusion | flops 268451840 | bytes 33816576 | tf_op jit(solution)/shard_map/dot_general | solution.py:153
  447.3 13.4 %all_gather.56 = bf16[8,8192]{1,0:T(8,128)(2,1)S(1)} all-gather(bf16[8,2048]{1,0:T(8,128)(2,1)S(1)} %maximum_bitcast_fusion), channel_id=1, replica_groups=mesh['groups'=2,'section'=4,'tp'=4] {'tp'}, dimensions={1}, use_global_device_ids=true | all-gather | bytes 163840 | tf_op jit(solution)/shard_map/all_gather | solution.py:181
  461.3 12.8 %fusion.35 = f32[8,16,128]{2,0,1:T(8,128)S(1)} fusion(bf16[8,8192]{1,0:T(8,128)(2,1)S(1)} %get-tuple-element.822, bf16[8192,2048]{1,0:T(8,128)(2,1)} %param.22, f32[8,1,2048]{2,1,0:T(1,128)S(1)} %fusion.181), kind=kOutput, calls=%fused_computation.77 | convolution fusion | flops 268451840 | bytes 33816576 | tf_op jit(solution)/shard_map/dot_general | solution.py:153
  474.3 13.3 %all_gather.64 = bf16[8,8192]{1,0:T(8,128)(2,1)S(1)} all-gather(bf16[8,2048]{1,0:T(8,128)(2,1)S(1)} %maximum_bitcast_fusion.2), channel_id=1, replica_groups=mesh['groups'=2,'section'=4,'tp'=4] {'tp'}, dimensions={1}, use_global_device_ids=true | all-gather | bytes 163840 | tf_op jit(solution)/shard_map/all_gather | solution.py:181
  488.3 12.8 %fusion.36 = f32[8,16,128]{2,0,1:T(8,128)S(1)} fusion(bf16[8,8192]{1,0:T(8,128)(2,1)S(1)} %get-tuple-element.820, bf16[8192,2048]{1,0:T(8,128)(2,1)} %param.22, f32[8,1,2048]{2,1,0:T(1,128)S(1)} %fusion.179), kind=kOutput, calls=%fused_computation.78 | convolution fusion | flops 268451840 | bytes 33816576 | tf_op jit(solution)/shard_map/dot_general | solution.py:153
  501.3 13.8 %all_gather.68 = bf16[8,8192]{1,0:T(8,128)(2,1)S(1)} all-gather(bf16[8,2048]{1,0:T(8,128)(2,1)S(1)} %maximum_bitcast_fusion.3), channel_id=1, replica_groups=mesh['groups'=2,'section'=4,'tp'=4] {'tp'}, dimensions={1}, use_global_device_ids=true | all-gather | bytes 163840 | tf_op jit(solution)/shard_map/all_gather | solution.py:181
  515.7 12.8 %fusion.34 = f32[8,16,128]{2,0,1:T(8,128)S(1)} fusion(bf16[8,8192]{1,0:T(8,128)(2,1)S(1)} %get-tuple-element.821, bf16[8192,2048]{1,0:T(8,128)(2,1)} %param.22, f32[8,1,2048]{2,1,0:T(1,128)S(1)} %fusion.183), kind=kOutput, calls=%fused_computation.76 | convolution fusion | flops 268451840 | bytes 33816576 | tf_op jit(solution)/shard_map/dot_general | solution.py:153
  528.8 13.3 %all_gather.60 = bf16[8,8192]{1,0:T(8,128)(2,1)S(1)} all-gather(bf16[8,2048]{1,0:T(8,128)(2,1)S(1)} %maximum_bitcast_fusion.1), channel_id=1, replica_groups=mesh['groups'=2,'section'=4,'tp'=4] {'tp'}, dimensions={1}, use_global_device_ids=true | all-gather | bytes 163840 | tf_op jit(solution)/shard_map/all_gather | solution.py:181
  547.4 20.1 %copy.222 = bf16[4,4,8,2,128,256]{5,1,4,0,3,2:T(4,128)(2,1)} copy(bf16[4,4,8,2,128,256]{5,4,3,2,1,0:T(8,128)(2,1)} %bitcast.24) | data formatting | bytes 33554432 | tf_op jit(solution)/shard_map/reshape | solution.py:141
  567.5 24.9 %reshape.745 = bf16[8,2,512,8,128]{4,3,2,1,0:T(8,128)(2,1)} reshape(bf16[8,2,4,128,4,256]{5,4,3,2,1,0:T(4,128)(2,1)} %bitcast.347) | data formatting | bytes 33554432 | tf_op jit(solution)/shard_map/reshape | solution.py:142
  592.4 9.2 %fusion.221 = (bf16[8,1,512,8,128]{4,3,2,1,0:T(8,128)(2,1)}, bf16[8,1,512,8,128]{4,3,2,1,0:T(8,128)(2,1)S(1)}) fusion(bf16[8,2,512,8,128]{4,3,2,1,0:T(8,128)(2,1)} %reshape.745), kind=kLoop, calls=%fused_computation.376 | loop fusion | bytes 33554432 | tf_op jit(solution)/shard_map/slice | solution.py:71
  626.6 13.4 %all_gather.69 = f32[4,8,64]{2,1,0:T(8,128)S(1)} all-gather(f32[1,8,64]{2,1,0:T(8,128)S(1)} %max.113), channel_id=1, replica_groups=mesh['groups'=2,'section'=4,'tp'=4] {'tp'}, dimensions={0}, use_global_device_ids=true | all-gather | bytes 10240 | tf_op jit(solution)/shard_map/all_gather | solution.py:20
  640.0 13.2 %all_gather.70 = f32[4,8,64]{2,1,0:T(8,128)S(1)} all-gather(f32[1,8,64]{2,1,0:T(8,128)S(1)} %add.524), channel_id=1, replica_groups=mesh['groups'=2,'section'=4,'tp'=4] {'tp'}, dimensions={0}, use_global_device_ids=true | all-gather | bytes 10240 | tf_op jit(solution)/shard_map/all_gather | solution.py:20
  661.1 13.2 %all_gather.65 = f32[4,8,64]{2,1,0:T(8,128)S(1)} all-gather(f32[1,8,64]{2,1,0:T(8,128)S(1)} %max.111), channel_id=1, replica_groups=mesh['groups'=2,'section'=4,'tp'=4] {'tp'}, dimensions={0}, use_global_device_ids=true | all-gather | bytes 10240 | tf_op jit(solution)/shard_map/all_gather | solution.py:20
  674.3 13.2 %all_gather.66 = f32[4,8,64]{2,1,0:T(8,128)S(1)} all-gather(f32[1,8,64]{2,1,0:T(8,128)S(1)} %add.516), channel_id=1, replica_groups=mesh['groups'=2,'section'=4,'tp'=4] {'tp'}, dimensions={0}, use_global_device_ids=true | all-gather | bytes 10240 | tf_op jit(solution)/shard_map/all_gather | solution.py:20
  694.7 13.1 %all_gather.61 = f32[4,8,64]{2,1,0:T(8,128)S(1)} all-gather(f32[1,8,64]{2,1,0:T(8,128)S(1)} %max.109), channel_id=1, replica_groups=mesh['groups'=2,'section'=4,'tp'=4] {'tp'}, dimensions={0}, use_global_device_ids=true | all-gather | bytes 10240 | tf_op jit(solution)/shard_map/all_gather | solution.py:20
  707.9 13.3 %all_gather.62 = f32[4,8,64]{2,1,0:T(8,128)S(1)} all-gather(f32[1,8,64]{2,1,0:T(8,128)S(1)} %add.508), channel_id=1, replica_groups=mesh['groups'=2,'section'=4,'tp'=4] {'tp'}, dimensions={0}, use_global_device_ids=true | all-gather | bytes 10240 | tf_op jit(solution)/shard_map/all_gather | solution.py:20
  721.1 13.1 %all_gather.57 = f32[4,8,64]{2,1,0:T(8,128)S(1)} all-gather(f32[1,8,64]{2,1,0:T(8,128)S(1)} %max.107), channel_id=1, replica_groups=mesh['groups'=2,'section'=4,'tp'=4] {'tp'}, dimensions={0}, use_global_device_ids=true | all-gather | bytes 10240 | tf_op jit(solution)/shard_map/all_gather | solution.py:20
  734.2 13.1 %all_gather.58 = f32[4,8,64]{2,1,0:T(8,128)S(1)} all-gather(f32[1,8,64]{2,1,0:T(8,128)S(1)} %add.499), channel_id=1, replica_groups=mesh['groups'=2,'section'=4,'tp'=4] {'tp'}, dimensions={0}, use_global_device_ids=true | all-gather | bytes 10240 | tf_op jit(solution)/shard_map/all_gather | solution.py:20
  765.0 13.6 %fusion.15 = bf16[1,8,8192]{2,1,0:T(8,128)(2,1)} fusion(bf16[2048,8192]{1,0:T(8,128)(2,1)} %param.24, bf16[1,8,16,128]{3,2,1,0:T(8,128)(2,1)S(1)} %fusion.170), kind=kOutput, calls=%fused_computation.46 | convolution fusion | flops 268500992 | bytes 33718272 | tf_op jit(solution)/shard_map/dot_general | solution.py:198
  778.8 13.5 %fusion.14 = bf16[1,8,8192]{2,1,0:T(8,128)(2,1)} fusion(bf16[2048,8192]{1,0:T(8,128)(2,1)} %param.24, bf16[1,8,16,128]{3,2,1,0:T(8,128)(2,1)S(1)} %fusion.169), kind=kOutput, calls=%fused_computation.45 | convolution fusion | flops 268500992 | bytes 33718272 | tf_op jit(solution)/shard_map/dot_general | solution.py:198
  797.2 13.5 %fusion.13 = bf16[1,8,8192]{2,1,0:T(8,128)(2,1)} fusion(bf16[2048,8192]{1,0:T(8,128)(2,1)} %param.24, bf16[1,8,16,128]{3,2,1,0:T(8,128)(2,1)S(1)} %fusion.168), kind=kOutput, calls=%fused_computation.44 | convolution fusion | flops 268500992 | bytes 33718272 | tf_op jit(solution)/shard_map/dot_general | solution.py:198
  815.6 13.5 %fusion.12 = bf16[1,8,8192]{2,1,0:T(8,128)(2,1)} fusion(bf16[2048,8192]{1,0:T(8,128)(2,1)} %param.24, bf16[1,8,16,128]{3,2,1,0:T(8,128)(2,1)S(1)} %fusion.167), kind=kOutput, calls=%fused_computation.43 | convolution fusion | flops 268500992 | bytes 33718272 | tf_op jit(solution)/shard_map/dot_general | solution.py:198
  829.1 37.6 %all-reduce.8.cloned.1.call-done = (bf16[1,8,8192]{2,1,0:T(8,128)(2,1)}, bf16[1,8,8192]{2,1,0:T(8,128)(2,1)}, bf16[1,8,8192]{2,1,0:T(8,128)(2,1)}, bf16[1,8,8192]{2,1,0:T(8,128)(2,1)}) async-done(((bf16[1,8,8192]{2,1,0:T(8,128)(2,1)}, bf16[1,8,8192]{2,1,0:T(8,128)(2,1)}, bf16[1,8,8192]{2,1,0:T(8,128)(2,1)}, bf16[1,8,8192]{2,1,0:T(8,128)(2,1)}), (bf16[1,8,8192]{2,1,0:T(8,128)(2,1)}, ...) | async-done | bytes 524304 | tf_op jit(solution)/shard_map/psum | solution.py:199
  (250 shorter events, 131.1 us)
Async XLA Ops:
  7.4 52.5 %copy-start = (s32[32]{0:T(128)S(1)}, s32[32]{0:T(128)}, u32[]{:S(2)}) copy-start(s32[32]{0:T(128)} %param.29) | copy-start | bytes 388
  7.4 54.3 %all-reduce.6.cloned.1.call-start = ((), (), s32[]{:S(2)}) async-start(), calls=%async_computation.7 | async-start | bytes 524288 | tf_op jit(solution)/shard_map/psum | solution.py:161
  10.8 4.8 slice-start
  10.8 5.9 slice-start.1
  20.9 188.0 %all-gather.9.cloned.1.call-start = ((), (), s32[]{:S(2)}) async-start(), calls=%async_computation.2 | async-start | bytes 10485760 | tf_op jit(solution)/shard_map/all_gather | solution.py:128
  51.6 8.9 %copy-start.28 = (s32[32]{0:T(128)S(1)}, s32[32]{0:T(128)}, u32[]{:S(2)}) copy-start(s32[32]{0:T(128)} %param.30) | copy-start | bytes 388
  51.6 9.0 %copy-start.2 = (s32[16]{0:T(128)S(1)}, s32[16]{0:T(128)}, u32[]{:S(2)}) copy-start(s32[16]{0:T(128)} %param.31) | copy-start | bytes 196
  51.6 495.8 %all-to-all-start = ((bf16[16,8,2,128,256]{4,3,2,1,0:T(8,128)(2,1)}), bf16[16,8,2,128,256]{4,3,2,1,0:T(8,128)(2,1)}, u32[]{:S(2)}, u32[]{:S(2)}) async-start(bf16[16,8,2,128,256]{4,3,2,1,0:T(8,128)(2,1)} %bitcast.345), calls=%async_computation | async-start | bytes 33554432 | tf_op jit(solution)/shard_map/all_to_all | solution.py:140
  59.2 238.2 %all-gather.7.cloned.1.call-start = ((), (), s32[]{:S(2)}) async-start(), calls=%async_computation.1 | async-start | bytes 10485760 | tf_op jit(solution)/shard_map/all_gather | solution.py:127
  59.8 693.4 %all-gather.17.cloned.1.call-start = ((), (), s32[]{:S(2)}) async-start(), calls=%async_computation.6 | async-start | bytes 1310720 | tf_op jit(solution)/shard_map/all_gather | solution.py:20
  303.9 5.9 copy-start.4
  434.1 26.5 %copy-start.3 = (bf16[8,128,2048]{2,1,0:T(8,128)(2,1)S(1)}, bf16[8,128,2048]{2,1,0:T(8,128)(2,1)}, u32[]{:S(2)}) copy-start(bf16[8,128,2048]{2,1,0:T(8,128)(2,1)} %gather_fusion.3) | copy-start | bytes 12582916
  608.7 4.8 copy-start.26
  609.3 10.9 %copy-start.7 = (bf16[1,8,8,128]{3,0,2,1:T(2,128)(2,1)S(1)}, bf16[1,8,8,128]{3,0,2,1:T(2,128)(2,1)}, u32[]{:S(2)}) copy-start(bf16[1,8,8,128]{3,0,2,1:T(2,128)(2,1)} %convert_element_type.312) | copy-start | bytes 49156
  609.3 10.9 %copy-start.9 = (bf16[1,8,8,128]{3,0,2,1:T(2,128)(2,1)S(1)}, bf16[1,8,8,128]{3,0,2,1:T(2,128)(2,1)}, u32[]{:S(2)}) copy-start(bf16[1,8,8,128]{3,0,2,1:T(2,128)(2,1)} %convert_element_type.311) | copy-start | bytes 49156
  613.5 6.7 copy-start.6
  613.6 6.6 copy-start.13
  613.6 6.6 copy-start.23
  621.2 37.5 %copy-start.8 = (bf16[1,8,8,128]{3,0,2,1:T(2,128)(2,1)S(1)}, bf16[1,8,8,128]{3,0,2,1:T(2,128)(2,1)}, u32[]{:S(2)}) copy-start(bf16[1,8,8,128]{3,0,2,1:T(2,128)(2,1)} %convert_element_type.312) | copy-start | bytes 49156
  621.2 37.5 %copy-start.10 = (bf16[1,8,8,128]{3,0,2,1:T(2,128)(2,1)S(1)}, bf16[1,8,8,128]{3,0,2,1:T(2,128)(2,1)}, u32[]{:S(2)}) copy-start(bf16[1,8,8,128]{3,0,2,1:T(2,128)(2,1)} %convert_element_type.311) | copy-start | bytes 49156
  621.2 37.6 %copy-start.14 = (bf16[1,8,8,128]{3,0,2,1:T(2,128)(2,1)S(1)}, bf16[1,8,8,128]{3,0,2,1:T(2,128)(2,1)}, u32[]{:S(2)}) copy-start(bf16[1,8,8,128]{3,0,2,1:T(2,128)(2,1)} %convert_element_type.313) | copy-start | bytes 49156
  621.3 66.3 %copy-start.12 = (f32[8,8,8]{2,1,0:T(8,128)S(1)}, f32[8,8,8]{2,1,0:T(8,128)}, u32[]{:S(2)}) copy-start(f32[8,8,8]{2,1,0:T(8,128)} %copy-done.11) | copy-start | bytes 6148
  621.3 138.7 %all-gather.15.cloned.1.call-start = ((), (), s32[]{:S(2)}) async-start(), calls=%async_computation.5 | async-start | bytes 1310720 | tf_op jit(solution)/shard_map/all_gather | solution.py:20
  625.7 62.7 %copy-start.5 = (f32[8,8,8,512]{3,2,1,0:T(8,128)S(1)}, f32[8,8,8,512]{3,2,1,0:T(8,128)}, u32[]{:S(2)}) copy-start(f32[8,8,8,512]{3,2,1,0:T(8,128)} %get-tuple-element.866) | copy-start | bytes 3145732
  640.0 20.2 %copy-start.24 = (f32[4,8,64]{2,1,0:T(8,128)}, f32[4,8,64]{2,1,0:T(8,128)S(1)}, u32[]{:S(2)}) copy-start(f32[4,8,64]{2,1,0:T(8,128)S(1)} %all_gather.69) | copy-start | bytes 24580
  658.8 34.5 %copy-start.15 = (f32[8,8,8,2]{2,3,1,0:T(2,128)S(1)}, f32[8,8,8,2]{2,3,1,0:T(2,128)}, u32[]{:S(2)}) copy-start(f32[8,8,8,2]{2,3,1,0:T(2,128)} %get-tuple-element.870) | copy-start | bytes 12292
  658.8 35.8 %copy-start.20 = (f32[8,8,8]{2,1,0:T(8,128)S(1)}, f32[8,8,8]{2,1,0:T(8,128)}, u32[]{:S(2)}) copy-start(f32[8,8,8]{2,1,0:T(8,128)} %get-tuple-element.729) | copy-start | bytes 6148
  658.8 88.6 %copy-start.21 = (f32[8,8,128]{2,1,0:T(8,128)S(1)}, f32[8,8,128]{2,1,0:T(8,128)}, u32[]{:S(2)}) copy-start(f32[8,8,128]{2,1,0:T(8,128)} %copy.61) | copy-start | bytes 98308
  659.9 132.4 %all-gather.13.cloned.1.call-start = ((), (), s32[]{:S(2)}) async-start(), calls=%async_computation.4 | async-start | bytes 1310720 | tf_op jit(solution)/shard_map/all_gather | solution.py:20
  694.4 116.3 %all-gather.11.cloned.1.call-start = ((), (), s32[]{:S(2)}) async-start(), calls=%async_computation.3 | async-start | bytes 1310720 | tf_op jit(solution)/shard_map/all_gather | solution.py:20
  753.1 113.6 %all-reduce.8.cloned.1.call-start = ((), (), s32[]{:S(2)}) async-start(), calls=%async_computation.8 | async-start | bytes 1048576 | tf_op jit(solution)/shard_map/psum | solution.py:199
  815.6 53.0 %copy-start.1 = (s32[32]{0:T(128)S(1)}, s32[32]{0:T(128)}, u32[]{:S(2)}) copy-start(s32[32]{0:T(128)} %param.29) | copy-start | bytes 388
  (8 other events, 16.2 us)
Sparse Core Ops, SparseCore 0:
  21.0 38.5 all-reduce.5
  621.4 26.6 all-gather.16
  660.0 26.8 all-gather.14
  694.5 26.6 all-gather.12
  753.2 26.2 all-gather.10
  829.3 37.3 all-reduce.7
Sparse Core Ops, SparseCore 1:
  23.0 185.9 all-gather.8
  210.5 86.8 all-gather.6
where the time goes:
time: 886 us; the launch traced here: 876 us
  blocking collectives  280 us (32%)
  waiting for transfers between devices  258 us (29%)
  matrix products  166 us (19%)
  local copies, waits for them, and re-layouts  115 us (13%)
  other arithmetic  33.6 us (4%)
  between operations  16 us (2%)
    all_gather x1, waiting for transfers between devices, per_device(): lax.all_gather(adapter_up, 'section', axis=0, tiled=True)  137 us
    psum x1, blocking collectives, per_device(): rank_products_sum, kv_full = lax.psum((rank_part, widened), 'tp')  120 us
    all_gather x8, blocking collectives, merged(): gathered = jax.tree.map(lambda a: lax.all_gather(a, axis), part)  106 us
    all_gather x1, waiting for transfers between devices, per_device(): lax.all_gather(adapter_down, 'section', axis=0, tiled=True)  82.1 us
    dot_general x4, matrix products, per_device(): partial_out = jnp.dot(attended, wo, preferred_element_type=jnp.float32)  54.1 us
    all_gather x4, blocking collectives, per_device(): lax.all_gather(query_rows.reshape(slot_row_index, local_heads * HEAD_DIM)...  53.8 us
    dot_general x4, matrix products, per_device(): plain_query = jnp.dot(normed, wq, preferred_element_type=jnp.float32)  51.4 us
    psum x1, waiting for transfers between devices, per_device(): results.append(lax.psum(partial_out.astype(jnp.bfloat16), 'tp'))  37.6 us
  transfers between devices with their start and end apart: 9, of which 3 were waited for; matrix products, arithmetic and copies ran while one was open for 24% of the time, Pallas kernels for 0%

commit v1 on v0

v1 whole, which is shorter than its diff:
```python
import functools
import math

import jax
import jax.numpy as jnp
from jax import lax
from jax.experimental import pallas as pl
from jax.experimental.pallas import tpu as pltpu
from jax.sharding import PartitionSpec as P

QUERY_HEADS = 64
KVH = 8
HEAD_DIM = 128
PER_KV = QUERY_HEADS // KVH

EPSILON = 1e-05
ROPE_BASE = 500000.0
ADAPTER_ALPHA = 16.0
NEGATIVE = -1e30
STAT_ROWS = 8
FRESH_ROWS = 16
F32 = jnp.float32
BF16 = jnp.bfloat16
VMEM = pl.BlockSpec(memory_space=pltpu.VMEM)
SMEM = pl.BlockSpec(memory_space=pltpu.SMEM)
ANYWHERE = pl.BlockSpec(memory_space=pl.ANY)


def params(mebibytes):
    return pltpu.CompilerParams(vmem_limit_bytes=mebibytes * 1024 * 1024)


def swap(value, axis, bit):
    size = lax.axis_size(axis)
    pairs = [(i, i ^ bit) for i in range(size)]
    return jax.tree.map(lambda a: lax.ppermute(a, axis, pairs), value)


def normalize(hidden_rows, input_norm_gain):
    values_f32 = hidden_rows.astype(F32)
    inverse = lax.rsqrt(jnp.mean(values_f32 * values_f32, axis=-1, keepdims=True) + EPSILON)
    return (values_f32 * inverse * input_norm_gain.astype(F32)).astype(BF16)


def rotary_tables(positions):
    half_dim = HEAD_DIM // 2
    exponents = jnp.arange(half_dim, dtype=F32) * (2.0 / HEAD_DIM)
    frequency = ROPE_BASE ** (-exponents)
    angles = positions.astype(F32)[:, None] * frequency[None, :]
    cosine, sine = jnp.cos(angles), jnp.sin(angles)
    return jnp.concatenate([cosine, cosine], -1), jnp.concatenate([-sine, sine], -1)


def down_kernel(own, across, beside, beside_across, pick, down, out):
    rows = own.shape[0]
    for position, ref in enumerate((own, beside, across, beside_across)):
        block = slice(position * rows, (position + 1) * rows)
        total = jnp.zeros((rows, down.shape[2]), F32)
        for a in range(down.shape[0]):
            product = jnp.dot(ref[...], down[a], preferred_element_type=F32)
            total = jnp.where(pick[block, a : a + 1] > 0, product, total)
        out[block, :] = total


def query_kernel(parts, scale, pick, up, own, across, beside, beside_across, cosine, sine, out):
    rank_sum = parts[0]
    for i in range(1, parts.shape[0]):
        rank_sum = rank_sum + parts[i]
    low_rank = jnp.where(scale[...] > 0, rank_sum * scale[...], 0.0)
    adapters = up.shape[0]
    wide = jnp.concatenate(
        [jnp.where(pick[:, a : a + 1] > 0, low_rank, 0.0) for a in range(adapters)], axis=1
    ).astype(BF16)
    up_rows = up.reshape(adapters * up.shape[1], up.shape[2])
    rows = own.shape[0]
    here = jnp.sum(pick[...], axis=1, keepdims=True) > 0
    for head in range(up.shape[2] // HEAD_DIM):
        cols = slice(head * HEAD_DIM, (head + 1) * HEAD_DIM)
        change = jnp.dot(wide, up_rows[:, cols], preferred_element_type=F32)
        plain = jnp.concatenate([ref[:, cols] for ref in (own, beside, across, beside_across)], 0)
        query = plain + change
        turned = query * cosine[...] + pltpu.roll(query, HEAD_DIM // 2, 1) * sine[...]
        out[:, cols] = jnp.where(here, turned, 0.0).astype(BF16)


def attend_kernel(fresh, steps, slots, kvl, owners, limits, qa, qb, nk, nv, cache, out, kv, qf, qs, sems):
    count = 2 * slots
    heads = qa.shape[1] // HEAD_DIM
    per_kv = heads // kvl
    rows = heads * steps
    tokens = cache.shape[2]
    root = 1.0 / math.sqrt(HEAD_DIM)

    def copy(i):
        return pltpu.make_async_copy(cache.at[owners[i]], kv.at[i], sems.at[i])

    for i in range(count):
        copy(i).start()
    qs[...] = jnp.zeros_like(qs)
    eye = lax.broadcasted_iota(jnp.int32, (rows, rows), 0) == lax.broadcasted_iota(
        jnp.int32, (rows, rows), 1
    )
    token = lax.broadcasted_iota(jnp.int32, (rows, tokens), 1)
    step_of_row = lax.broadcasted_iota(jnp.int32, (rows, FRESH_ROWS), 0) % steps
    fresh_valid = lax.broadcasted_iota(jnp.int32, (rows, FRESH_ROWS), 1) <= step_of_row
    for i in range(count):
        part, slot = divmod(i, slots)
        if slot == 0:
            for h in range(heads):
                qf[h] = (qa, qb)[part][:, h * HEAD_DIM : (h + 1) * HEAD_DIM].astype(F32)
        buf = i % 2
        for h in range(heads):
            k = h // per_kv
            qs[buf, h * steps : (h + 1) * steps, k * HEAD_DIM : (k + 1) * HEAD_DIM] = qf[
                h, pl.ds(slot, steps, stride=slots), :
            ]
        query = qs[buf].astype(BF16)
        copy(i).wait()
        nt = (((1,), (1,)), ((), ()))
        scores = lax.dot_general(query, kv[i, 0], nt, preferred_element_type=F32) * root
        valid = token < limits[i]
        scores = jnp.where(valid, scores, NEGATIVE)
        top = jnp.max(scores, axis=1, keepdims=True)
        with_fresh = fresh and part == 0
        if with_fresh:
            new_scores = lax.dot_general(query, nk[slot], nt, preferred_element_type=F32) * root
            new_scores = jnp.where(fresh_valid, new_scores, NEGATIVE)
            top = jnp.maximum(top, jnp.max(new_scores, axis=1, keepdims=True))
        weights = jnp.where(valid, jnp.exp(scores - top), 0.0)
        total = jnp.sum(weights, axis=1, keepdims=True)
        value = jnp.dot(weights.astype(BF16), kv[i, 1], preferred_element_type=F32)
        if with_fresh:
            new_weights = jnp.where(fresh_valid, jnp.exp(new_scores - top), 0.0)
            total = total + jnp.sum(new_weights, axis=1, keepdims=True)
            value = value + jnp.dot(new_weights.astype(BF16), nv[slot], preferred_element_type=F32)
        for k in range(kvl):
            block = slice(k * per_kv * steps, (k + 1) * per_kv * steps)
            out[i, block, :] = value[block, k * HEAD_DIM : (k + 1) * HEAD_DIM]
        out[i, rows : rows + 1, :rows] = jnp.sum(jnp.where(eye, top, 0.0), axis=0, keepdims=True)
        out[i, rows + 1 : rows + 2, :rows] = jnp.sum(jnp.where(eye, total, 0.0), axis=0, keepdims=True)


def merge_stats(a, b, i, rows):
    top_a, total_a = a[i, rows : rows + 1, :rows], a[i, rows + 1 : rows + 2, :rows]
    top_b, total_b = b[i, rows : rows + 1, :rows], b[i, rows + 1 : rows + 2, :rows]
    top = jnp.maximum(top_a, top_b)
    scale_a, scale_b = jnp.exp(top_a - top), jnp.exp(top_b - top)
    return top, total_a * scale_a + total_b * scale_b, scale_a, scale_b


def as_column(row, eye):
    return jnp.sum(jnp.where(eye, row, 0.0), axis=1, keepdims=True)


def merge_kernel(a, b, out):
    rows = a.shape[1] - STAT_ROWS
    eye = lax.broadcasted_iota(jnp.int32, (rows, rows), 0) == lax.broadcasted_iota(
        jnp.int32, (rows, rows), 1
    )
    for i in range(a.shape[0]):
        top, total, scale_a, scale_b = merge_stats(a, b, i, rows)
        out[i, :rows, :] = a[i, :rows, :] * as_column(scale_a, eye) + b[i, :rows, :] * as_column(scale_b, eye)
        out[i, rows : rows + 1, :rows] = top
        out[i, rows + 1 : rows + 2, :rows] = total


def finish_kernel(steps, a, b, out, wide):
    rows = a.shape[1] - STAT_ROWS
    slots = a.shape[0]
    eye = lax.broadcasted_iota(jnp.int32, (rows, rows), 0) == lax.broadcasted_iota(
        jnp.int32, (rows, rows), 1
    )
    for i in range(slots):
        _, total, scale_a, scale_b = merge_stats(a, b, i, rows)
        weighted = a[i, :rows, :] * as_column(scale_a, eye) + b[i, :rows, :] * as_column(scale_b, eye)
        weighted = weighted / as_column(total, eye)
        for h in range(rows // steps):
            wide[h, pl.ds(i, steps, stride=slots), :] = weighted[h * steps : (h + 1) * steps, :]
    for h in range(rows // steps):
        out[:, h * HEAD_DIM : (h + 1) * HEAD_DIM] = wide[h].astype(BF16)


def attend(fresh, steps, slots, kvl, owners, limits, queries, new_keys, new_values, cache):
    rows = queries[0].shape[1] // HEAD_DIM * steps
    count = 2 * slots
    tokens, columns = cache.shape[2:]
    return pl.pallas_call(
        functools.partial(attend_kernel, fresh, steps, slots, kvl),
        out_shape=jax.ShapeDtypeStruct((count, rows + STAT_ROWS, HEAD_DIM), F32),
        in_specs=[SMEM, SMEM, VMEM, VMEM, VMEM, VMEM, ANYWHERE],
        out_specs=VMEM,
        scratch_shapes=[
            pltpu.VMEM((count, 2, tokens, columns), BF16),
            pltpu.VMEM((rows // steps, queries[0].shape[0], HEAD_DIM), F32),
            pltpu.VMEM((2, rows, columns), F32),
            pltpu.SemaphoreType.DMA((count,)),
        ],
        compiler_params=params(32),
        cost_estimate=pl.CostEstimate(
            flops=count * 4 * rows * tokens * columns,
            bytes_accessed=count * 4 * tokens * columns,
            transcendentals=count * rows * tokens,
        ),
        name="attend",
    )(owners, limits, *queries, new_keys, new_values, cache)


def merge(a, b):
    return pl.pallas_call(
        merge_kernel,
        out_shape=jax.ShapeDtypeStruct(a.shape, F32),
        in_specs=[VMEM] * 2,
        out_specs=VMEM,
        name="merge",
    )(a, b)


def per_device(
    step_token_states,
    input_norm_gain,
    wq,
    wkv,
    wo,
    adapter_down,
    adapter_up,
    prompt_cache_pool,
    prompt_slot,
    prompt_cache_length,
    slot_adapter,
    adapter_ranks,
):
    sections = lax.axis_size("section")
    tp_width = lax.axis_size("tp")
    section_id = lax.axis_index("section")
    tp_id = lax.axis_index("tp")
    steps, slots, model_width = step_token_states.shape
    requests = prompt_slot.shape[0]
    section_tokens = prompt_cache_pool.shape[2]
    cols_dev = prompt_cache_pool.shape[3]
    adapters = adapter_down.shape[0]
    rank = adapter_down.shape[2]
    local_heads = QUERY_HEADS // tp_width
    kvl = max(1, local_heads // PER_KV)
    kv_start = tp_id * local_heads // PER_KV * HEAD_DIM
    rows = steps * slots
    slice_cols = model_width // tp_width
    assert sections == 4

    position_section = section_id ^ jnp.arange(sections, dtype=jnp.int32)
    slot_ids = (position_section[:, None] * slots + jnp.arange(slots, dtype=jnp.int32)).reshape(-1)
    owns = prompt_slot[None, :] == slot_ids[:, None]
    owners = jnp.sum(jnp.where(owns, jnp.arange(requests, dtype=jnp.int32), 0), axis=1)
    lengths = jnp.sum(jnp.where(owns, prompt_cache_length, 0), axis=1)
    slot_here = jnp.arange(requests, dtype=jnp.int32)[None, :] == slot_ids[:, None]
    adapter_of = jnp.sum(jnp.where(slot_here, slot_adapter, 0), axis=1)
    rank_is = jnp.arange(adapter_ranks.shape[0], dtype=jnp.int32)[None, :] == adapter_of[:, None]
    ranks = jnp.sum(jnp.where(rank_is, adapter_ranks, 0), axis=1)
    limits = jnp.clip(lengths - section_id * section_tokens, 0, section_tokens)

    def by_row(per_slot):
        wide = jnp.broadcast_to(
            per_slot.reshape((sections, 1, slots) + per_slot.shape[1:]),
            (sections, steps, slots) + per_slot.shape[1:],
        )
        return wide.reshape((sections * rows,) + per_slot.shape[1:])

    local = adapter_of - section_id * adapters
    pick = by_row((local[:, None] == jnp.arange(adapters, dtype=jnp.int32)).astype(F32))
    scale = jnp.where(
        jnp.arange(rank)[None, :] < ranks[:, None], ADAPTER_ALPHA / ranks.astype(F32)[:, None], 0.0
    )
    scale = by_row(scale)
    step_of = jnp.broadcast_to(
        jnp.arange(steps, dtype=jnp.int32)[None, :, None], (sections, steps, slots)
    ).reshape(-1)
    cosine, sine = rotary_tables(by_row(lengths) + step_of)

    normed = normalize(step_token_states, input_norm_gain).reshape(rows, model_width)
    piece = lax.dynamic_slice_in_dim(normed, tp_id * slice_cols, slice_cols, 1)
    piece_across = swap(piece, "section", 2)
    piece_beside, piece_beside_across = swap((piece, piece_across), "section", 1)

    plain = jnp.dot(normed, wq, preferred_element_type=F32)
    plain_across = swap(plain, "section", 2)
    plain_beside, plain_beside_across = swap((plain, plain_across), "section", 1)
    kv_part = jnp.dot(normed, wkv, preferred_element_type=F32)

    rank_part = pl.pallas_call(
        down_kernel,
        out_shape=jax.ShapeDtypeStruct((sections * rows, rank), F32),
        in_specs=[VMEM] * 6,
        out_specs=VMEM,
        name="down",
    )(piece, piece_across, piece_beside, piece_beside_across, pick, adapter_down)
    if tp_width <= 4:
        parts = jnp.stack([rank_part] + [swap(rank_part, "tp", bit) for bit in range(1, tp_width)])
    else:
        parts = lax.psum(rank_part, "tp")[None]

    masked = pl.pallas_call(
        query_kernel,
        out_shape=jax.ShapeDtypeStruct((sections * rows, plain.shape[1]), BF16),
        in_specs=[VMEM] * 10,
        out_specs=VMEM,
        name="queries",
    )(
        parts,
        scale,
        pick,
        adapter_up,
        plain,
        plain_across,
        plain_beside,
        plain_beside_across,
        cosine,
        sine,
    ).reshape(sections, rows, plain.shape[1])
    other = swap(masked, "section", 1)
    own_pair, across_pair = masked[0] + other[1], masked[2] + other[3]
    own_far, across_far = swap((across_pair, own_pair), "section", 2)
    query_own, query_across = own_pair + own_far, across_pair + across_far
    query_beside, query_beside_across = swap((query_own, query_across), "section", 1)

    kv_full = lax.all_gather(kv_part, "tp", axis=1, tiled=True)
    kv_cols = KVH * HEAD_DIM
    key_rows = lax.dynamic_slice_in_dim(kv_full, kv_start, kvl * HEAD_DIM, 1)
    value_rows = lax.dynamic_slice_in_dim(kv_full, kv_cols + kv_start, kvl * HEAD_DIM, 1)

    def by_slot(array):
        array = array.astype(BF16).reshape(steps, slots, kvl * HEAD_DIM).transpose(1, 0, 2)
        return jnp.pad(array, ((0, 0), (0, FRESH_ROWS - steps), (0, 0)))

    turned = [
        key_rows[:, k * HEAD_DIM : (k + 1) * HEAD_DIM] * cosine[:rows]
        + jnp.roll(key_rows[:, k * HEAD_DIM : (k + 1) * HEAD_DIM], HEAD_DIM // 2, 1) * sine[:rows]
        for k in range(kvl)
    ]
    new_keys, new_values = by_slot(jnp.concatenate(turned, 1)), by_slot(value_rows)

    cache = prompt_cache_pool
    if cols_dev < HEAD_DIM:
        share = HEAD_DIM // cols_dev
        groups = [list(range(g, g + share)) for g in range(0, tp_width, share)]
        cache = lax.all_gather(cache, "tp", axis=3, tiled=True, axis_index_groups=groups)

    owners, limits = owners.reshape(sections, slots), limits.reshape(sections, slots)

    def attend_two(positions, fresh, queries):
        chosen = jnp.asarray(positions)
        return attend(
            fresh, steps, slots, kvl, jnp.concatenate([owners[j] for j in positions]),
            jnp.concatenate([limits[j] for j in positions]), queries, new_keys, new_values, cache,
        )

    sent = attend_two((3, 1), False, (query_beside_across, query_beside))
    kept = attend_two((0, 2), True, (query_own, query_across))
    received = swap(sent, "section", 1)
    across = merge(kept[slots:], received[:slots])
    own = merge(kept[:slots], received[slots:])
    far = swap(across, "section", 2)
    attended = pl.pallas_call(
        functools.partial(finish_kernel, steps),
        out_shape=jax.ShapeDtypeStruct((rows, plain.shape[1]), BF16),
        in_specs=[VMEM] * 2,
        out_specs=VMEM,
        scratch_shapes=[pltpu.VMEM((local_heads, rows, HEAD_DIM), F32)],
        name="finish",
    )(own, far)

    partial_out = jnp.dot(attended, wo, preferred_element_type=F32).astype(BF16)
    if tp_width <= 4:
        quarter = model_width // tp_width

        def part_of(bit):
            return lax.dynamic_slice_in_dim(partial_out, (tp_id ^ bit) * quarter, quarter, 1)

        total = part_of(0).astype(F32)
        for bit in range(1, tp_width):
            total = total + swap(part_of(bit), "tp", bit).astype(F32)
        total = total.astype(BF16)
        result = jnp.zeros((rows, model_width), BF16)
        for bit in range(tp_width):
            chunk = swap(total, "tp", bit) if bit else total
            result = lax.dynamic_update_slice_in_dim(result, chunk, (tp_id ^ bit) * quarter, 1)
    else:
        result = lax.psum(partial_out, "tp")
    return result.reshape(steps, slots, model_width)


def solution(mesh):
    return jax.shard_map(
        per_device,
        mesh=mesh,
        in_specs=(
            P(None, ("groups", "section"), None),
            P(),
            P(None, "tp"),
            P(None, "tp"),
            P("tp", None),
            P(("groups", "section"), "tp", None),
            P(("groups", "section"), None, "tp"),
            P("groups", None, "section", "tp"),
            P("groups"),
            P("groups"),
            P("groups"),
            P("groups"),
        ),
        out_specs=P(None, ("groups", "section"), None),
        check_vma=False,
    )
```

time: 886 us -> 168 us (0.19); the launches traced: 876 us -> 168 us
  blocking collectives: 280 us -> 14 us
  waiting for transfers between devices: 258 us -> 42 us
  matrix products: 166 us -> 34.9 us
  local copies, waits for them, and re-layouts: 115 us -> 17.2 us
  Pallas kernels: 0 us -> 31.6 us
  other arithmetic: 33.6 us -> 8.83 us
  between operations: 16 us -> 0.29 us
  starting transfers between devices: 7.84 us -> 18.8 us
    all_gather x6 -> x0, waiting for transfers between devices: 220 us -> none  [the longest x1 137 us: per_device(): lax.all_gather(adapter_up, 'section', axis=0, tiled=True)]
    all_gather x12 -> x1, blocking collectives: 159 us -> 14 us  [per_device(): kv_full = lax.all_gather(kv_part, 'tp', axis=1, tiled=True)]
    dot_general x35 -> x3, matrix products: 166 us -> 34.9 us  [the longest x1 16.5 us: per_device(): partial_out = jnp.dot(attended, wo, preferred_element_type=F32).astype(BF16)]
    psum x1 -> x0, blocking collectives: 120 us -> none  [per_device(): rank_products_sum, kv_full = lax.psum((rank_part, widened), 'tp')]
    reshape x2, local copies, waits for them, and re-layouts: 45 us -> 0.01 us  [by_slot(): array.astype(BF16).reshape(steps, slots, kvl * HEAD_DIM).transpose(1, 0, 2)]
    ppermute x0 -> x22, waiting for transfers between devices: none -> 42 us  [swap(): return jax.tree.map(lambda a: lax.ppermute(a, axis, pairs), value)]
    psum x2 -> x0, waiting for transfers between devices: 37.6 us -> none  [the longest x1 37.6 us: per_device(): results.append(lax.psum(partial_out.astype(jnp.bfloat16), 'tp'))]
    pallas_call x0 -> x7, Pallas kernels: none -> 31.6 us  [the longest x2 18.1 us: attend(): pl.pallas_call(functools.partial(attend_kernel, fresh, steps, slots, kvl)...]
  transfers between devices with their start and end apart: 9 -> 22, of which waited for: 3 -> 12; matrix products, arithmetic and copies ran while one was open for 24% -> 15% of each run, Pallas kernels for 0% -> 9%
where the time goes in v1:
time: 168 us
  waiting for transfers between devices  42 us (25%)
  matrix products  34.9 us (21%)
  Pallas kernels  31.6 us (19%)
  starting transfers between devices  18.8 us (11%)
  local copies, waits for them, and re-layouts  17.2 us (10%)
  blocking collectives  14 us (8%)
  other arithmetic  8.83 us (5%)
    ppermute x22, waiting for transfers between devices, swap(): return jax.tree.map(lambda a: lax.ppermute(a, axis, pairs), value)  42 us
    ppermute x22, starting transfers between devices, swap(): return jax.tree.map(lambda a: lax.ppermute(a, axis, pairs), value)  18.8 us
    pallas_call x2, Pallas kernels, attend(): pl.pallas_call(functools.partial(attend_kernel, fresh, steps, slots, kvl)...  18.1 us
    dot_general x1, matrix products, per_device(): partial_out = jnp.dot(attended, wo, preferred_element_type=F32).astype(BF16)  16.5 us
    all_gather x1, blocking collectives, per_device(): kv_full = lax.all_gather(kv_part, 'tp', axis=1, tiled=True)  14 us
    dot_general x1, matrix products, per_device(): plain = jnp.dot(normed, wq, preferred_element_type=F32)  13.5 us
    unnamed x32, local copies, waits for them, and re-layouts  13.3 us
    dot_general x1, matrix products, per_device(): kv_part = jnp.dot(normed, wkv, preferred_element_type=F32)  4.9 us
  transfers between devices with their start and end apart: 22, of which 12 were waited for; matrix products, arithmetic and copies ran while one was open for 15% of the time, Pallas kernels for 9%

profile of v1, /device:TPU:0, one launch (start us, length us, event | category | flops | bytes accessed | tf_op | source)
XLA Modules:
  0.0 167.6 jit_solution(10068695625591362605)
XLA Ops:
  0.0 1.3 fusion
  2.1 1.2 fusion.3
  3.8 2.6 %collective-permute-start = (bf16[32,2048]{1,0:T(8,128)(2,1)S(1)}, bf16[32,2048]{1,0:T(8,128)(2,1)S(1)}, u32[]{:S(2)}, u32[]{:S(2)}) collective-permute-start(bf16[32,2048]{1,0:T(8,128)(2,1)S(1)} %constant_dynamic-slice_fusion.6.own), channel_id=1, source_target_pairs={{0,8},{4,12},{8,0},{12,4},{1,9},{5,13},{9,1},{13,5},{2,10},{6,14},... | collective-permute-start | bytes 393224 | tf_op jit(solution)/shard_map/ppermute | solution.py:36
  6.4 13.5 %fusion.26.own = f32[32,2048]{1,0:T(8,128)S(1)} fusion(bf16[32,8192]{1,0:T(8,128)(2,1)S(1)} %fusion.3, bf16[8192,2048]{1,0:T(8,128)(2,1)} %param.14), kind=kOutput, calls=%fused_computation.79 | convolution fusion | flops 1073741824 | bytes 34340864 | tf_op jit(solution)/shard_map/dot_general | solution.py:283
  21.2 4.9 %fusion.27 = f32[32,512]{1,0:T(8,128)S(1)} fusion(bf16[32,8192]{1,0:T(8,128)(2,1)S(1)} %fusion.3, bf16[8192,512]{1,0:T(8,128)(2,1)} %param.15), kind=kOutput, calls=%fused_computation.80 | convolution fusion | flops 268435456 | bytes 8978432 | tf_op jit(solution)/shard_map/dot_general | solution.py:286
  26.8 1.9 %collective-permute-done.6.across = f32[32,2048]{1,0:T(8,128)S(1)} collective-permute-done((f32[32,2048]{1,0:T(8,128)S(1)}, f32[32,2048]{1,0:T(8,128)S(1)}, u32[]{:S(2)}, u32[]{:S(2)}) %collective-permute-start.6) | collective-permute-done | bytes 262176 | tf_op jit(solution)/shard_map/ppermute | solution.py:36
  29.5 3.8 %down.2 = f32[128,128]{1,0:T(8,128)} custom-call(bf16[32,2048]{1,0:T(8,128)(2,1)} %copy-done.4, bf16[32,2048]{1,0:T(8,128)(2,1)} %copy-done.10, bf16[32,2048]{1,0:T(8,128)(2,1)} %copy-done.9, bf16[32,2048]{1,0:T(8,128)(2,1)} %copy-done.11, f32[128,4]{1,0:T(8,128)} %bitcast.37, bf16[4,2048,128]{2,1,0:T(8,128)(2,1)} %down.3), custom_call_target="tpu_custom_call" | custom-call | tf_op jit(solution)/shard_map/down/pallas_call | solution.py:288
  33.3 3.6 %collective-permute-start.5 = (f32[128,128]{1,0:T(8,128)}, f32[128,128]{1,0:T(8,128)S(1)}, u32[]{:S(2)}, u32[]{:S(2)}) collective-permute-start(f32[128,128]{1,0:T(8,128)} %down.2), channel_id=1, source_target_pairs={{0,3},{1,2},{2,1},{3,0},{4,7},{5,6},{6,5},{7,4},{8,11},{9,10},{10,... | collective-permute-start | bytes 196616 | tf_op jit(solution)/shard_map/ppermute | solution.py:36
  38.5 1.6 collective-permute-done.5
  40.1 3.1 %collective-permute-done.4 = f32[128,128]{1,0:T(8,128)S(1)} collective-permute-done((f32[128,128]{1,0:T(8,128)}, f32[128,128]{1,0:T(8,128)S(1)}, u32[]{:S(2)}, u32[]{:S(2)}) %collective-permute-start.4) | collective-permute-done | bytes 65568 | tf_op jit(solution)/shard_map/ppermute | solution.py:36
  43.2 1.6 pad_maximum_fusion.parts
  45.6 3.8 %queries.1 = bf16[128,2048]{1,0:T(8,128)(2,1)} custom-call(f32[4,128,128]{2,1,0:T(8,128)} %pad_maximum_fusion.parts, f32[128,128]{1,0:T(8,128)} %bitcast.39, f32[128,4]{1,0:T(8,128)} %bitcast.38, bf16[4,128,2048]{2,1,0:T(8,128)(2,1)} %up.1, f32[32,2048]{1,0:T(8,128)} %copy-done.2, f32[32,2048]{1,0:T(8,128)} %copy-done.7, f32[32,2048]{1,0:T(8,128)} %copy-done.6, ...), custom_call_target="tpu_custom_call" | custom-call | tf_op jit(solution)/shard_map/queries/pallas_call | solution.py:300
  49.4 14.0 %all_gather.3 = f32[32,2048]{1,0:T(8,128)S(1)} all-gather(f32[32,512]{1,0:T(8,128)S(1)} %fusion.27), channel_id=1, replica_groups=mesh['groups'=2,'section'=4,'tp'=4] {'tp'}, dimensions={1}, use_global_device_ids=true | all-gather | bytes 327680 | tf_op jit(solution)/shard_map/all_gather | solution.py:324
  65.4 4.2 %collective-permute-done.11 = bf16[32,2048]{1,0:T(8,128)(2,1)S(1)} collective-permute-done((bf16[32,2048]{1,0:T(8,128)(2,1)S(1)}, bf16[32,2048]{1,0:T(8,128)(2,1)S(1)}, u32[]{:S(2)}, u32[]{:S(2)}) %collective-permute-start.11) | collective-permute-done | bytes 131104 | tf_op jit(solution)/shard_map/ppermute | solution.py:36
  71.5 4.0 %collective-permute-done.10 = bf16[32,2048]{1,0:T(8,128)(2,1)S(1)} collective-permute-done((bf16[32,2048]{1,0:T(8,128)(2,1)S(1)}, bf16[32,2048]{1,0:T(8,128)(2,1)S(1)}, u32[]{:S(2)}, u32[]{:S(2)}) %collective-permute-start.10) | collective-permute-done | bytes 131104 | tf_op jit(solution)/shard_map/ppermute | solution.py:36
  77.0 5.8 %copy-done = bf16[32,2,512,256]{3,2,1,0:T(8,128)(2,1)S(1)} copy-done((bf16[32,2,512,256]{3,2,1,0:T(8,128)(2,1)S(1)}, bf16[32,2,512,256]{3,2,1,0:T(8,128)(2,1)}, u32[]{:S(2)}) %copy-start) | copy-done | bytes 16777240
  82.8 8.8 %attend.3 = f32[16,72,128]{2,1,0:T(8,128)S(1)} custom-call(s32[16]{0:T(128)S(1)} %pad_add_fusion.2.owners, s32[16]{0:T(128)S(1)} %pad_add_fusion.3.limits, bf16[32,2048]{1,0:T(8,128)(2,1)S(1)} %collective-permute-done.12.qa, bf16[32,2048]{1,0:T(8,128)(2,1)S(1)} %collective-permute-done.13.qb, bf16[8,16,256]{2,1,0:T(8,128)(2,1)S(1)} %pad.7.nk, ...), custom_call_target="tpu_custom_call" | custom-call | flops 536870912 | bytes 8388608 | tf_op jit(solution)/shard_map/attend/pallas_call | solution.py:187
  91.9 5.8 %copy-done.1 = bf16[32,2,512,256]{3,2,1,0:T(8,128)(2,1)S(1)} copy-done((bf16[32,2,512,256]{3,2,1,0:T(8,128)(2,1)S(1)}, bf16[32,2,512,256]{3,2,1,0:T(8,128)(2,1)}, u32[]{:S(2)}) %copy-start.1) | copy-done | bytes 16777240
  97.7 9.4 %attend.2 = f32[16,72,128]{2,1,0:T(8,128)S(1)} custom-call(s32[16]{0:T(128)S(1)} %pad_add_fusion.owners, s32[16]{0:T(128)S(1)} %pad_add_fusion.1.limits, bf16[32,2048]{1,0:T(8,128)(2,1)S(1)} %add.106.qa, bf16[32,2048]{1,0:T(8,128)(2,1)S(1)} %get-tuple-element.10.qb, bf16[8,16,256]{2,1,0:T(8,128)(2,1)S(1)} %pad.7.nk, bf16[8,16,256]{2,1,0:T(8,128)(2,1)S(1)} %pad.8.nv, ...), custom_call_target="tpu_custom_call" | custom-call | flops 536870912 | bytes 8388608 | tf_op jit(solution)/shard_map/attend/pallas_call | solution.py:187
  108.7 2.0 %merge.3 = f32[8,72,128]{2,1,0:T(8,128)} custom-call(f32[8,72,128]{2,1,0:T(8,128)} %get-tuple-element.14.a, f32[8,72,128]{2,1,0:T(8,128)} %get-tuple-element.12.b), custom_call_target="tpu_custom_call" | custom-call | tf_op jit(solution)/shard_map/merge/pallas_call | solution.py:209
  111.4 2.0 %merge.2.a = f32[8,72,128]{2,1,0:T(8,128)} custom-call(f32[8,72,128]{2,1,0:T(8,128)} %get-tuple-element.15.a, f32[8,72,128]{2,1,0:T(8,128)} %get-tuple-element.13.b), custom_call_target="tpu_custom_call" | custom-call | tf_op jit(solution)/shard_map/merge/pallas_call | solution.py:209
  113.4 6.8 %collective-permute-done.15.b = f32[8,72,128]{2,1,0:T(8,128)S(1)} collective-permute-done((f32[8,72,128]{2,1,0:T(8,128)}, f32[8,72,128]{2,1,0:T(8,128)S(1)}, u32[]{:S(2)}, u32[]{:S(2)}) %collective-permute-start.15) | collective-permute-done | bytes 294944 | tf_op jit(solution)/shard_map/ppermute | solution.py:36
  120.9 2.0 %finish.1 = bf16[32,2048]{1,0:T(8,128)(2,1)} custom-call(f32[8,72,128]{2,1,0:T(8,128)} %merge.2.a, f32[8,72,128]{2,1,0:T(8,128)} %copy-done.5), custom_call_target="tpu_custom_call" | custom-call | tf_op jit(solution)/shard_map/finish/pallas_call | solution.py:361
  123.0 16.5 %convolution_convert_fusion = bf16[32,8192]{1,0:T(8,128)(2,1)S(1)} fusion(bf16[32,2048]{1,0:T(8,128)(2,1)} %finish.1, bf16[2048,8192]{1,0:T(8,128)(2,1)} %param.16), kind=kOutput, calls=%fused_computation | convolution fusion | flops 1074003968 | bytes 34209792 | tf_op jit(solution)/shard_map/dot_general | solution.py:370
  140.2 2.0 %collective-permute-start.18 = (bf16[32,2048]{1,0:T(8,128)(2,1)S(1)}, bf16[32,2048]{1,0:T(8,128)(2,1)S(1)}, u32[]{:S(2)}, u32[]{:S(2)}) collective-permute-start(bf16[32,2048]{1,0:T(8,128)(2,1)S(1)} %get-tuple-element.17), channel_id=1, source_target_pairs={{0,3},{1,2},{2,1},{3,0},{4,7},{5,6},{6,5},{7,4},{8,11},{9,10},{10,... | collective-permute-start | bytes 393224 | tf_op jit(solution)/shard_map/ppermute | solution.py:36
  143.0 1.8 %collective-permute-done.16 = bf16[32,2048]{1,0:T(8,128)(2,1)S(1)} collective-permute-done((bf16[32,2048]{1,0:T(8,128)(2,1)S(1)}, bf16[32,2048]{1,0:T(8,128)(2,1)S(1)}, u32[]{:S(2)}, u32[]{:S(2)}) %collective-permute-start.16) | collective-permute-done | bytes 131104 | tf_op jit(solution)/shard_map/ppermute | solution.py:36
  144.9 4.5 %collective-permute-done.18 = bf16[32,2048]{1,0:T(8,128)(2,1)S(1)} collective-permute-done((bf16[32,2048]{1,0:T(8,128)(2,1)S(1)}, bf16[32,2048]{1,0:T(8,128)(2,1)S(1)}, u32[]{:S(2)}, u32[]{:S(2)}) %collective-permute-start.18) | collective-permute-done | bytes 131104 | tf_op jit(solution)/shard_map/ppermute | solution.py:36
  149.4 4.8 %collective-permute-done.17 = bf16[32,2048]{1,0:T(8,128)(2,1)S(1)} collective-permute-done((bf16[32,2048]{1,0:T(8,128)(2,1)S(1)}, bf16[32,2048]{1,0:T(8,128)(2,1)S(1)}, u32[]{:S(2)}, u32[]{:S(2)}) %collective-permute-start.17) | collective-permute-done | bytes 131104 | tf_op jit(solution)/shard_map/ppermute | solution.py:36
  154.4 3.0 %collective-permute-start.20 = (bf16[32,2048]{1,0:T(8,128)(2,1)S(1)}, bf16[32,2048]{1,0:T(8,128)(2,1)S(1)}, u32[]{:S(2)}, u32[]{:S(2)}) collective-permute-start(bf16[32,2048]{1,0:T(8,128)(2,1)S(1)} %get-tuple-element.9), channel_id=1, source_target_pairs={{0,2},{1,3},{2,0},{3,1},{4,6},{5,7},{6,4},{7,5},{8,10},{9,11},{10,... | collective-permute-start | bytes 393224 | tf_op jit(solution)/shard_map/ppermute | solution.py:36
  157.4 1.3 collective-permute-start.21
  158.8 1.6 collective-permute-done.19
  160.4 6.3 %collective-permute-done.20 = bf16[32,2048]{1,0:T(8,128)(2,1)S(1)} collective-permute-done((bf16[32,2048]{1,0:T(8,128)(2,1)S(1)}, bf16[32,2048]{1,0:T(8,128)(2,1)S(1)}, u32[]{:S(2)}, u32[]{:S(2)}) %collective-permute-start.20) | collective-permute-done | bytes 131104 | tf_op jit(solution)/shard_map/ppermute | solution.py:36
  (106 shorter events, 17.8 us)
Async XLA Ops:
  0.0 20.6 %copy-start.14 = (s32[32]{0:T(128)S(1)}, s32[32]{0:T(128)}, u32[]{:S(2)}) copy-start(s32[32]{0:T(128)} %param.22) | copy-start | bytes 388
  0.0 20.6 %copy-start.12 = (s32[32]{0:T(128)S(1)}, s32[32]{0:T(128)}, u32[]{:S(2)}) copy-start(s32[32]{0:T(128)} %param.21) | copy-start | bytes 388
  0.0 20.6 %copy-start.13 = (s32[32]{0:T(128)S(1)}, s32[32]{0:T(128)}, u32[]{:S(2)}) copy-start(s32[32]{0:T(128)} %param.20) | copy-start | bytes 388
  0.0 20.8 %copy-start.15 = (s32[16]{0:T(128)S(1)}, s32[16]{0:T(128)}, u32[]{:S(2)}) copy-start(s32[16]{0:T(128)} %param.23) | copy-start | bytes 196
  3.3 26.2 %copy-start.4 = (bf16[32,2048]{1,0:T(8,128)(2,1)}, bf16[32,2048]{1,0:T(8,128)(2,1)S(1)}, u32[]{:S(2)}) copy-start(bf16[32,2048]{1,0:T(8,128)(2,1)S(1)} %constant_dynamic-slice_fusion.6.own) | copy-start | bytes 393220
  3.3 25.5 %collective-permute-start.1 = (bf16[32,2048]{1,0:T(8,128)(2,1)S(1)}, bf16[32,2048]{1,0:T(8,128)(2,1)S(1)}, u32[]{:S(2)}, u32[]{:S(2)}) collective-permute-start(bf16[32,2048]{1,0:T(8,128)(2,1)S(1)} %constant_dynamic-slice_fusion.6.own), channel_id=1, source_target_pairs={{0,4},{4,0},{8,12},{12,8},{1,5},{5,1},{9,13},{13,9},{2,6},{6,2},{1... | collective-permute-start | bytes 393224 | tf_op jit(solution)/shard_map/ppermute | solution.py:36
  3.8 22.8 %collective-permute-start = (bf16[32,2048]{1,0:T(8,128)(2,1)S(1)}, bf16[32,2048]{1,0:T(8,128)(2,1)S(1)}, u32[]{:S(2)}, u32[]{:S(2)}) collective-permute-start(bf16[32,2048]{1,0:T(8,128)(2,1)S(1)} %constant_dynamic-slice_fusion.6.own), channel_id=1, source_target_pairs={{0,8},{4,12},{8,0},{12,4},{1,9},{5,13},{9,1},{13,5},{2,10},{6,14},... | collective-permute-start | bytes 393224 | tf_op jit(solution)/shard_map/ppermute | solution.py:36
  19.9 25.6 %copy-start.2 = (f32[32,2048]{1,0:T(8,128)}, f32[32,2048]{1,0:T(8,128)S(1)}, u32[]{:S(2)}) copy-start(f32[32,2048]{1,0:T(8,128)S(1)} %fusion.26.own) | copy-start | bytes 786436
  19.9 24.9 %collective-permute-start.7 = (f32[32,2048]{1,0:T(8,128)S(1)}, f32[32,2048]{1,0:T(8,128)S(1)}, u32[]{:S(2)}, u32[]{:S(2)}) collective-permute-start(f32[32,2048]{1,0:T(8,128)S(1)} %fusion.26.own), channel_id=1, source_target_pairs={{0,4},{4,0},{8,12},{12,8},{1,5},{5,1},{9,13},{13,9},{2,6},{6,2},{1... | collective-permute-start | bytes 786440 | tf_op jit(solution)/shard_map/ppermute | solution.py:36
  20.2 8.6 %collective-permute-start.6 = (f32[32,2048]{1,0:T(8,128)S(1)}, f32[32,2048]{1,0:T(8,128)S(1)}, u32[]{:S(2)}, u32[]{:S(2)}) collective-permute-start(f32[32,2048]{1,0:T(8,128)S(1)} %fusion.26.own), channel_id=1, source_target_pairs={{0,8},{4,12},{8,0},{12,4},{1,9},{5,13},{9,1},{13,5},{2,10},{6,14},... | collective-permute-start | bytes 786440 | tf_op jit(solution)/shard_map/ppermute | solution.py:36
  26.6 2.9 %copy-start.10 = (bf16[32,2048]{1,0:T(8,128)(2,1)}, bf16[32,2048]{1,0:T(8,128)(2,1)S(1)}, u32[]{:S(2)}) copy-start(bf16[32,2048]{1,0:T(8,128)(2,1)S(1)} %collective-permute-done.across) | copy-start | bytes 393220
  26.6 2.2 %collective-permute-start.2 = (bf16[32,2048]{1,0:T(8,128)(2,1)S(1)}, bf16[32,2048]{1,0:T(8,128)(2,1)S(1)}, u32[]{:S(2)}, u32[]{:S(2)}) collective-permute-start(bf16[32,2048]{1,0:T(8,128)(2,1)S(1)} %collective-permute-done.across), channel_id=1, source_target_pairs={{0,4},{4,0},{8,12},{12,8},{1,5},{5,1},{9,13},{13,9},{2,6},{6,2},{1... | collective-permute-start | bytes 393224 | tf_op jit(solution)/shard_map/ppermute | solution.py:36
  28.7 16.8 %copy-start.7 = (f32[32,2048]{1,0:T(8,128)}, f32[32,2048]{1,0:T(8,128)S(1)}, u32[]{:S(2)}) copy-start(f32[32,2048]{1,0:T(8,128)S(1)} %collective-permute-done.6.across) | copy-start | bytes 786436
  28.7 16.1 %collective-permute-start.8 = (f32[32,2048]{1,0:T(8,128)S(1)}, f32[32,2048]{1,0:T(8,128)S(1)}, u32[]{:S(2)}, u32[]{:S(2)}) collective-permute-start(f32[32,2048]{1,0:T(8,128)S(1)} %collective-permute-done.6.across), channel_id=1, source_target_pairs={{0,4},{4,0},{8,12},{12,8},{1,5},{5,1},{9,13},{13,9},{2,6},{6,2},{1... | collective-permute-start | bytes 786440 | tf_op jit(solution)/shard_map/ppermute | solution.py:36
  33.3 6.8 %collective-permute-start.5 = (f32[128,128]{1,0:T(8,128)}, f32[128,128]{1,0:T(8,128)S(1)}, u32[]{:S(2)}, u32[]{:S(2)}) collective-permute-start(f32[128,128]{1,0:T(8,128)} %down.2), channel_id=1, source_target_pairs={{0,3},{1,2},{2,1},{3,0},{4,7},{5,6},{6,5},{7,4},{8,11},{9,10},{10,... | collective-permute-start | bytes 196616 | tf_op jit(solution)/shard_map/ppermute | solution.py:36
  36.9 6.3 %collective-permute-start.4 = (f32[128,128]{1,0:T(8,128)}, f32[128,128]{1,0:T(8,128)S(1)}, u32[]{:S(2)}, u32[]{:S(2)}) collective-permute-start(f32[128,128]{1,0:T(8,128)} %down.2), channel_id=1, source_target_pairs={{0,2},{1,3},{2,0},{3,1},{4,6},{5,7},{6,4},{7,5},{8,10},{9,11},{10,... | collective-permute-start | bytes 196616 | tf_op jit(solution)/shard_map/ppermute | solution.py:36
  36.9 6.3 %collective-permute-start.3 = (f32[128,128]{1,0:T(8,128)}, f32[128,128]{1,0:T(8,128)S(1)}, u32[]{:S(2)}, u32[]{:S(2)}) collective-permute-start(f32[128,128]{1,0:T(8,128)} %down.2), channel_id=1, source_target_pairs={{0,1},{1,0},{2,3},{3,2},{4,5},{5,4},{6,7},{7,6},{8,9},{9,8},{10,11... | collective-permute-start | bytes 196616 | tf_op jit(solution)/shard_map/ppermute | solution.py:36
  49.4 14.2 %collective-permute-start.9 = (bf16[4,32,2048]{2,1,0:T(8,128)(2,1)}, bf16[4,32,2048]{2,1,0:T(8,128)(2,1)S(1)}, u32[]{:S(2)}, u32[]{:S(2)}) collective-permute-start(bf16[4,32,2048]{2,1,0:T(8,128)(2,1)} %bitcast.36), channel_id=1, source_target_pairs={{0,4},{4,0},{8,12},{12,8},{1,5},{5,1},{9,13},{13,9},{2,6},{6,2},{1... | collective-permute-start | bytes 1572872 | tf_op jit(solution)/shard_map/ppermute | solution.py:36
  64.5 5.0 %collective-permute-start.11 = (bf16[32,2048]{1,0:T(8,128)(2,1)S(1)}, bf16[32,2048]{1,0:T(8,128)(2,1)S(1)}, u32[]{:S(2)}, u32[]{:S(2)}) collective-permute-start(bf16[32,2048]{1,0:T(8,128)(2,1)S(1)} %fusion.5), channel_id=1, source_target_pairs={{0,8},{4,12},{8,0},{12,4},{1,9},{5,13},{9,1},{13,5},{2,10},{6,14},... | collective-permute-start | bytes 393224 | tf_op jit(solution)/shard_map/ppermute | solution.py:36
  70.5 5.0 %collective-permute-start.10 = (bf16[32,2048]{1,0:T(8,128)(2,1)S(1)}, bf16[32,2048]{1,0:T(8,128)(2,1)S(1)}, u32[]{:S(2)}, u32[]{:S(2)}) collective-permute-start(bf16[32,2048]{1,0:T(8,128)(2,1)S(1)} %get-tuple-element.11), channel_id=1, source_target_pairs={{0,8},{4,12},{8,0},{12,4},{1,9},{5,13},{9,1},{13,5},{2,10},{6,14},... | collective-permute-start | bytes 393224 | tf_op jit(solution)/shard_map/ppermute | solution.py:36
  71.4 4.4 %collective-permute-start.12 = (bf16[32,2048]{1,0:T(8,128)(2,1)S(1)}, bf16[32,2048]{1,0:T(8,128)(2,1)S(1)}, u32[]{:S(2)}, u32[]{:S(2)}) collective-permute-start(bf16[32,2048]{1,0:T(8,128)(2,1)S(1)} %get-tuple-element.10.qb), channel_id=1, source_target_pairs={{0,4},{4,0},{8,12},{12,8},{1,5},{5,1},{9,13},{13,9},{2,6},{6,2},{1... | collective-permute-start | bytes 393224 | tf_op jit(solution)/shard_map/ppermute | solution.py:36
  75.6 1.4 collective-permute-start.13
  77.0 5.8 %copy-start = (bf16[32,2,512,256]{3,2,1,0:T(8,128)(2,1)S(1)}, bf16[32,2,512,256]{3,2,1,0:T(8,128)(2,1)}, u32[]{:S(2)}) copy-start(bf16[32,2,512,256]{3,2,1,0:T(8,128)(2,1)} %cache.3) | copy-start | bytes 50331652
  91.5 16.4 %collective-permute-start.14 = (f32[16,72,128]{2,1,0:T(8,128)S(1)}, f32[16,72,128]{2,1,0:T(8,128)S(1)}, u32[]{:S(2)}, u32[]{:S(2)}) collective-permute-start(f32[16,72,128]{2,1,0:T(8,128)S(1)} %attend.3), channel_id=1, source_target_pairs={{0,4},{4,0},{8,12},{12,8},{1,5},{5,1},{9,13},{13,9},{2,6},{6,2},{1... | collective-permute-start | bytes 1769480 | tf_op jit(solution)/shard_map/ppermute | solution.py:36
  91.9 5.8 %copy-start.1 = (bf16[32,2,512,256]{3,2,1,0:T(8,128)(2,1)S(1)}, bf16[32,2,512,256]{3,2,1,0:T(8,128)(2,1)}, u32[]{:S(2)}) copy-start(bf16[32,2,512,256]{3,2,1,0:T(8,128)(2,1)} %cache.3) | copy-start | bytes 50331652
  110.7 9.5 %collective-permute-start.15 = (f32[8,72,128]{2,1,0:T(8,128)}, f32[8,72,128]{2,1,0:T(8,128)S(1)}, u32[]{:S(2)}, u32[]{:S(2)}) collective-permute-start(f32[8,72,128]{2,1,0:T(8,128)} %merge.3), channel_id=1, source_target_pairs={{0,8},{4,12},{8,0},{12,4},{1,9},{5,13},{9,1},{13,5},{2,10},{6,14},... | collective-permute-start | bytes 884744 | tf_op jit(solution)/shard_map/ppermute | solution.py:36
  139.5 5.4 %collective-permute-start.16 = (bf16[32,2048]{1,0:T(8,128)(2,1)S(1)}, bf16[32,2048]{1,0:T(8,128)(2,1)S(1)}, u32[]{:S(2)}, u32[]{:S(2)}) collective-permute-start(bf16[32,2048]{1,0:T(8,128)(2,1)S(1)} %get-tuple-element.16), channel_id=1, source_target_pairs={{0,1},{1,0},{2,3},{3,2},{4,5},{5,4},{6,7},{7,6},{8,9},{9,8},{10,11... | collective-permute-start | bytes 393224 | tf_op jit(solution)/shard_map/ppermute | solution.py:36
  140.2 9.2 %collective-permute-start.18 = (bf16[32,2048]{1,0:T(8,128)(2,1)S(1)}, bf16[32,2048]{1,0:T(8,128)(2,1)S(1)}, u32[]{:S(2)}, u32[]{:S(2)}) collective-permute-start(bf16[32,2048]{1,0:T(8,128)(2,1)S(1)} %get-tuple-element.17), channel_id=1, source_target_pairs={{0,3},{1,2},{2,1},{3,0},{4,7},{5,6},{6,5},{7,4},{8,11},{9,10},{10,... | collective-permute-start | bytes 393224 | tf_op jit(solution)/shard_map/ppermute | solution.py:36
  142.2 12.0 %collective-permute-start.17 = (bf16[32,2048]{1,0:T(8,128)(2,1)S(1)}, bf16[32,2048]{1,0:T(8,128)(2,1)S(1)}, u32[]{:S(2)}, u32[]{:S(2)}) collective-permute-start(bf16[32,2048]{1,0:T(8,128)(2,1)S(1)} %get-tuple-element.18), channel_id=1, source_target_pairs={{0,2},{1,3},{2,0},{3,1},{4,6},{5,7},{6,4},{7,5},{8,10},{9,11},{10,... | collective-permute-start | bytes 393224 | tf_op jit(solution)/shard_map/ppermute | solution.py:36
  154.3 6.1 %collective-permute-start.19 = (bf16[32,2048]{1,0:T(8,128)(2,1)S(1)}, bf16[32,2048]{1,0:T(8,128)(2,1)S(1)}, u32[]{:S(2)}, u32[]{:S(2)}) collective-permute-start(bf16[32,2048]{1,0:T(8,128)(2,1)S(1)} %get-tuple-element.9), channel_id=1, source_target_pairs={{0,1},{1,0},{2,3},{3,2},{4,5},{5,4},{6,7},{7,6},{8,9},{9,8},{10,11... | collective-permute-start | bytes 393224 | tf_op jit(solution)/shard_map/ppermute | solution.py:36
  154.4 12.3 %collective-permute-start.20 = (bf16[32,2048]{1,0:T(8,128)(2,1)S(1)}, bf16[32,2048]{1,0:T(8,128)(2,1)S(1)}, u32[]{:S(2)}, u32[]{:S(2)}) collective-permute-start(bf16[32,2048]{1,0:T(8,128)(2,1)S(1)} %get-tuple-element.9), channel_id=1, source_target_pairs={{0,2},{1,3},{2,0},{3,1},{4,6},{5,7},{6,4},{7,5},{8,10},{9,11},{10,... | collective-permute-start | bytes 393224 | tf_op jit(solution)/shard_map/ppermute | solution.py:36
  157.4 9.3 %collective-permute-start.21 = (bf16[32,2048]{1,0:T(8,128)(2,1)S(1)}, bf16[32,2048]{1,0:T(8,128)(2,1)S(1)}, u32[]{:S(2)}, u32[]{:S(2)}) collective-permute-start(bf16[32,2048]{1,0:T(8,128)(2,1)S(1)} %get-tuple-element.9), channel_id=1, source_target_pairs={{0,3},{1,2},{2,1},{3,0},{4,7},{5,6},{6,5},{7,4},{8,11},{9,10},{10,... | collective-permute-start | bytes 393224 | tf_op jit(solution)/shard_map/ppermute | solution.py:36
  (6 other events, 4.5 us)

commit v2 on v1

v2 whole, which is shorter than its diff:
```python
import functools
import math

import jax
import jax.numpy as jnp
from jax import lax
from jax.experimental import pallas as pl
from jax.experimental.pallas import tpu as pltpu
from jax.sharding import PartitionSpec as P

QUERY_HEADS = 64
KVH = 8
HEAD_DIM = 128
PER_KV = QUERY_HEADS // KVH

EPSILON = 1e-05
ROPE_BASE = 500000.0
ADAPTER_ALPHA = 16.0
NEGATIVE = -1e30
STAT_ROWS = 8
FRESH_ROWS = 16
GROUP = 4
F32 = jnp.float32
BF16 = jnp.bfloat16
VMEM = pl.BlockSpec(memory_space=pltpu.VMEM)
SMEM = pl.BlockSpec(memory_space=pltpu.SMEM)
IN_HBM = pl.BlockSpec(memory_space=pltpu.HBM)
QUICK = pl.CostEstimate(flops=1, bytes_accessed=1, transcendentals=0)


def in_hbm(value):
    return pltpu.with_memory_space_constraint(value, pltpu.HBM)


def in_vmem(*values):
    return [pltpu.with_memory_space_constraint(value, pltpu.VMEM) for value in values]


def params(mebibytes):
    return pltpu.CompilerParams(vmem_limit_bytes=mebibytes * 1024 * 1024)


def swap(value, axis, bit):
    size = lax.axis_size(axis)
    pairs = [(i, i ^ bit) for i in range(size)]
    return jax.tree.map(lambda a: lax.ppermute(a, axis, pairs), value)


def tables_kernel(slots, section_tokens, adapters, here, prompt_slot, prompt_length, slot_adapter, ranks, frequency, *outs):
    owners, limits, pick, scale, cosine, sine = outs
    section = here[0]
    requests = owners.shape[0]
    shape = pick.shape
    row = lax.broadcasted_iota(jnp.int32, shape, 0)
    lane = lax.broadcasted_iota(jnp.int32, shape, 1)

    def place(slot):
        return (lax.div(slot, slots) ^ section) * slots + lax.rem(slot, slots)

    lengths = jnp.zeros(shape, jnp.int32)
    adapter = jnp.zeros(shape, jnp.int32)
    rank = jnp.zeros(shape, jnp.int32)
    for i in range(requests):
        at, length = place(prompt_slot[i]), prompt_length[i]
        owners[at] = i
        limits[at] = jnp.clip(length - section * section_tokens, 0, section_tokens)
        lengths = jnp.where(row == at, length, lengths)
        at, chosen = place(i), slot_adapter[i]
        adapter = jnp.where(row == at, chosen, adapter)
        rank = jnp.where(row == at, ranks[chosen], rank)
    held = jnp.where(lane < adapters, section * adapters + lane, (section ^ 1) * adapters + lane - adapters)
    pick[...] = jnp.where((lane < 2 * adapters) & (adapter == held), 1.0, 0.0)
    rank_f32 = rank.astype(F32)
    scale[...] = jnp.where(lane < rank, ADAPTER_ALPHA / rank_f32, 0.0)
    steps = cosine.shape[0] // requests
    positions = by_row(lengths, steps, slots).astype(F32)
    step = lax.rem(lax.div(lax.broadcasted_iota(jnp.int32, cosine.shape, 0), slots), steps)
    angles = (positions + step.astype(F32)) * frequency[...]
    cosine[...] = jnp.cos(angles)
    low = lax.broadcasted_iota(jnp.int32, cosine.shape, 1) < HEAD_DIM // 2
    sine[...] = jnp.where(low, -jnp.sin(angles), jnp.sin(angles))


def norm_kernel(here, states, gain, normed, piece, wide, gains):
    steps, slots, width = states.shape
    gains[...] = gain[...].astype(F32)
    for t in range(steps):
        values = states[t].astype(F32)
        inverse = lax.rsqrt(jnp.mean(values * values, axis=-1, keepdims=True) + EPSILON)
        for c in range(width // 128):
            cols = slice(c * 128, (c + 1) * 128)
            wide[t * slots : (t + 1) * slots, cols] = values[:, cols] * inverse * gains[c : c + 1, :]
    normed[...] = wide[...].astype(BF16)
    cols = piece.shape[1]
    piece[...] = wide[:, pl.ds(pl.multiple_of(here[1] * cols, 128), cols)].astype(BF16)


def product_kernel(chunk, count_left, starts, here, *refs):
    lefts, right, refs = refs[:count_left], refs[count_left], refs[count_left + 1 :]
    *refs, held, sems, carry_sems = refs
    half = (len(refs) - len(starts)) // 2
    sources, outs, targets = refs[:half], refs[half : half + len(starts)], refs[half + len(starts) :]
    carries = [
        pltpu.make_async_copy(source, target, carry_sems.at[i])
        for i, (source, target) in enumerate(zip(sources, targets))
    ]
    slots, cols = held.shape[0], held.shape[2]
    chunks = right.shape[0] // chunk
    count = chunks * len(outs)

    def copy(n):
        block, i = divmod(n, chunks)
        first = pl.multiple_of(starts[block](here) * 128, 128)
        source = right.at[pl.ds(i * chunk, chunk), pl.ds(first, cols)]
        return pltpu.make_async_copy(source, held.at[n % slots], sems.at[n % slots])

    for n in range(min(slots, count)):
        copy(n).start()
    for carry in carries:
        carry.start()
    for n in range(count):
        block, i = divmod(n, chunks)
        copy(n).wait()
        left = jnp.concatenate([ref[:, i * chunk : (i + 1) * chunk] for ref in lefts], axis=0)
        part = jnp.dot(left, held[n % slots], preferred_element_type=F32)
        total = part if i == 0 else total + part
        if n + slots < count:
            copy(n + slots).start()
        if i + 1 == chunks:
            outs[block][...] = total.astype(outs[block].dtype)
    for carry in carries:
        carry.wait()


def product(name, here, lefts, right, starts, cols, types, chunk, carried=()):
    rows = sum(left.shape[0] for left in lefts)
    slots = min(8, right.shape[0] // chunk * len(starts))
    return pl.pallas_call(
        functools.partial(product_kernel, chunk, len(lefts), starts),
        out_shape=tuple(pltpu.VMEM((rows, cols), dtype) for dtype in types)
        + tuple(pltpu.VMEM(c.shape, c.dtype) for c in carried),
        in_specs=[SMEM] + [VMEM] * len(lefts) + [IN_HBM] * (1 + len(carried)),
        out_specs=(VMEM,) * (len(types) + len(carried)),
        scratch_shapes=[
            pltpu.VMEM((slots, chunk, cols), BF16),
            pltpu.SemaphoreType.DMA((slots,)),
            pltpu.SemaphoreType.DMA((max(1, len(carried)),)),
        ],
        compiler_params=params(14),
        cost_estimate=QUICK,
        name=name,
    )(here, *in_vmem(*lefts), in_hbm(right), *[in_hbm(c) for c in carried])


def add_kernel(*refs):
    *terms, out = refs
    total = terms[0][...].astype(F32)
    for term in terms[1:]:
        total = total + term[...].astype(F32)
    out[...] = total.astype(out.dtype)


def add(*terms):
    return pl.pallas_call(
        add_kernel,
        out_shape=pltpu.VMEM(terms[0].shape, BF16),
        in_specs=[VMEM] * len(terms),
        out_specs=VMEM,
        compiler_params=params(8),
        cost_estimate=QUICK,
        name="add",
    )(*in_vmem(*terms))


def by_row(table, steps, slots):
    blocks = [table[i : i + slots] for i in range(0, table.shape[0], slots)]
    return jnp.concatenate([block for block in blocks for _ in range(steps)], axis=0)


def down_kernel(steps, slots, own, beside, across, beside_across, pick, down, down_beside, out):
    states = jnp.concatenate([ref[...] for ref in (own, beside, across, beside_across)], axis=0)
    picks = by_row(pick[...], steps, slots)
    adapters = down.shape[0]
    total = jnp.zeros(out.shape, F32)
    for a in range(2 * adapters):
        part = jnp.dot(states, (down, down_beside)[a // adapters][a % adapters], preferred_element_type=F32)
        total = jnp.where(picks[:, a : a + 1] > 0, part, total)
    out[...] = total


def query_kernel(steps, slots, count, here, *refs):
    parts, refs = refs[:count], refs[count:]
    scale, pick, up, up_beside, cosine, sine, plain_near, plain_far, near, far = refs
    rank_sum = parts[0][...]
    for part in parts[1:]:
        rank_sum = rank_sum + part[...]
    scales = by_row(scale[...], steps, slots)
    picks = by_row(pick[...], steps, slots)
    low_rank = jnp.where(scales > 0, rank_sum * scales, 0.0)
    adapters, rank, width = up.shape
    wide = jnp.concatenate(
        [jnp.where(picks[:, a : a + 1] > 0, low_rank, 0.0) for a in range(2 * adapters)], axis=1
    ).astype(BF16)
    depth = adapters * rank
    ups = [ref.reshape(depth, width) for ref in (up, up_beside)]
    half = plain_near.shape[1]
    rows = steps * slots
    shown = jnp.sum(picks, axis=1, keepdims=True) > 0
    first = (here[0] & 1) * half
    step = min(2 * HEAD_DIM, half)
    for c in range(0, half, step):
        block = pl.ds(pl.multiple_of(first + c, 128), step)
        changes = jnp.dot(wide[:, :depth], ups[0][:, block], preferred_element_type=F32)
        changes = changes + jnp.dot(wide[:, depth:], ups[1][:, block], preferred_element_type=F32)
        for h in range(0, step, HEAD_DIM):
            cols = slice(c + h, c + h + HEAD_DIM)
            plain = jnp.concatenate([plain_near[:, cols], plain_far[:, cols]], axis=0)
            query = plain + changes[:, h : h + HEAD_DIM]
            turned = query * cosine[...] + pltpu.roll(query, HEAD_DIM // 2, 1) * sine[...]
            turned = jnp.where(shown, turned, 0.0).astype(BF16)
            for position in range(4):
                target = (near, far)[position // 2]
                target[position % 2, :, cols] = turned[position * rows : (position + 1) * rows]


def fetch_kernel(owners, cache, up, *refs):
    *outs, up_out, done, held, key_sems, value_sems, up_sem = refs
    sections = len(outs) // 2
    slots, ring = outs[0].shape[0], held.shape[0]
    count = sections * slots
    order = [(p, i) for p in (3, 2, 1, 0) for i in range(slots)]

    def key_copy(n):
        position, i = order[n]
        source = cache.at[owners[position * slots + i], 0]
        return pltpu.make_async_copy(source, held.at[n % ring], key_sems.at[n % ring])

    def value_copy(n):
        position, i = order[n]
        source = cache.at[owners[position * slots + i], 1]
        return pltpu.make_async_copy(source, outs[sections + position].at[i], value_sems.at[n])

    up_copy = pltpu.make_async_copy(up, up_out, up_sem.at[0])
    for n in range(ring):
        key_copy(n).start()
        value_copy(n).start()
    up_copy.start()
    for n in range(count):
        position, i = order[n]
        key_copy(n).wait()
        outs[position][i] = held[n % ring].T
        if n + ring < count:
            key_copy(n + ring).start()
            value_copy(n + ring).start()
    done[...] = jnp.zeros_like(done)
    up_copy.wait()
    for n in range(count):
        value_copy(n).wait()


def hold_kernel(starts, here, source, *refs):
    *outs, done, sems = refs
    cols = outs[0].shape[1]
    copies = []
    for i, out in enumerate(outs):
        first = pl.multiple_of(starts[i](here) * 128, 128)
        copies.append(pltpu.make_async_copy(source.at[:, pl.ds(first, cols)], out, sems.at[i]))
    for copy in copies:
        copy.start()
    done[...] = jnp.zeros_like(done)
    for copy in copies:
        copy.wait()


def place_kernel(starts, here, *refs):
    *blocks, out, sems = refs
    copies = []
    for i, block in enumerate(blocks):
        cols = block.shape[1]
        first = pl.multiple_of(starts[i](here) * 128, 128)
        copies.append(pltpu.make_async_copy(block, out.at[:, pl.ds(first, cols)], sems.at[i]))
    for copy in copies:
        copy.start()
    for copy in copies:
        copy.wait()


def held_output_kernel(left, *refs):
    half = len(refs) // 2
    for right, out in zip(refs[:half], refs[half:]):
        out[...] = jnp.dot(left[...], right[...], preferred_element_type=F32).astype(out.dtype)


def attend_kernel(position, steps, slots, kvl, here, limits, own, other, keys, values, *refs):
    fresh = position == 0
    if fresh:
        first, second, cosine, sine, out, qf, qs, turned, nk, nv = refs
    else:
        out, qf, qs = refs
    half = own.shape[2] // HEAD_DIM
    heads = 2 * half
    per_kv = heads // kvl
    rows = heads * steps
    tokens = values.shape[1]
    root = 1.0 / math.sqrt(HEAD_DIM)
    qs[...] = jnp.zeros_like(qs)
    lower = here[0] & 1 == 0
    for h in range(half):
        cols = slice(h * HEAD_DIM, (h + 1) * HEAD_DIM)
        mine = own[position % 2, :, cols].astype(F32)
        theirs = other[1 - position % 2, :, cols].astype(F32)
        qf[h] = jnp.where(lower, mine, theirs)
        qf[half + h] = jnp.where(lower, theirs, mine)
    for i in range(slots):
        for h in range(heads):
            k = h // per_kv
            qs[i, h * steps : (h + 1) * steps, k * HEAD_DIM : (k + 1) * HEAD_DIM] = qf[
                h, pl.ds(i, steps, stride=slots), :
            ]
    if fresh:
        step_of_row = lax.broadcasted_iota(jnp.int32, (rows, FRESH_ROWS), 0) % steps
        fresh_valid = lax.broadcasted_iota(jnp.int32, (rows, FRESH_ROWS), 1) <= step_of_row
        rows_here = steps * slots
        nk[...] = jnp.zeros_like(nk)
        nv[...] = jnp.zeros_like(nv)
        for k in range(kvl):
            cols = slice(k * HEAD_DIM, (k + 1) * HEAD_DIM)
            swapped = here[1] & 1 == 1
            key = jnp.where(swapped, second[:, cols], first[:, cols])
            turned[0, k] = key * cosine[:rows_here, :] + pltpu.roll(key, HEAD_DIM // 2, 1) * sine[:rows_here, :]
            turned[1, k] = jnp.where(swapped, first[:, cols], second[:, cols])
            for i in range(slots):
                nk[i, :steps, cols] = turned[0, k, pl.ds(i, steps, stride=slots), :]
                nv[i, :steps, cols] = turned[1, k, pl.ds(i, steps, stride=slots), :]
    eye = diagonal(rows)
    token = lax.broadcasted_iota(jnp.int32, (rows, tokens), 1)
    for i in range(slots):
        limit = limits[position * slots + i]
        queries = qs[i].astype(BF16)
        scores = jnp.dot(queries, keys[i], preferred_element_type=F32) * root
        valid = token < limit
        scores = jnp.where(valid, scores, NEGATIVE)
        top = jnp.max(scores, axis=1, keepdims=True)
        if fresh:
            new_scores = lax.dot_general(
                queries, nk[i].astype(BF16), (((1,), (1,)), ((), ())), preferred_element_type=F32
            )
            new_scores = jnp.where(fresh_valid, new_scores * root, NEGATIVE)
            top = jnp.maximum(top, jnp.max(new_scores, axis=1, keepdims=True))
        weights = jnp.where(valid, jnp.exp(scores - top), 0.0)
        total = jnp.sum(weights, axis=1, keepdims=True)
        value = jnp.dot(weights.astype(BF16), values[i], preferred_element_type=F32)
        if fresh:
            new_weights = jnp.where(fresh_valid, jnp.exp(new_scores - top), 0.0)
            total = total + jnp.sum(new_weights, axis=1, keepdims=True)
            value = value + jnp.dot(
                new_weights.astype(BF16), nv[i].astype(BF16), preferred_element_type=F32
            )
        for k in range(kvl):
            block = slice(k * per_kv * steps, (k + 1) * per_kv * steps)
            out[i, block, :] = value[block, k * HEAD_DIM : (k + 1) * HEAD_DIM]
        out[i, rows : rows + 1, :rows] = jnp.sum(jnp.where(eye, top, 0.0), axis=0, keepdims=True)
        out[i, rows + 1 : rows + 2, :rows] = jnp.sum(jnp.where(eye, total, 0.0), axis=0, keepdims=True)


def joined(refs, i, rows, eye):
    tops = [ref[i, rows : rows + 1, :rows] for ref in refs]
    top = functools.reduce(jnp.maximum, tops)
    total, weighted = 0.0, 0.0
    for ref, part_top in zip(refs, tops):
        scale = jnp.exp(part_top - top)
        total = total + ref[i, rows + 1 : rows + 2, :rows] * scale
        column = jnp.sum(jnp.where(eye, scale, 0.0), axis=1, keepdims=True)
        weighted = weighted + ref[i, :rows, :] * column
    return weighted, top, total


def diagonal(rows):
    return lax.broadcasted_iota(jnp.int32, (rows, rows), 0) == lax.broadcasted_iota(
        jnp.int32, (rows, rows), 1
    )


def merge_kernel(a, b, out):
    rows = a.shape[1] - STAT_ROWS
    eye = diagonal(rows)
    for i in range(a.shape[0]):
        weighted, top, total = joined((a, b), i, rows, eye)
        out[i, :rows, :] = weighted
        out[i, rows : rows + 1, :rows] = top
        out[i, rows + 1 : rows + 2, :rows] = total


def finish_kernel(steps, a, b, c, out, wide):
    rows = a.shape[1] - STAT_ROWS
    slots = a.shape[0]
    eye = diagonal(rows)
    for i in range(slots):
        weighted, _, total = joined((a, b, c), i, rows, eye)
        weighted = weighted / jnp.sum(jnp.where(eye, total, 0.0), axis=1, keepdims=True)
        for h in range(rows // steps):
            wide[h, pl.ds(i, steps, stride=slots), :] = weighted[h * steps : (h + 1) * steps, :]
    for h in range(rows // steps):
        out[:, h * HEAD_DIM : (h + 1) * HEAD_DIM] = wide[h].astype(BF16)


def attend(position, steps, slots, kvl, here, limits, own, other, keys, values, *new):
    heads = 2 * own.shape[2] // HEAD_DIM
    rows, columns = heads * steps, values.shape[2]
    scratch = [
        pltpu.VMEM((heads, steps * slots, HEAD_DIM), F32),
        pltpu.VMEM((slots, rows, columns), F32),
    ]
    if new:
        scratch += [
            pltpu.VMEM((2, kvl, steps * slots, HEAD_DIM), F32),
            pltpu.VMEM((slots, FRESH_ROWS, columns), F32),
            pltpu.VMEM((slots, FRESH_ROWS, columns), F32),
        ]
    return pl.pallas_call(
        functools.partial(attend_kernel, position, steps, slots, kvl),
        out_shape=pltpu.VMEM((slots, rows + STAT_ROWS, HEAD_DIM), F32),
        in_specs=[SMEM] * 2 + [VMEM] * (4 + len(new)),
        out_specs=VMEM,
        scratch_shapes=scratch,
        compiler_params=params(8),
        cost_estimate=QUICK,
        name="attend",
    )(here, limits, *in_vmem(own, other, keys, values, *new))


def merge(a, b):
    return pl.pallas_call(
        merge_kernel,
        out_shape=pltpu.VMEM(a.shape, F32),
        in_specs=[VMEM] * 2,
        out_specs=VMEM,
        compiler_params=params(8),
        cost_estimate=QUICK,
        name="merge",
    )(*in_vmem(a, b))


def per_device(
    step_token_states,
    input_norm_gain,
    wq,
    wkv,
    wo,
    adapter_down,
    adapter_up,
    prompt_cache_pool,
    prompt_slot,
    prompt_cache_length,
    slot_adapter,
    adapter_ranks,
):
    sections = lax.axis_size("section")
    tp_width = lax.axis_size("tp")
    here = jnp.stack([lax.axis_index("section"), lax.axis_index("tp")]).astype(jnp.int32)
    steps, slots, model_width = step_token_states.shape
    requests = prompt_slot.shape[0]
    section_tokens = prompt_cache_pool.shape[2]
    cols_dev = prompt_cache_pool.shape[3]
    adapters, slice_cols, rank = adapter_down.shape
    local_heads = QUERY_HEADS // tp_width
    half_cols = local_heads // 2 * HEAD_DIM
    kvl = max(1, local_heads // PER_KV)
    width = kvl * HEAD_DIM
    rows = steps * slots
    assert sections == 4

    exponents = jnp.arange(HEAD_DIM // 2, dtype=F32) * (2.0 / HEAD_DIM)
    frequency = ROPE_BASE ** (-exponents)
    frequency = jnp.concatenate([frequency, frequency])[None]
    ints = jax.ShapeDtypeStruct((requests,), jnp.int32)
    owners, limits, pick, scale, cosine, sine = pl.pallas_call(
        functools.partial(tables_kernel, slots, section_tokens, adapters),
        out_shape=(ints, ints)
        + (pltpu.VMEM((requests, rank), F32),) * 2
        + (pltpu.VMEM((sections * rows, HEAD_DIM), F32),) * 2,
        in_specs=[SMEM] * 5 + [VMEM],
        out_specs=(SMEM, SMEM) + (VMEM,) * 4,
        compiler_params=params(8),
        cost_estimate=QUICK,
        name="tables",
    )(here, prompt_slot, prompt_cache_length, slot_adapter, adapter_ranks, frequency)

    normed, piece = pl.pallas_call(
        norm_kernel,
        out_shape=(pltpu.VMEM((rows, model_width), BF16), pltpu.VMEM((rows, slice_cols), BF16)),
        in_specs=[SMEM, VMEM, VMEM],
        out_specs=(VMEM, VMEM),
        scratch_shapes=[
            pltpu.VMEM((rows, model_width), F32),
            pltpu.VMEM((model_width // 128, 128), F32),
        ],
        compiler_params=params(8),
        cost_estimate=QUICK,
        name="norm",
    )(here, step_token_states, input_norm_gain.reshape(model_width // 128, 128))
    normed_beside = swap(normed, "section", 1)
    piece_across = swap(piece, "section", 2)
    piece_beside = swap(piece, "section", 1)
    late_down, late_up, _ = lax.optimization_barrier((adapter_down, adapter_up, normed_beside))
    down_beside = swap(late_down, "section", 1)
    up_beside = swap(late_up, "section", 1)

    chunk = min(256, model_width // 2)
    plain_near, held_down = product(
        "query", here, (normed, normed_beside), wq,
        [lambda at: (at[0] & 1) * (half_cols // 128)], half_cols, [F32], chunk, (adapter_down,),
    )
    plain_far = swap(plain_near, "section", 2)
    piece_beside_across = swap(piece_across, "section", 1)
    rank_part = pl.pallas_call(
        functools.partial(down_kernel, steps, slots),
        out_shape=pltpu.VMEM((sections * rows, rank), F32),
        in_specs=[VMEM] * 7,
        out_specs=VMEM,
        compiler_params=params(8),
        cost_estimate=QUICK,
        name="down",
    )(*in_vmem(piece, piece_beside, piece_across, piece_beside_across, pick, held_down, down_beside))
    if tp_width <= 4:
        parts = [rank_part] + [swap(rank_part, "tp", bit) for bit in range(tp_width - 1, 0, -1)]
    else:
        parts = [lax.psum(rank_part, "tp")]

    cache = prompt_cache_pool
    if cols_dev < HEAD_DIM:
        share = HEAD_DIM // cols_dev
        groups = [list(range(g, g + share)) for g in range(0, tp_width, share)]
        cache = lax.all_gather(cache, "tp", axis=3, tiled=True, axis_index_groups=groups)
    cache_ring = min(8, requests)
    *fetched, held_up, fetch_done = pl.pallas_call(
        fetch_kernel,
        out_shape=(pltpu.VMEM((slots, width, section_tokens), BF16),) * sections
        + (pltpu.VMEM((slots, section_tokens, width), BF16),) * sections
        + (pltpu.VMEM(adapter_up.shape, BF16), pltpu.VMEM((8, 128), F32)),
        in_specs=[SMEM, IN_HBM, IN_HBM],
        out_specs=(VMEM,) * (2 * sections + 2),
        scratch_shapes=[
            pltpu.VMEM((cache_ring, section_tokens, width), BF16),
            pltpu.SemaphoreType.DMA((cache_ring,)),
            pltpu.SemaphoreType.DMA((requests,)),
            pltpu.SemaphoreType.DMA((1,)),
        ],
        compiler_params=params(12),
        cost_estimate=QUICK,
        name="fetch",
    )(lax.optimization_barrier((owners, rank_part))[0], in_hbm(cache), in_hbm(adapter_up))
    scale = lax.optimization_barrier((scale, fetch_done))[0]

    pair = pltpu.VMEM((2, rows, half_cols), BF16)
    masked_near, masked_far = pl.pallas_call(
        functools.partial(query_kernel, steps, slots, len(parts)),
        out_shape=(pair, pair),
        in_specs=[SMEM] + [VMEM] * (len(parts) + 8),
        out_specs=(VMEM, VMEM),
        compiler_params=params(8),
        cost_estimate=QUICK,
        name="queries",
    )(here, *in_vmem(*parts, scale, pick, held_up, up_beside, cosine, sine, plain_near, plain_far))
    query_far = add(masked_far, swap(masked_near, "section", 2))
    query_near = add(masked_near, swap(masked_far, "section", 2))
    beside_far = swap(query_far, "section", 1)
    beside_near = swap(query_near, "section", 1)

    late_normed = lax.optimization_barrier((normed, masked_near))[0]
    if tp_width == 4:
        starts = [
            lambda at: jnp.where(at[1] >= 2, width // 128, 0),
            lambda at: jnp.where(at[1] >= 2, 0, width // 128),
        ]
        first, second = product("new_kv", here, (late_normed,), wkv, starts, width, [F32, F32], 1024)
        first = lax.ppermute(first, "tp", [(0, 0), (1, 2), (2, 1), (3, 3)])
        second = lax.ppermute(second, "tp", [(0, 1), (1, 3), (2, 0), (3, 2)])
    else:
        kv_part = jnp.dot(late_normed, wkv, preferred_element_type=F32)
        kv_full = lax.all_gather(kv_part, "tp", axis=1, tiled=True)
        kv_start = here[1] * local_heads // PER_KV * HEAD_DIM
        first = lax.dynamic_slice_in_dim(kv_full, kv_start, width, 1)
        second = lax.dynamic_slice_in_dim(kv_full, KVH * HEAD_DIM + kv_start, width, 1)
        odd = here[1] % 2 == 1
        first, second = jnp.where(odd, second, first), jnp.where(odd, first, second)

    def attend_to(position, own, other, *new):
        return attend(
            position, steps, slots, kvl, here, limits, own, other, fetched[position],
            fetched[sections + position], *new,
        )

    part_beside_across = attend_to(3, query_far, beside_far)
    part_across = attend_to(2, query_far, beside_far)
    across = merge(part_across, swap(part_beside_across, "section", 1))
    far = swap(across, "section", 2)
    late_near, late_beside, _ = lax.optimization_barrier((query_near, beside_near, across))
    part_beside = attend_to(1, late_near, late_beside)
    part_own = attend_to(0, late_near, late_beside, first, second, cosine, sine)
    final = (part_own, swap(part_beside, "section", 1), far)
    if tp_width <= 4:
        quarter = model_width // tp_width
        columns = [
            functools.partial(lambda bit, at: (at[1] ^ bit) * (quarter // 128), bit)
            for bit in range(tp_width)
        ]
        far_columns = columns[: tp_width // 2 - 1 : -1]
        near_columns = columns[tp_width // 2 - 1 :: -1]
        *held_wo, hold_done = pl.pallas_call(
            functools.partial(hold_kernel, far_columns),
            out_shape=(pltpu.VMEM((wo.shape[0], quarter), BF16),) * len(far_columns)
            + (pltpu.VMEM((8, 128), F32),),
            in_specs=[SMEM, IN_HBM],
            out_specs=(VMEM,) * (len(far_columns) + 1),
            scratch_shapes=[pltpu.SemaphoreType.DMA((len(far_columns),))],
            compiler_params=params(8),
            cost_estimate=QUICK,
            name="hold",
        )(lax.optimization_barrier((here, part_own, part_beside))[0], in_hbm(wo))
        final = lax.optimization_barrier((*final, hold_done))[:3]
    attended = pl.pallas_call(
        functools.partial(finish_kernel, steps),
        out_shape=pltpu.VMEM((rows, local_heads * HEAD_DIM), BF16),
        in_specs=[VMEM] * 3,
        out_specs=VMEM,
        scratch_shapes=[pltpu.VMEM((local_heads, rows, HEAD_DIM), F32)],
        compiler_params=params(8),
        cost_estimate=QUICK,
        name="finish",
    )(*in_vmem(*final))

    if tp_width <= 4:
        sent = pl.pallas_call(
            held_output_kernel,
            out_shape=(pltpu.VMEM((rows, quarter), BF16),) * len(held_wo),
            in_specs=[VMEM] * (1 + len(held_wo)),
            out_specs=(VMEM,) * len(held_wo),
            compiler_params=params(8),
            cost_estimate=QUICK,
            name="far_output",
        )(*in_vmem(attended, *held_wo))
        late = lax.optimization_barrier((attended, sent[0]))[0]
        types = [BF16] * (len(near_columns) - 1) + [F32]
        *more, total = product("near_output", here, (late,), wo, near_columns, quarter, types, wo.shape[0] // 8)
        sent = [*sent, *more]
        total = add(total, *[swap(sent[tp_width - 1 - bit], "tp", bit) for bit in range(1, tp_width)])
        blocks = [total] + [swap(total, "tp", bit) for bit in range(1, tp_width)]
        result = pl.pallas_call(
            functools.partial(place_kernel, columns),
            out_shape=jax.ShapeDtypeStruct((rows, model_width), BF16),
            in_specs=[SMEM] + [VMEM] * tp_width,
            out_specs=IN_HBM,
            scratch_shapes=[pltpu.SemaphoreType.DMA((tp_width,))],
            compiler_params=params(8),
            cost_estimate=QUICK,
            name="place",
        )(here, *in_vmem(*blocks))
    else:
        partial_out = jnp.dot(attended, wo, preferred_element_type=F32).astype(BF16)
        result = lax.psum(partial_out, "tp")
    return result.reshape(steps, slots, model_width)


def solution(mesh):
    return jax.shard_map(
        per_device,
        mesh=mesh,
        in_specs=(
            P(None, ("groups", "section"), None),
            P(),
            P(None, "tp"),
            P(None, "tp"),
            P("tp", None),
            P(("groups", "section"), "tp", None),
            P(("groups", "section"), None, "tp"),
            P("groups", None, "section", "tp"),
            P("groups"),
            P("groups"),
            P("groups"),
            P("groups"),
        ),
        out_specs=P(None, ("groups", "section"), None),
        check_vma=False,
    )
```

time: 168 us -> 111 us (0.66)
  matrix products: 34.9 us -> 0 us
  Pallas kernels: 31.6 us -> 51 us
  local copies, waits for them, and re-layouts: 17.2 us -> 1.77 us
  blocking collectives: 14 us -> 0 us
  waiting for transfers between devices: 42 us -> 32.1 us
  other arithmetic: 8.83 us -> 0.16 us
  starting transfers between devices: 18.8 us -> 25.6 us
    dot_general x3 -> x0, matrix products: 34.9 us -> none  [the longest x1 16.5 us: per_device(): partial_out = jnp.dot(attended, wo, preferred_element_type=F32).astype(BF16)]
    pallas_call x7 -> x20, Pallas kernels: 31.6 us -> 51 us  [the longest x3 19.2 us: product(): pl.pallas_call(functools.partial(product_kernel, chunk, len(lefts), start...]
    all_gather x1 -> x0, blocking collectives: 14 us -> none  [per_device(): kv_full = lax.all_gather(kv_part, 'tp', axis=1, tiled=True)]
    ppermute x22 -> x23, waiting for transfers between devices: 42 us -> 30.1 us  [swap(): return jax.tree.map(lambda a: lax.ppermute(a, axis, pairs), value)]
    unnamed x32 -> x12, local copies, waits for them, and re-layouts: 13.3 us -> 1.77 us
    ppermute x0 -> x2, starting transfers between devices: none -> 4.34 us  [the longest x1 3.68 us: per_device(): second = lax.ppermute(second, 'tp', [(0, 1), (1, 3), (2, 0), (3, 2)])]
    ppermute x22 -> x23, starting transfers between devices: 18.8 us -> 21.3 us  [swap(): return jax.tree.map(lambda a: lax.ppermute(a, axis, pairs), value)]
    ppermute x0 -> x2, waiting for transfers between devices: none -> 2.05 us  [the longest x1 2.05 us: per_device(): second = lax.ppermute(second, 'tp', [(0, 1), (1, 3), (2, 0), (3, 2)])]
  transfers between devices with their start and end apart: 22 -> 25, of which waited for: 12 -> 10; matrix products, arithmetic and copies ran while one was open for 15% -> 0% of each run, Pallas kernels for 9% -> 37%
where the time goes in v2:
time: 111 us
  Pallas kernels  51 us (46%)
  waiting for transfers between devices  32.1 us (29%)
  starting transfers between devices  25.6 us (23%)
  local copies, waits for them, and re-layouts  1.77 us (2%)
    ppermute x23, waiting for transfers between devices, swap(): return jax.tree.map(lambda a: lax.ppermute(a, axis, pairs), value)  30.1 us
    ppermute x23, starting transfers between devices, swap(): return jax.tree.map(lambda a: lax.ppermute(a, axis, pairs), value)  21.3 us
    pallas_call x3, Pallas kernels, product(): pl.pallas_call(functools.partial(product_kernel, chunk, len(lefts), start...  19.2 us
    pallas_call x1, Pallas kernels, per_device(): pl.pallas_call(fetch_kernel, out_shape=(pltpu.VMEM((slots, width, section...  8.25 us
    pallas_call x1, Pallas kernels, per_device(): pl.pallas_call(functools.partial(hold_kernel, far_columns), out_shape=(pl...  6.94 us
    pallas_call x4, Pallas kernels, attend(): pl.pallas_call(functools.partial(attend_kernel, position, steps, slots, k...  6.74 us
    ppermute x1, starting transfers between devices, per_device(): second = lax.ppermute(second, 'tp', [(0, 1), (1, 3), (2, 0), (3, 2)])  3.68 us
    pallas_call x1, Pallas kernels, per_device(): pl.pallas_call(held_output_kernel, out_shape=(pltpu.VMEM((rows, quarter),...  2.97 us
  transfers between devices with their start and end apart: 25, of which 10 were waited for; matrix products, arithmetic and copies ran while one was open for 0% of the time, Pallas kernels for 37%

profile of v2, /device:TPU:0, one launch (start us, length us, event | category | flops | bytes accessed | tf_op | source)
XLA Modules:
  0.0 111.1 jit_solution(8499036334794463147)
XLA Ops:
  3.2 1.5 %collective-permute-done.3.refs_1_ = bf16[32,8192]{1,0:T(8,128)(2,1)S(1)} collective-permute-done((bf16[32,8192]{1,0:T(8,128)(2,1)S(1)}, bf16[32,8192]{1,0:T(8,128)(2,1)S(1)}, u32[]{:S(2)}, u32[]{:S(2)}) %collective-permute-start.3) | collective-permute-done | bytes 524320 | tf_op jit(solution)/shard_map/ppermute | solution.py:46
  5.3 2.9 %collective-permute-start.1 = (bf16[32,2048]{1,0:T(8,128)(2,1)S(1)}, bf16[32,2048]{1,0:T(8,128)(2,1)S(1)}, u32[]{:S(2)}, u32[]{:S(2)}) collective-permute-start(bf16[32,2048]{1,0:T(8,128)(2,1)S(1)} %get-tuple-element.46.own), channel_id=1, source_target_pairs={{0,8},{4,12},{8,0},{12,4},{1,9},{5,13},{9,1},{13,5},{2,10},{6,14},... | collective-permute-start | bytes 393224 | tf_op jit(solution)/shard_map/ppermute | solution.py:46
  8.2 3.8 %collective-permute-done.1.across = bf16[32,2048]{1,0:T(8,128)(2,1)S(1)} collective-permute-done((bf16[32,2048]{1,0:T(8,128)(2,1)S(1)}, bf16[32,2048]{1,0:T(8,128)(2,1)S(1)}, u32[]{:S(2)}, u32[]{:S(2)}) %collective-permute-start.1) | collective-permute-done | bytes 131104 | tf_op jit(solution)/shard_map/ppermute | solution.py:46
  12.0 7.7 %query.1 = (f32[64,1024]{1,0:T(8,128)S(1)}, bf16[4,2048,128]{2,1,0:T(8,128)(2,1)S(1)}) custom-call(s32[2]{0:T(128)S(1)} %pad_add_fusion.here, bf16[32,8192]{1,0:T(8,128)(2,1)S(1)} %get-tuple-element.69.refs_0_, bf16[32,8192]{1,0:T(8,128)(2,1)S(1)} %collective-permute-done.3.refs_1_, bf16[8192,2048]{1,0:T(8,128)(2,1)} %refs_2_.1, bf16[4,2048,128]{2,1,0:T(8,128)(2,1)} %refs_3_.1), custom_call_target="tpu_custom_call" | custom-call | flops 1 | bytes 1 | tf_op jit(solution)/shard_map/query/pallas_call | solution.py:138
  19.7 1.8 %collective-permute-start.9 = (f32[64,1024]{1,0:T(8,128)S(1)}, f32[64,1024]{1,0:T(8,128)S(1)}, u32[]{:S(2)}, u32[]{:S(2)}) collective-permute-start(f32[64,1024]{1,0:T(8,128)S(1)} %get-tuple-element.58.refs_10_), channel_id=1, source_target_pairs={{0,8},{4,12},{8,0},{12,4},{1,9},{5,13},{9,1},{13,5},{2,10},{6,14},... | collective-permute-start | bytes 786440 | tf_op jit(solution)/shard_map/ppermute | solution.py:46
  21.6 1.5 %tables.1 = (s32[32]{0:T(128)S(1)}, s32[32]{0:T(128)S(1)}, f32[32,128]{1,0:T(8,128)S(1)}, f32[32,128]{1,0:T(8,128)S(1)}, f32[128,128]{1,0:T(8,128)S(1)}, /*index=5*/f32[128,128]{1,0:T(8,128)S(1)}) custom-call(s32[2]{0:T(128)S(1)} %pad_add_fusion.here, s32[32]{0:T(128)S(1)} %copy-done.2, s32[32]{0:T(128)S(1)} %copy-done.3, s32[32]{0:T(128)S(1)} %copy-done.4, ...), custom_call_target="tpu_custom_call" | custom-call | flops 1 | bytes 1 | tf_op jit(solution)/shard_map/tables/pallas_call | solution.py:477
  23.1 1.3 %down.1.refs_0_ = f32[128,128]{1,0:T(8,128)S(1)} custom-call(bf16[32,2048]{1,0:T(8,128)(2,1)S(1)} %get-tuple-element.46.own, bf16[32,2048]{1,0:T(8,128)(2,1)S(1)} %collective-permute-done.beside, bf16[32,2048]{1,0:T(8,128)(2,1)S(1)} %collective-permute-done.1.across, bf16[32,2048]{1,0:T(8,128)(2,1)S(1)} %collective-permute-done.2.beside_across, ...), custom_call_target="tpu_custom_call" | custom-call | flops 1 | bytes 1 | tf_op jit(solution)/shard_map/down/pallas_call | solution.py:516
  24.4 1.6 %collective-permute-start.7 = (f32[128,128]{1,0:T(8,128)S(1)}, f32[128,128]{1,0:T(8,128)S(1)}, u32[]{:S(2)}, u32[]{:S(2)}) collective-permute-start(f32[128,128]{1,0:T(8,128)S(1)} %down.1.refs_0_), channel_id=1, source_target_pairs={{0,1},{1,0},{2,3},{3,2},{4,5},{5,4},{6,7},{7,6},{8,9},{9,8},{10,11... | collective-permute-start | bytes 196616 | tf_op jit(solution)/shard_map/ppermute | solution.py:46
  26.0 2.6 %collective-permute-start.6 = (f32[128,128]{1,0:T(8,128)S(1)}, f32[128,128]{1,0:T(8,128)S(1)}, u32[]{:S(2)}, u32[]{:S(2)}) collective-permute-start(f32[128,128]{1,0:T(8,128)S(1)} %down.1.refs_0_), channel_id=1, source_target_pairs={{0,2},{1,3},{2,0},{3,1},{4,6},{5,7},{6,4},{7,5},{8,10},{9,11},{10,... | collective-permute-start | bytes 196616 | tf_op jit(solution)/shard_map/ppermute | solution.py:46
  28.8 8.3 %fetch.1 = (bf16[8,256,512]{2,1,0:T(8,128)(2,1)S(1)}, bf16[8,256,512]{2,1,0:T(8,128)(2,1)S(1)}, bf16[8,256,512]{2,1,0:T(8,128)(2,1)S(1)}, bf16[8,256,512]{2,1,0:...) custom-call(s32[32]{0:T(128)S(1)} %get-tuple-element.53.owners, ...), custom_call_target="tpu_custom_call" | custom-call | flops 1 | bytes 1 | tf_op jit(solution)/shard_map/fetch/pallas_call | solution.py:536
  37.1 1.1 %queries.1 = (bf16[2,32,1024]{2,1,0:T(8,128)(2,1)S(1)}, bf16[2,32,1024]{2,1,0:T(8,128)(2,1)S(1)}) custom-call(s32[2]{0:T(128)S(1)} %pad_add_fusion.here, f32[128,128]{1,0:T(8,128)S(1)} %down.1.refs_0_, f32[128,128]{1,0:T(8,128)S(1)} %collective-permute-done.5.refs_1_, f32[128,128]{1,0:T(8,128)S(1)} %collective-permute-done.6.refs_2_, ...), custom_call_target="tpu_custom_call" | custom-call | flops 1 | bytes 1 | tf_op jit(solution)/shard_map/queries/pallas_call | solution.py:556
  38.7 4.7 %collective-permute-done.12.refs_1_ = bf16[2,32,1024]{2,1,0:T(8,128)(2,1)S(1)} collective-permute-done((bf16[2,32,1024]{2,1,0:T(8,128)(2,1)S(1)}, bf16[2,32,1024]{2,1,0:T(8,128)(2,1)S(1)}, u32[]{:S(2)}, u32[]{:S(2)}) %collective-permute-start.12) | collective-permute-done | bytes 131104 | tf_op jit(solution)/shard_map/ppermute | solution.py:46
  43.4 1.3 %collective-permute-done.13.other = bf16[2,32,1024]{2,1,0:T(8,128)(2,1)S(1)} collective-permute-done((bf16[2,32,1024]{2,1,0:T(8,128)(2,1)S(1)}, bf16[2,32,1024]{2,1,0:T(8,128)(2,1)S(1)}, u32[]{:S(2)}, u32[]{:S(2)}) %collective-permute-start.13) | collective-permute-done | bytes 131104 | tf_op jit(solution)/shard_map/ppermute | solution.py:46
  44.8 1.6 %attend.5 = f32[8,72,128]{2,1,0:T(8,128)S(1)} custom-call(s32[2]{0:T(128)S(1)} %pad_add_fusion.here, s32[32]{0:T(128)S(1)} %get-tuple-element.45.limits, bf16[2,32,1024]{2,1,0:T(8,128)(2,1)S(1)} %add.6.own, bf16[2,32,1024]{2,1,0:T(8,128)(2,1)S(1)} %collective-permute-done.13.other, bf16[8,256,512]{2,1,0:T(8,128)(2,1)S(1)} %get-tuple-element.63.keys, ...), custom_call_target="tpu_custom_call" | custom-call | flops 1 | bytes 1 | tf_op jit(solution)/shard_map/attend/pallas_call | solution.py:420
  47.0 5.3 %collective-permute-done.10.refs_1_ = bf16[2,32,1024]{2,1,0:T(8,128)(2,1)S(1)} collective-permute-done((bf16[2,32,1024]{2,1,0:T(8,128)(2,1)S(1)}, bf16[2,32,1024]{2,1,0:T(8,128)(2,1)S(1)}, u32[]{:S(2)}, u32[]{:S(2)}) %collective-permute-start.10) | collective-permute-done | bytes 131104 | tf_op jit(solution)/shard_map/ppermute | solution.py:46
  52.5 1.6 %attend.4.a = f32[8,72,128]{2,1,0:T(8,128)S(1)} custom-call(s32[2]{0:T(128)S(1)} %pad_add_fusion.here, s32[32]{0:T(128)S(1)} %get-tuple-element.45.limits, bf16[2,32,1024]{2,1,0:T(8,128)(2,1)S(1)} %add.6.own, bf16[2,32,1024]{2,1,0:T(8,128)(2,1)S(1)} %collective-permute-done.13.other, bf16[8,256,512]{2,1,0:T(8,128)(2,1)S(1)} %get-tuple-element.61.keys, ...), custom_call_target="tpu_custom_call" | custom-call | flops 1 | bytes 1 | tf_op jit(solution)/shard_map/attend/pallas_call | solution.py:420
  54.3 1.6 %attend.7 = f32[8,72,128]{2,1,0:T(8,128)S(1)} custom-call(s32[2]{0:T(128)S(1)} %pad_add_fusion.here, s32[32]{0:T(128)S(1)} %get-tuple-element.45.limits, bf16[2,32,1024]{2,1,0:T(8,128)(2,1)S(1)} %add.5.own, bf16[2,32,1024]{2,1,0:T(8,128)(2,1)S(1)} %collective-permute-done.11.other, bf16[8,256,512]{2,1,0:T(8,128)(2,1)S(1)} %get-tuple-element.72.keys, ...), custom_call_target="tpu_custom_call" | custom-call | flops 1 | bytes 1 | tf_op jit(solution)/shard_map/attend/pallas_call | solution.py:420
  56.9 4.6 %new_kv.1 = (f32[32,256]{1,0:T(8,128)S(1)}, f32[32,256]{1,0:T(8,128)S(1)}) custom-call(s32[2]{0:T(128)S(1)} %pad_add_fusion.here, bf16[32,8192]{1,0:T(8,128)(2,1)S(1)} %get-tuple-element.69.refs_0_, bf16[8192,512]{1,0:T(8,128)(2,1)} %refs_1_.2), custom_call_target="tpu_custom_call" | custom-call | flops 1 | bytes 1 | tf_op jit(solution)/shard_map/new_kv/pallas_call | solution.py:138
  62.2 3.7 %collective-permute-start.16 = (f32[32,256]{1,0:T(8,128)S(1)}, f32[32,256]{1,0:T(8,128)S(1)}, u32[]{:S(2)}, u32[]{:S(2)}) collective-permute-start(f32[32,256]{1,0:T(8,128)S(1)} %get-tuple-element.71), channel_id=1, source_target_pairs={{0,1},{1,3},{2,0},{3,2},{4,5},{5,7},{6,4},{7,6},{8,9},{9,11},{10,8... | collective-permute-start | bytes 98312 | tf_op jit(solution)/shard_map/ppermute | solution.py:578
  65.9 2.0 %collective-permute-done.16.refs_1_ = f32[32,256]{1,0:T(8,128)S(1)} collective-permute-done((f32[32,256]{1,0:T(8,128)S(1)}, f32[32,256]{1,0:T(8,128)S(1)}, u32[]{:S(2)}, u32[]{:S(2)}) %collective-permute-start.16) | collective-permute-done | bytes 32800 | tf_op jit(solution)/shard_map/ppermute | solution.py:578
  67.9 2.0 %attend.6.a = f32[8,72,128]{2,1,0:T(8,128)S(1)} custom-call(s32[2]{0:T(128)S(1)} %pad_add_fusion.here, s32[32]{0:T(128)S(1)} %get-tuple-element.45.limits, bf16[2,32,1024]{2,1,0:T(8,128)(2,1)S(1)} %add.5.own, bf16[2,32,1024]{2,1,0:T(8,128)(2,1)S(1)} %collective-permute-done.11.other, bf16[8,256,512]{2,1,0:T(8,128)(2,1)S(1)} %get-tuple-element.67.keys, ...), custom_call_target="tpu_custom_call" | custom-call | flops 1 | bytes 1 | tf_op jit(solution)/shard_map/attend/pallas_call | solution.py:420
  69.9 6.9 %hold.1 = (bf16[2048,2048]{1,0:T(8,128)(2,1)S(1)}, bf16[2048,2048]{1,0:T(8,128)(2,1)S(1)}, f32[8,128]{1,0:T(8,128)}) custom-call(s32[2]{0:T(128)S(1)} %pad_add_fusion.here, bf16[2048,8192]{1,0:T(8,128)(2,1)} %refs_1_.3), custom_call_target="tpu_custom_call" | custom-call | flops 1 | bytes 1 | tf_op jit(solution)/shard_map/hold/pallas_call | solution.py:610
  77.2 3.0 %far_output.1 = (bf16[32,2048]{1,0:T(8,128)(2,1)S(1)}, bf16[32,2048]{1,0:T(8,128)(2,1)S(1)}) custom-call(bf16[32,2048]{1,0:T(8,128)(2,1)S(1)} %finish.1.left.refs_0_, bf16[2048,2048]{1,0:T(8,128)(2,1)S(1)} %get-tuple-element.78.refs_0_, bf16[2048,2048]{1,0:T(8,128)(2,1)S(1)} %get-tuple-element.79.refs_1_), custom_call_target="tpu_custom_call" | custom-call | flops 1 | bytes 1 | tf_op jit(solution)/shard_map/far_output/pallas_call | solution.py:634
  80.2 2.9 %collective-permute-start.21 = (bf16[32,2048]{1,0:T(8,128)(2,1)S(1)}, bf16[32,2048]{1,0:T(8,128)(2,1)S(1)}, u32[]{:S(2)}, u32[]{:S(2)}) collective-permute-start(bf16[32,2048]{1,0:T(8,128)(2,1)S(1)} %get-tuple-element.80), channel_id=1, source_target_pairs={{0,3},{1,2},{2,1},{3,0},{4,7},{5,6},{6,5},{7,4},{8,11},{9,10},{10,... | collective-permute-start | bytes 393224 | tf_op jit(solution)/shard_map/ppermute | solution.py:46
  83.5 6.9 %near_output.1 = (bf16[32,2048]{1,0:T(8,128)(2,1)S(1)}, f32[32,2048]{1,0:T(8,128)S(1)}) custom-call(s32[2]{0:T(128)S(1)} %pad_add_fusion.here, bf16[32,2048]{1,0:T(8,128)(2,1)S(1)} %finish.1.left.refs_0_, bf16[2048,8192]{1,0:T(8,128)(2,1)} %refs_1_.3), custom_call_target="tpu_custom_call" | custom-call | flops 1 | bytes 1 | tf_op jit(solution)/shard_map/near_output/pallas_call | solution.py:138
  91.6 2.3 %collective-permute-done.20.refs_2_ = bf16[32,2048]{1,0:T(8,128)(2,1)S(1)} collective-permute-done((bf16[32,2048]{1,0:T(8,128)(2,1)S(1)}, bf16[32,2048]{1,0:T(8,128)(2,1)S(1)}, u32[]{:S(2)}, u32[]{:S(2)}) %collective-permute-start.20) | collective-permute-done | bytes 131104 | tf_op jit(solution)/shard_map/ppermute | solution.py:46
  93.9 2.3 %collective-permute-done.19.refs_1_ = bf16[32,2048]{1,0:T(8,128)(2,1)S(1)} collective-permute-done((bf16[32,2048]{1,0:T(8,128)(2,1)S(1)}, bf16[32,2048]{1,0:T(8,128)(2,1)S(1)}, u32[]{:S(2)}, u32[]{:S(2)}) %collective-permute-start.19) | collective-permute-done | bytes 131104 | tf_op jit(solution)/shard_map/ppermute | solution.py:46
  96.3 1.8 %collective-permute-start.24 = (bf16[32,2048]{1,0:T(8,128)(2,1)S(1)}, bf16[32,2048]{1,0:T(8,128)(2,1)S(1)}, u32[]{:S(2)}, u32[]{:S(2)}) collective-permute-start(bf16[32,2048]{1,0:T(8,128)(2,1)S(1)} %add.7.refs_0_), channel_id=1, source_target_pairs={{0,3},{1,2},{2,1},{3,0},{4,7},{5,6},{6,5},{7,4},{8,11},{9,10},{10,... | collective-permute-start | bytes 393224 | tf_op jit(solution)/shard_map/ppermute | solution.py:46
  98.2 2.5 %collective-permute-start.22 = (bf16[32,2048]{1,0:T(8,128)(2,1)S(1)}, bf16[32,2048]{1,0:T(8,128)(2,1)S(1)}, u32[]{:S(2)}, u32[]{:S(2)}) collective-permute-start(bf16[32,2048]{1,0:T(8,128)(2,1)S(1)} %add.7.refs_0_), channel_id=1, source_target_pairs={{0,1},{1,0},{2,3},{3,2},{4,5},{5,4},{6,7},{7,6},{8,9},{9,8},{10,11... | collective-permute-start | bytes 393224 | tf_op jit(solution)/shard_map/ppermute | solution.py:46
  100.7 3.8 %collective-permute-done.24.refs_3_ = bf16[32,2048]{1,0:T(8,128)(2,1)S(1)} collective-permute-done((bf16[32,2048]{1,0:T(8,128)(2,1)S(1)}, bf16[32,2048]{1,0:T(8,128)(2,1)S(1)}, u32[]{:S(2)}, u32[]{:S(2)}) %collective-permute-start.24) | collective-permute-done | bytes 131104 | tf_op jit(solution)/shard_map/ppermute | solution.py:46
  104.6 5.0 %collective-permute-done.23.refs_2_ = bf16[32,2048]{1,0:T(8,128)(2,1)S(1)} collective-permute-done((bf16[32,2048]{1,0:T(8,128)(2,1)S(1)}, bf16[32,2048]{1,0:T(8,128)(2,1)S(1)}, u32[]{:S(2)}, u32[]{:S(2)}) %collective-permute-start.23) | collective-permute-done | bytes 131104 | tf_op jit(solution)/shard_map/ppermute | solution.py:46
  109.5 1.4 %place.1 = bf16[32,8192]{1,0:T(8,128)(2,1)} custom-call(s32[2]{0:T(128)S(1)} %pad_add_fusion.here, bf16[32,2048]{1,0:T(8,128)(2,1)S(1)} %add.7.refs_0_, bf16[32,2048]{1,0:T(8,128)(2,1)S(1)} %collective-permute-done.22.refs_1_, bf16[32,2048]{1,0:T(8,128)(2,1)S(1)} %collective-permute-done.23.refs_2_, bf16[32,2048]{1,0:T(8,128)(2,1)S(1)} %collective-permute-done.24.refs_3_), custom_call_target="tpu_custom_call" | custom-call | flops 1 | bytes 1 | tf_op jit(solution)/shard_map/place/pallas_call | solution.py:649
  (53 shorter events, 9.3 us)
Async XLA Ops:
  0.1 1.0 copy-start
  1.1 0.7 copy-start.1
  2.7 2.1 %collective-permute-start.3 = (bf16[32,8192]{1,0:T(8,128)(2,1)S(1)}, bf16[32,8192]{1,0:T(8,128)(2,1)S(1)}, u32[]{:S(2)}, u32[]{:S(2)}) collective-permute-start(bf16[32,8192]{1,0:T(8,128)(2,1)S(1)} %get-tuple-element.69.refs_0_), channel_id=1, source_target_pairs={{0,4},{4,0},{8,12},{12,8},{1,5},{5,1},{9,13},{13,9},{2,6},{6,2},{1... | collective-permute-start | bytes 1572872 | tf_op jit(solution)/shard_map/ppermute | solution.py:46
  4.8 18.3 %collective-permute-start.4 = (bf16[4,2048,128]{2,1,0:T(8,128)(2,1)}, bf16[4,2048,128]{2,1,0:T(8,128)(2,1)S(1)}, u32[]{:S(2)}, u32[]{:S(2)}) collective-permute-start(bf16[4,2048,128]{2,1,0:T(8,128)(2,1)} %refs_3_.1), channel_id=1, source_target_pairs={{0,4},{4,0},{8,12},{12,8},{1,5},{5,1},{9,13},{13,9},{2,6},{6,2},{1... | collective-permute-start | bytes 6291464 | tf_op jit(solution)/shard_map/ppermute | solution.py:46
  5.2 31.9 %collective-permute-start.8 = (bf16[4,128,2048]{2,1,0:T(8,128)(2,1)}, bf16[4,128,2048]{2,1,0:T(8,128)(2,1)S(1)}, u32[]{:S(2)}, u32[]{:S(2)}) collective-permute-start(bf16[4,128,2048]{2,1,0:T(8,128)(2,1)} %up.1), channel_id=1, source_target_pairs={{0,4},{4,0},{8,12},{12,8},{1,5},{5,1},{9,13},{13,9},{2,6},{6,2},{1... | collective-permute-start | bytes 6291464 | tf_op jit(solution)/shard_map/ppermute | solution.py:46
  5.3 16.3 %copy-start.2 = (s32[32]{0:T(128)S(1)}, s32[32]{0:T(128)}, u32[]{:S(2)}) copy-start(s32[32]{0:T(128)} %prompt_slot.1) | copy-start | bytes 388
  5.3 16.3 %copy-start.3 = (s32[32]{0:T(128)S(1)}, s32[32]{0:T(128)}, u32[]{:S(2)}) copy-start(s32[32]{0:T(128)} %prompt_length.1) | copy-start | bytes 388
  5.3 16.3 %copy-start.4 = (s32[32]{0:T(128)S(1)}, s32[32]{0:T(128)}, u32[]{:S(2)}) copy-start(s32[32]{0:T(128)} %slot_adapter.1) | copy-start | bytes 388
  5.3 16.3 %copy-start.5 = (s32[16]{0:T(128)S(1)}, s32[16]{0:T(128)}, u32[]{:S(2)}) copy-start(s32[16]{0:T(128)} %ranks.1) | copy-start | bytes 196
  5.3 6.7 %collective-permute-start.1 = (bf16[32,2048]{1,0:T(8,128)(2,1)S(1)}, bf16[32,2048]{1,0:T(8,128)(2,1)S(1)}, u32[]{:S(2)}, u32[]{:S(2)}) collective-permute-start(bf16[32,2048]{1,0:T(8,128)(2,1)S(1)} %get-tuple-element.46.own), channel_id=1, source_target_pairs={{0,8},{4,12},{8,0},{12,4},{1,9},{5,13},{9,1},{13,5},{2,10},{6,14},... | collective-permute-start | bytes 393224 | tf_op jit(solution)/shard_map/ppermute | solution.py:46
  8.2 14.8 %collective-permute-start = (bf16[32,2048]{1,0:T(8,128)(2,1)S(1)}, bf16[32,2048]{1,0:T(8,128)(2,1)S(1)}, u32[]{:S(2)}, u32[]{:S(2)}) collective-permute-start(bf16[32,2048]{1,0:T(8,128)(2,1)S(1)} %get-tuple-element.46.own), channel_id=1, source_target_pairs={{0,4},{4,0},{8,12},{12,8},{1,5},{5,1},{9,13},{13,9},{2,6},{6,2},{1... | collective-permute-start | bytes 393224 | tf_op jit(solution)/shard_map/ppermute | solution.py:46
  12.0 11.1 %collective-permute-start.2 = (bf16[32,2048]{1,0:T(8,128)(2,1)S(1)}, bf16[32,2048]{1,0:T(8,128)(2,1)S(1)}, u32[]{:S(2)}, u32[]{:S(2)}) collective-permute-start(bf16[32,2048]{1,0:T(8,128)(2,1)S(1)} %collective-permute-done.1.across), channel_id=1, source_target_pairs={{0,4},{4,0},{8,12},{12,8},{1,5},{5,1},{9,13},{13,9},{2,6},{6,2},{1... | collective-permute-start | bytes 393224 | tf_op jit(solution)/shard_map/ppermute | solution.py:46
  19.7 17.4 %collective-permute-start.9 = (f32[64,1024]{1,0:T(8,128)S(1)}, f32[64,1024]{1,0:T(8,128)S(1)}, u32[]{:S(2)}, u32[]{:S(2)}) collective-permute-start(f32[64,1024]{1,0:T(8,128)S(1)} %get-tuple-element.58.refs_10_), channel_id=1, source_target_pairs={{0,8},{4,12},{8,0},{12,4},{1,9},{5,13},{9,1},{13,5},{2,10},{6,14},... | collective-permute-start | bytes 786440 | tf_op jit(solution)/shard_map/ppermute | solution.py:46
  24.4 12.7 %collective-permute-start.7 = (f32[128,128]{1,0:T(8,128)S(1)}, f32[128,128]{1,0:T(8,128)S(1)}, u32[]{:S(2)}, u32[]{:S(2)}) collective-permute-start(f32[128,128]{1,0:T(8,128)S(1)} %down.1.refs_0_), channel_id=1, source_target_pairs={{0,1},{1,0},{2,3},{3,2},{4,5},{5,4},{6,7},{7,6},{8,9},{9,8},{10,11... | collective-permute-start | bytes 196616 | tf_op jit(solution)/shard_map/ppermute | solution.py:46
  26.0 11.1 %collective-permute-start.6 = (f32[128,128]{1,0:T(8,128)S(1)}, f32[128,128]{1,0:T(8,128)S(1)}, u32[]{:S(2)}, u32[]{:S(2)}) collective-permute-start(f32[128,128]{1,0:T(8,128)S(1)} %down.1.refs_0_), channel_id=1, source_target_pairs={{0,2},{1,3},{2,0},{3,1},{4,6},{5,7},{6,4},{7,5},{8,10},{9,11},{10,... | collective-permute-start | bytes 196616 | tf_op jit(solution)/shard_map/ppermute | solution.py:46
  28.6 8.5 %collective-permute-start.5 = (f32[128,128]{1,0:T(8,128)S(1)}, f32[128,128]{1,0:T(8,128)S(1)}, u32[]{:S(2)}, u32[]{:S(2)}) collective-permute-start(f32[128,128]{1,0:T(8,128)S(1)} %down.1.refs_0_), channel_id=1, source_target_pairs={{0,3},{1,2},{2,1},{3,0},{4,7},{5,6},{6,5},{7,4},{8,11},{9,10},{10,... | collective-permute-start | bytes 196616 | tf_op jit(solution)/shard_map/ppermute | solution.py:46
  38.3 5.0 %collective-permute-start.12 = (bf16[2,32,1024]{2,1,0:T(8,128)(2,1)S(1)}, bf16[2,32,1024]{2,1,0:T(8,128)(2,1)S(1)}, u32[]{:S(2)}, u32[]{:S(2)}) collective-permute-start(bf16[2,32,1024]{2,1,0:T(8,128)(2,1)S(1)} %get-tuple-element.59.refs_0_), channel_id=1, source_target_pairs={{0,8},{4,12},{8,0},{12,4},{1,9},{5,13},{9,1},{13,5},{2,10},{6,14},... | collective-permute-start | bytes 393224 | tf_op jit(solution)/shard_map/ppermute | solution.py:46
  43.4 1.4 %collective-permute-start.13 = (bf16[2,32,1024]{2,1,0:T(8,128)(2,1)S(1)}, bf16[2,32,1024]{2,1,0:T(8,128)(2,1)S(1)}, u32[]{:S(2)}, u32[]{:S(2)}) collective-permute-start(bf16[2,32,1024]{2,1,0:T(8,128)(2,1)S(1)} %add.6.own), channel_id=1, source_target_pairs={{0,4},{4,0},{8,12},{12,8},{1,5},{5,1},{9,13},{13,9},{2,6},{6,2},{1... | collective-permute-start | bytes 393224 | tf_op jit(solution)/shard_map/ppermute | solution.py:46
  46.4 7.7 %collective-permute-start.14 = (f32[8,72,128]{2,1,0:T(8,128)S(1)}, f32[8,72,128]{2,1,0:T(8,128)S(1)}, u32[]{:S(2)}, u32[]{:S(2)}) collective-permute-start(f32[8,72,128]{2,1,0:T(8,128)S(1)} %attend.5), channel_id=1, source_target_pairs={{0,4},{4,0},{8,12},{12,8},{1,5},{5,1},{9,13},{13,9},{2,6},{6,2},{1... | collective-permute-start | bytes 884744 | tf_op jit(solution)/shard_map/ppermute | solution.py:46
  46.6 5.8 %collective-permute-start.10 = (bf16[2,32,1024]{2,1,0:T(8,128)(2,1)S(1)}, bf16[2,32,1024]{2,1,0:T(8,128)(2,1)S(1)}, u32[]{:S(2)}, u32[]{:S(2)}) collective-permute-start(bf16[2,32,1024]{2,1,0:T(8,128)(2,1)S(1)} %get-tuple-element.60.refs_0_), channel_id=1, source_target_pairs={{0,8},{4,12},{8,0},{12,4},{1,9},{5,13},{9,1},{13,5},{2,10},{6,14},... | collective-permute-start | bytes 393224 | tf_op jit(solution)/shard_map/ppermute | solution.py:46
  52.4 1.9 %collective-permute-start.11 = (bf16[2,32,1024]{2,1,0:T(8,128)(2,1)S(1)}, bf16[2,32,1024]{2,1,0:T(8,128)(2,1)S(1)}, u32[]{:S(2)}, u32[]{:S(2)}) collective-permute-start(bf16[2,32,1024]{2,1,0:T(8,128)(2,1)S(1)} %add.5.own), channel_id=1, source_target_pairs={{0,4},{4,0},{8,12},{12,8},{1,5},{5,1},{9,13},{13,9},{2,6},{6,2},{1... | collective-permute-start | bytes 393224 | tf_op jit(solution)/shard_map/ppermute | solution.py:46
  55.9 20.9 %collective-permute-start.17 = (f32[8,72,128]{2,1,0:T(8,128)S(1)}, f32[8,72,128]{2,1,0:T(8,128)S(1)}, u32[]{:S(2)}, u32[]{:S(2)}) collective-permute-start(f32[8,72,128]{2,1,0:T(8,128)S(1)} %attend.7), channel_id=1, source_target_pairs={{0,4},{4,0},{8,12},{12,8},{1,5},{5,1},{9,13},{13,9},{2,6},{6,2},{1... | collective-permute-start | bytes 884744 | tf_op jit(solution)/shard_map/ppermute | solution.py:46
  56.5 20.4 %collective-permute-start.18 = (f32[8,72,128]{2,1,0:T(8,128)S(1)}, f32[8,72,128]{2,1,0:T(8,128)S(1)}, u32[]{:S(2)}, u32[]{:S(2)}) collective-permute-start(f32[8,72,128]{2,1,0:T(8,128)S(1)} %merge.1), channel_id=1, source_target_pairs={{0,8},{4,12},{8,0},{12,4},{1,9},{5,13},{9,1},{13,5},{2,10},{6,14},... | collective-permute-start | bytes 884744 | tf_op jit(solution)/shard_map/ppermute | solution.py:46
  61.5 4.4 %collective-permute-start.15 = (f32[32,256]{1,0:T(8,128)S(1)}, f32[32,256]{1,0:T(8,128)S(1)}, u32[]{:S(2)}, u32[]{:S(2)}) collective-permute-start(f32[32,256]{1,0:T(8,128)S(1)} %get-tuple-element.70), channel_id=1, source_target_pairs={{0,0},{1,2},{2,1},{3,3},{4,4},{5,6},{6,5},{7,7},{8,8},{9,10},{10,9... | collective-permute-start | bytes 98312 | tf_op jit(solution)/shard_map/ppermute | solution.py:577
  62.2 5.7 %collective-permute-start.16 = (f32[32,256]{1,0:T(8,128)S(1)}, f32[32,256]{1,0:T(8,128)S(1)}, u32[]{:S(2)}, u32[]{:S(2)}) collective-permute-start(f32[32,256]{1,0:T(8,128)S(1)} %get-tuple-element.71), channel_id=1, source_target_pairs={{0,1},{1,3},{2,0},{3,2},{4,5},{5,7},{6,4},{7,6},{8,9},{9,11},{10,8... | collective-permute-start | bytes 98312 | tf_op jit(solution)/shard_map/ppermute | solution.py:578
  80.2 13.7 %collective-permute-start.21 = (bf16[32,2048]{1,0:T(8,128)(2,1)S(1)}, bf16[32,2048]{1,0:T(8,128)(2,1)S(1)}, u32[]{:S(2)}, u32[]{:S(2)}) collective-permute-start(bf16[32,2048]{1,0:T(8,128)(2,1)S(1)} %get-tuple-element.80), channel_id=1, source_target_pairs={{0,3},{1,2},{2,1},{3,0},{4,7},{5,6},{6,5},{7,4},{8,11},{9,10},{10,... | collective-permute-start | bytes 393224 | tf_op jit(solution)/shard_map/ppermute | solution.py:46
  83.1 10.8 %collective-permute-start.20 = (bf16[32,2048]{1,0:T(8,128)(2,1)S(1)}, bf16[32,2048]{1,0:T(8,128)(2,1)S(1)}, u32[]{:S(2)}, u32[]{:S(2)}) collective-permute-start(bf16[32,2048]{1,0:T(8,128)(2,1)S(1)} %get-tuple-element.84), channel_id=1, source_target_pairs={{0,2},{1,3},{2,0},{3,1},{4,6},{5,7},{6,4},{7,5},{8,10},{9,11},{10,... | collective-permute-start | bytes 393224 | tf_op jit(solution)/shard_map/ppermute | solution.py:46
  90.5 5.7 %collective-permute-start.19 = (bf16[32,2048]{1,0:T(8,128)(2,1)S(1)}, bf16[32,2048]{1,0:T(8,128)(2,1)S(1)}, u32[]{:S(2)}, u32[]{:S(2)}) collective-permute-start(bf16[32,2048]{1,0:T(8,128)(2,1)S(1)} %get-tuple-element.83), channel_id=1, source_target_pairs={{0,1},{1,0},{2,3},{3,2},{4,5},{5,4},{6,7},{7,6},{8,9},{9,8},{10,11... | collective-permute-start | bytes 393224 | tf_op jit(solution)/shard_map/ppermute | solution.py:46
  96.3 8.3 %collective-permute-start.24 = (bf16[32,2048]{1,0:T(8,128)(2,1)S(1)}, bf16[32,2048]{1,0:T(8,128)(2,1)S(1)}, u32[]{:S(2)}, u32[]{:S(2)}) collective-permute-start(bf16[32,2048]{1,0:T(8,128)(2,1)S(1)} %add.7.refs_0_), channel_id=1, source_target_pairs={{0,3},{1,2},{2,1},{3,0},{4,7},{5,6},{6,5},{7,4},{8,11},{9,10},{10,... | collective-permute-start | bytes 393224 | tf_op jit(solution)/shard_map/ppermute | solution.py:46
  98.1 11.5 %collective-permute-start.23 = (bf16[32,2048]{1,0:T(8,128)(2,1)S(1)}, bf16[32,2048]{1,0:T(8,128)(2,1)S(1)}, u32[]{:S(2)}, u32[]{:S(2)}) collective-permute-start(bf16[32,2048]{1,0:T(8,128)(2,1)S(1)} %add.7.refs_0_), channel_id=1, source_target_pairs={{0,2},{1,3},{2,0},{3,1},{4,6},{5,7},{6,4},{7,5},{8,10},{9,11},{10,... | collective-permute-start | bytes 393224 | tf_op jit(solution)/shard_map/ppermute | solution.py:46
  98.2 11.4 %collective-permute-start.22 = (bf16[32,2048]{1,0:T(8,128)(2,1)S(1)}, bf16[32,2048]{1,0:T(8,128)(2,1)S(1)}, u32[]{:S(2)}, u32[]{:S(2)}) collective-permute-start(bf16[32,2048]{1,0:T(8,128)(2,1)S(1)} %add.7.refs_0_), channel_id=1, source_target_pairs={{0,1},{1,0},{2,3},{3,2},{4,5},{5,4},{6,7},{7,6},{8,9},{9,8},{10,11... | collective-permute-start | bytes 393224 | tf_op jit(solution)/shard_map/ppermute | solution.py:46

commit v3 on v2

v3 whole, which is shorter than its diff:
```python
import functools
import math

import jax
import jax.numpy as jnp
from jax import lax
from jax.experimental import pallas as pl
from jax.experimental.pallas import tpu as pltpu
from jax.sharding import PartitionSpec as P

QUERY_HEADS = 64
KVH = 8
HEAD_DIM = 128
PER_KV = QUERY_HEADS // KVH

EPSILON = 1e-05
ROPE_BASE = 500000.0
ADAPTER_ALPHA = 16.0
NEGATIVE = -1e30
STAT_ROWS = 8
FRESH_ROWS = 16
AHEAD = 6
CUTS = 4
F32 = jnp.float32
BF16 = jnp.bfloat16
VMEM = pl.BlockSpec(memory_space=pltpu.VMEM)
SMEM = pl.BlockSpec(memory_space=pltpu.SMEM)
IN_HBM = pl.BlockSpec(memory_space=pltpu.HBM)
ANYWHERE = pl.BlockSpec(memory_space=pl.ANY)
QUICK = pl.CostEstimate(flops=1, bytes_accessed=1, transcendentals=0)


def in_hbm(value):
    return pltpu.with_memory_space_constraint(value, pltpu.HBM)


def in_vmem(*values):
    return [pltpu.with_memory_space_constraint(value, pltpu.VMEM) for value in values]


def params(mebibytes):
    return pltpu.CompilerParams(vmem_limit_bytes=mebibytes * 1024 * 1024)


def swap(value, axis, bit):
    size = lax.axis_size(axis)
    pairs = [(i, i ^ bit) for i in range(size)]
    return jax.tree.map(lambda a: lax.ppermute(a, axis, pairs), value)


def tables(slots, section_tokens, adapters, here, prompt_slot, prompt_length, slot_adapter, ranks, frequency, *outs):
    owners, limits, pick, scale, cosine, sine = outs
    section = here[0]
    requests = owners.shape[0]
    shape = pick.shape
    row = lax.broadcasted_iota(jnp.int32, shape, 0)
    lane = lax.broadcasted_iota(jnp.int32, shape, 1)

    def place(slot):
        return (lax.div(slot, slots) ^ section) * slots + lax.rem(slot, slots)

    lengths = jnp.zeros(shape, jnp.int32)
    adapter = jnp.zeros(shape, jnp.int32)
    rank = jnp.zeros(shape, jnp.int32)
    for i in range(requests):
        at, length = place(prompt_slot[i]), prompt_length[i]
        owners[at] = i
        limits[at] = jnp.clip(length - section * section_tokens, 0, section_tokens)
        lengths = jnp.where(row == at, length, lengths)
        at, chosen = place(i), slot_adapter[i]
        adapter = jnp.where(row == at, chosen, adapter)
        rank = jnp.where(row == at, ranks[chosen], rank)
    held = jnp.where(lane < adapters, section * adapters + lane, (section ^ 1) * adapters + lane - adapters)
    pick[...] = jnp.where((lane < 2 * adapters) & (adapter == held), 1.0, 0.0)
    rank_f32 = rank.astype(F32)
    scale[...] = jnp.where(lane < rank, ADAPTER_ALPHA / rank_f32, 0.0)
    steps = cosine.shape[0] // requests
    positions = by_row(lengths, steps, slots).astype(F32)
    step = lax.rem(lax.div(lax.broadcasted_iota(jnp.int32, cosine.shape, 0), slots), steps)
    angles = (positions + step.astype(F32)) * frequency[...]
    cosine[...] = jnp.cos(angles)
    low = lax.broadcasted_iota(jnp.int32, cosine.shape, 1) < HEAD_DIM // 2
    sine[...] = jnp.where(low, -jnp.sin(angles), jnp.sin(angles))


def start_kernel(section_tokens, adapters, here, *refs):
    slot_arrays, frequency, refs = refs[:4], refs[4], refs[5:]
    states, gain, normed, piece, *outs, wide, gains, states_in, gain_in, sems = refs[:-4]
    slot_refs = refs[-4:]
    steps, slots, width = states.shape
    copies = [
        pltpu.make_async_copy(gain, gain_in, sems.at[0]),
        pltpu.make_async_copy(states, states_in, sems.at[1]),
    ]
    small = [
        pltpu.make_async_copy(source, target, sems.at[2 + i])
        for i, (source, target) in enumerate(zip(slot_arrays, slot_refs))
    ]
    for copy in small + copies:
        copy.start()
    for copy in small:
        copy.wait()
    tables(slots, section_tokens, adapters, here, *slot_refs, frequency, *outs)
    for copy in copies:
        copy.wait()
    gains[...] = gain_in[...].astype(F32)
    for t in range(steps):
        values = states_in[t].astype(F32)
        inverse = lax.rsqrt(jnp.mean(values * values, axis=-1, keepdims=True) + EPSILON)
        for c in range(width // 128):
            cols = slice(c * 128, (c + 1) * 128)
            wide[t * slots : (t + 1) * slots, cols] = values[:, cols] * inverse * gains[c : c + 1, :]
    normed[...] = wide[...].astype(BF16)
    cols = piece.shape[1]
    piece[...] = wide[:, pl.ds(pl.multiple_of(here[1] * cols, 128), cols)].astype(BF16)


class Stream:
    def __init__(self, here, rights, jobs, held, sems):
        self.items = [
            (j, i) for j, job in enumerate(jobs) for i in range(rights[job[0]].shape[0] // job[3])
        ]
        self.here, self.rights, self.jobs, self.held, self.sems = here, rights, jobs, held, sems
        for n in range(min(AHEAD, len(self.items))):
            self.copy(n).start()

    def copy(self, n):
        j, i = self.items[n]
        which, start, cols, chunk = self.jobs[j]
        first = pl.multiple_of(start(self.here) * 128, 128)
        source = self.rights[which].at[pl.ds(i * chunk, chunk), pl.ds(first, cols)]
        held = self.held[j]
        return pltpu.make_async_copy(source, held.at[i % held.shape[0]], self.sems.at[n])

    def multiply(self, left_rows, outs):
        for n, (j, i) in enumerate(self.items):
            chunk, held = self.jobs[j][3], self.held[j]
            self.copy(n).wait()
            part = jnp.dot(
                left_rows(i * chunk, chunk), held[i % held.shape[0]], preferred_element_type=F32
            )
            total = part if i == 0 else total + part
            if n + AHEAD < len(self.items):
                self.copy(n + AHEAD).start()
            if (i + 1) * chunk == self.rights[self.jobs[j][0]].shape[0]:
                outs[j][...] = total.astype(outs[j].dtype)


def stream_scratch(rights, jobs):
    counts = [rights[which].shape[0] // chunk for which, _, _, chunk in jobs]
    return [
        pltpu.VMEM((min(AHEAD, count), chunk, cols), BF16)
        for count, (_, _, cols, chunk) in zip(counts, jobs)
    ] + [pltpu.SemaphoreType.DMA((sum(counts),))]


def product_kernel(sizes, jobs, here, *refs):
    refs = list(refs)

    def take(count):
        taken = refs[:count]
        del refs[:count]
        return taken

    lefts, rights, sources, _ = [take(size) for size in sizes]
    outs, targets = take(len(jobs)), take(len(sources))
    held, (sems, carry_sems) = take(len(jobs)), refs
    stream = Stream(here, rights, jobs, held, sems)
    carries = [
        pltpu.make_async_copy(source, target, carry_sems.at[i])
        for i, (source, target) in enumerate(zip(sources, targets))
    ]
    for carry in carries:
        carry.start()
    stream.multiply(
        lambda first, count: jnp.concatenate([ref[:, first : first + count] for ref in lefts], axis=0), outs
    )
    for carry in carries:
        carry.wait()


def product(name, here, lefts, rights, jobs, types, carried=(), after=()):
    rows = sum(left.shape[0] for left in lefts)
    sizes = (len(lefts), len(rights), len(carried), len(after))
    return pl.pallas_call(
        functools.partial(product_kernel, sizes, jobs),
        out_shape=tuple(pltpu.VMEM((rows, job[2]), dtype) for job, dtype in zip(jobs, types))
        + tuple(pltpu.VMEM(c.shape, c.dtype) for c in carried),
        in_specs=[SMEM] + [VMEM] * len(lefts) + [IN_HBM] * (len(rights) + len(carried)) + [ANYWHERE] * len(after),
        out_specs=(VMEM,) * (len(types) + len(carried)),
        scratch_shapes=stream_scratch(rights, jobs) + [pltpu.SemaphoreType.DMA((max(1, len(carried)),))],
        compiler_params=params(20),
        cost_estimate=QUICK,
        name=name,
    )(here, *in_vmem(*lefts), *[in_hbm(c) for c in (*rights, *carried)], *after)


def cross_add_kernel(own, across, after, out):
    for p in range(own.shape[0]):
        out[p] = (own[p].astype(F32) + across[p ^ 2].astype(F32)).astype(out.dtype)


def add_kernel(*refs):
    *terms, out = refs
    total = terms[0][...].astype(F32)
    for term in terms[1:]:
        total = total + term[...].astype(F32)
    out[...] = total.astype(out.dtype)


def add(*terms):
    return pl.pallas_call(
        add_kernel,
        out_shape=pltpu.VMEM(terms[0].shape, BF16),
        in_specs=[VMEM] * len(terms),
        out_specs=VMEM,
        compiler_params=params(8),
        cost_estimate=QUICK,
        name="add",
    )(*in_vmem(*terms))


def by_row(table, steps, slots):
    blocks = [table[i : i + slots] for i in range(0, table.shape[0], slots)]
    return jnp.concatenate([block for block in blocks for _ in range(steps)], axis=0)


def down_kernel(steps, slots, here, own, beside, across, beside_across, pick, down, down_beside, kv, *outs):
    states = jnp.concatenate([ref[...] for ref in (own, beside, across, beside_across)], axis=0)
    picks = by_row(pick[...], steps, slots)
    adapters = down.shape[0]
    rows, rank = states.shape[0], down.shape[2]
    total = jnp.zeros((rows, rank), F32)
    for a in range(2 * adapters):
        part = jnp.dot(states, (down, down_beside)[a // adapters][a % adapters], preferred_element_type=F32)
        total = jnp.where(picks[:, a : a + 1] > 0, part, total)
    half = kv.shape[1] // 2
    new_rows = steps * slots
    for bit, out in enumerate(outs):
        out[:rows, :] = total
        if bit == 0:
            continue
        upper = here[1] == (0, 0, 1, 2)[bit]
        for k in range(half // HEAD_DIM):
            low = kv[:new_rows, k * HEAD_DIM : (k + 1) * HEAD_DIM]
            high = kv[:new_rows, half + k * HEAD_DIM : half + (k + 1) * HEAD_DIM]
            out[rows + k * new_rows : rows + (k + 1) * new_rows, :] = jnp.where(upper, high, low)


def query_kernel(steps, slots, count, here, after, *refs):
    parts, refs = refs[:count], refs[count:]
    scale, pick, up, up_beside, cosine, sine, plain_near, plain_far, out = refs
    all_rows = cosine.shape[0]
    rank_sum = parts[0][:all_rows, :]
    for part in parts[1:]:
        rank_sum = rank_sum + part[:all_rows, :]
    scales = by_row(scale[...], steps, slots)
    picks = by_row(pick[...], steps, slots)
    low_rank = jnp.where(scales > 0, rank_sum * scales, 0.0)
    adapters, rank, width = up.shape
    wide = jnp.concatenate(
        [jnp.where(picks[:, a : a + 1] > 0, low_rank, 0.0) for a in range(2 * adapters)], axis=1
    ).astype(BF16)
    depth = adapters * rank
    ups = [ref.reshape(depth, width) for ref in (up, up_beside)]
    half = plain_near.shape[1]
    rows = steps * slots
    shown = jnp.sum(picks, axis=1, keepdims=True) > 0
    first = (here[0] & 1) * half
    step = min(2 * HEAD_DIM, half)
    for c in range(0, half, step):
        block = pl.ds(pl.multiple_of(first + c, 128), step)
        changes = jnp.dot(wide[:, :depth], ups[0][:, block], preferred_element_type=F32)
        changes = changes + jnp.dot(wide[:, depth:], ups[1][:, block], preferred_element_type=F32)
        for h in range(0, step, HEAD_DIM):
            cols = slice(c + h, c + h + HEAD_DIM)
            plain = jnp.concatenate([plain_near[:, cols], plain_far[:, cols]], axis=0)
            query = plain + changes[:, h : h + HEAD_DIM]
            turned = query * cosine[...] + pltpu.roll(query, HEAD_DIM // 2, 1) * sine[...]
            turned = jnp.where(shown, turned, 0.0).astype(BF16)
            for position in range(4):
                out[position, :, cols] = turned[position * rows : (position + 1) * rows]


def fetch_kernel(places, slots, starts, here, owners, cache, after, *refs):
    sections = len(places)
    *refs, held, key_sems, value_sems, up_sem = refs
    carried = len(refs) // 2 - sections
    ups, outs, targets, done = refs[:carried], refs[carried:][: 2 * sections], refs[carried + 2 * sections : -1], refs[-1]
    ring = held.shape[0]
    count = sections * slots
    order = [(p, i) for p in range(sections) for i in range(slots)]

    def part(up, start, target):
        if start is None:
            return up
        return up.at[:, pl.ds(pl.multiple_of(start(here) * 128, 128), target.shape[1])]

    up_copies = [
        pltpu.make_async_copy(part(up, start, target), target, up_sem.at[0])
        for up, start, target in zip(ups, starts, targets)
    ]

    def key_copy(n):
        position, i = order[n]
        source = cache.at[owners[places[position] * slots + i], 0]
        return pltpu.make_async_copy(source, held.at[n % ring], key_sems.at[n % ring])

    def value_copy(n):
        position, i = order[n]
        source = cache.at[owners[places[position] * slots + i], 1]
        return pltpu.make_async_copy(source, outs[sections + position].at[i], value_sems.at[n])

    for n in range(ring):
        key_copy(n).start()
        value_copy(n).start()
    for copy in up_copies:
        copy.start()
    for n in range(count):
        position, i = order[n]
        key_copy(n).wait()
        outs[position][i] = held[n % ring].T
        if n + ring < count:
            key_copy(n + ring).start()
            value_copy(n + ring).start()
    done[...] = jnp.zeros_like(done)
    for copy in up_copies:
        copy.wait()
    for n in range(count):
        value_copy(n).wait()


def hold_kernel(starts, here, source, after, *refs):
    *outs, sems = refs
    cols = outs[0].shape[1]
    copies = []
    for i, out in enumerate(outs):
        first = pl.multiple_of(starts[i](here) * 128, 128)
        copies.append(pltpu.make_async_copy(source.at[:, pl.ds(first, cols)], out, sems.at[i]))
    for copy in copies:
        copy.start()
    for copy in copies:
        copy.wait()


def place_kernel(starts, here, *refs):
    *blocks, out, sems = refs
    copies = []
    for i, block in enumerate(blocks):
        cols = block.shape[1]
        first = pl.multiple_of(starts[i](here) * 128, 128)
        copies.append(pltpu.make_async_copy(block, out.at[:, pl.ds(first, cols)], sems.at[i]))
    for copy in copies:
        copy.start()
    for copy in copies:
        copy.wait()


def attend_kernel(position, steps, slots, kvl, here, limits, after, own, other, keys, values, *refs):
    fresh = position == 0
    if fresh:
        kv, *received, cosine, sine, out, qf, qs, turned, nk, nv = refs
    else:
        out, qf, qs = refs
    half = own.shape[2] // HEAD_DIM
    heads = 2 * half
    per_kv = heads // kvl
    rows = heads * steps
    tokens = values.shape[1]
    root = 1.0 / math.sqrt(HEAD_DIM)
    qs[...] = jnp.zeros_like(qs)
    lower = here[0] & 1 == 0
    for h in range(half):
        cols = slice(h * HEAD_DIM, (h + 1) * HEAD_DIM)
        mine = own[position, :, cols].astype(F32)
        theirs = other[position ^ 1, :, cols].astype(F32)
        qf[h] = jnp.where(lower, mine, theirs)
        qf[half + h] = jnp.where(lower, theirs, mine)
    for i in range(slots):
        for h in range(heads):
            k = h // per_kv
            qs[i, h * steps : (h + 1) * steps, k * HEAD_DIM : (k + 1) * HEAD_DIM] = qf[
                h, pl.ds(i, steps, stride=slots), :
            ]
    if fresh:
        step_of_row = lax.broadcasted_iota(jnp.int32, (rows, FRESH_ROWS), 0) % steps
        fresh_valid = lax.broadcasted_iota(jnp.int32, (rows, FRESH_ROWS), 1) <= step_of_row
        rows_here = steps * slots
        nk[...] = jnp.zeros_like(nk)
        nv[...] = jnp.zeros_like(nv)
        for k in range(kvl):
            cols = slice(k * HEAD_DIM, (k + 1) * HEAD_DIM)
            if received:
                tp, half_kv = here[1], kvl * HEAD_DIM
                first = cosine.shape[0] + k * rows_here
                one, two, three = [ref[first : first + rows_here, :] for ref in received]
                low, high = kv[:rows_here, cols], kv[:rows_here, half_kv + k * HEAD_DIM : half_kv + (k + 1) * HEAD_DIM]
                key = jnp.where(tp == 0, low, jnp.where(tp == 1, one, jnp.where(tp == 2, three, two)))
                value = jnp.where(tp == 0, two, jnp.where(tp == 1, three, jnp.where(tp == 2, one, high)))
            else:
                key, value = kv[:, cols], kv[:, (kvl + k) * HEAD_DIM : (kvl + k + 1) * HEAD_DIM]
            turned[0, k] = key * cosine[:rows_here, :] + pltpu.roll(key, HEAD_DIM // 2, 1) * sine[:rows_here, :]
            turned[1, k] = value
            for i in range(slots):
                nk[i, :steps, cols] = turned[0, k, pl.ds(i, steps, stride=slots), :]
                nv[i, :steps, cols] = turned[1, k, pl.ds(i, steps, stride=slots), :]
    eye = diagonal(rows)
    token = lax.broadcasted_iota(jnp.int32, (rows, tokens), 1)
    for i in range(slots):
        limit = limits[position * slots + i]
        queries = qs[i].astype(BF16)
        scores = jnp.dot(queries, keys[i], preferred_element_type=F32) * root
        valid = token < limit
        scores = jnp.where(valid, scores, NEGATIVE)
        top = jnp.max(scores, axis=1, keepdims=True)
        if fresh:
            new_scores = lax.dot_general(
                queries, nk[i].astype(BF16), (((1,), (1,)), ((), ())), preferred_element_type=F32
            )
            new_scores = jnp.where(fresh_valid, new_scores * root, NEGATIVE)
            top = jnp.maximum(top, jnp.max(new_scores, axis=1, keepdims=True))
        weights = jnp.where(valid, jnp.exp(scores - top), 0.0)
        total = jnp.sum(weights, axis=1, keepdims=True)
        value = jnp.dot(weights.astype(BF16), values[i], preferred_element_type=F32)
        if fresh:
            new_weights = jnp.where(fresh_valid, jnp.exp(new_scores - top), 0.0)
            total = total + jnp.sum(new_weights, axis=1, keepdims=True)
            value = value + jnp.dot(
                new_weights.astype(BF16), nv[i].astype(BF16), preferred_element_type=F32
            )
        for k in range(kvl):
            block = slice(k * per_kv * steps, (k + 1) * per_kv * steps)
            out[i, block, :] = value[block, k * HEAD_DIM : (k + 1) * HEAD_DIM]
        out[i, rows : rows + 1, :rows] = jnp.sum(jnp.where(eye, top, 0.0), axis=0, keepdims=True)
        out[i, rows + 1 : rows + 2, :rows] = jnp.sum(jnp.where(eye, total, 0.0), axis=0, keepdims=True)


def joined(refs, i, rows, eye):
    tops = [ref[i, rows : rows + 1, :rows] for ref in refs]
    top = functools.reduce(jnp.maximum, tops)
    total, weighted = 0.0, 0.0
    for ref, part_top in zip(refs, tops):
        scale = jnp.exp(part_top - top)
        total = total + ref[i, rows + 1 : rows + 2, :rows] * scale
        column = jnp.sum(jnp.where(eye, scale, 0.0), axis=1, keepdims=True)
        weighted = weighted + ref[i, :rows, :] * column
    return weighted, top, total


def diagonal(rows):
    return lax.broadcasted_iota(jnp.int32, (rows, rows), 0) == lax.broadcasted_iota(
        jnp.int32, (rows, rows), 1
    )


def merge_kernel(a, b, out):
    rows = a.shape[1] - STAT_ROWS
    eye = diagonal(rows)
    for i in range(a.shape[0]):
        weighted, top, total = joined((a, b), i, rows, eye)
        out[i, :rows, :] = weighted
        out[i, rows : rows + 1, :rows] = top
        out[i, rows + 1 : rows + 2, :rows] = total


def finish_kernel(steps, a, b, c, out, wide):
    rows = a.shape[1] - STAT_ROWS
    slots = a.shape[0]
    eye = diagonal(rows)
    for i in range(slots):
        weighted, _, total = joined((a, b, c), i, rows, eye)
        weighted = weighted / jnp.sum(jnp.where(eye, total, 0.0), axis=1, keepdims=True)
        for h in range(rows // steps):
            wide[h, pl.ds(i, steps, stride=slots), :] = weighted[h * steps : (h + 1) * steps, :]
    for h in range(rows // steps):
        out[:, h * HEAD_DIM : (h + 1) * HEAD_DIM] = wide[h].astype(BF16)


def far_kernel(jobs, here, left, held_right, right, held_out, *refs):
    count = len(jobs)
    outs, held, sems = refs[:count], refs[count:-1], refs[-1]
    stream = Stream(here, [right], jobs, held, sems)
    held_out[...] = jnp.dot(left[...], held_right[...], preferred_element_type=F32).astype(BF16)
    stream.multiply(lambda first, count: left[:, first : first + count], outs)


def finish_far_kernel(steps, a, b, c, held_right, attended, held_out, wide):
    finish_kernel(steps, a, b, c, attended, wide)
    held_out[...] = jnp.dot(attended[...], held_right[...], preferred_element_type=F32).astype(BF16)


def attend(position, steps, slots, kvl, here, limits, after, own, other, keys, values, *new):
    heads = 2 * own.shape[2] // HEAD_DIM
    rows, columns = heads * steps, values.shape[2]
    scratch = [
        pltpu.VMEM((heads, steps * slots, HEAD_DIM), F32),
        pltpu.VMEM((slots, rows, columns), F32),
    ]
    if new:
        scratch += [
            pltpu.VMEM((2, kvl, steps * slots, HEAD_DIM), F32),
            pltpu.VMEM((slots, FRESH_ROWS, columns), F32),
            pltpu.VMEM((slots, FRESH_ROWS, columns), F32),
        ]
    return pl.pallas_call(
        functools.partial(attend_kernel, position, steps, slots, kvl),
        out_shape=pltpu.VMEM((slots, rows + STAT_ROWS, HEAD_DIM), F32),
        in_specs=[SMEM] * 2 + [ANYWHERE] + [VMEM] * (4 + len(new)),
        out_specs=VMEM,
        scratch_shapes=scratch,
        compiler_params=params(8),
        cost_estimate=QUICK,
        name="attend",
    )(here, limits, after, *in_vmem(own, other, keys, values, *new))


def merge(a, b):
    return pl.pallas_call(
        merge_kernel,
        out_shape=pltpu.VMEM(a.shape, F32),
        in_specs=[VMEM] * 2,
        out_specs=VMEM,
        compiler_params=params(8),
        cost_estimate=QUICK,
        name="merge",
    )(*in_vmem(a, b))


def per_device(
    step_token_states,
    input_norm_gain,
    wq,
    wkv,
    wo,
    adapter_down,
    adapter_up,
    prompt_cache_pool,
    prompt_slot,
    prompt_cache_length,
    slot_adapter,
    adapter_ranks,
):
    sections = lax.axis_size("section")
    tp_width = lax.axis_size("tp")
    here = jnp.stack([lax.axis_index("section"), lax.axis_index("tp")]).astype(jnp.int32)
    steps, slots, model_width = step_token_states.shape
    requests = prompt_slot.shape[0]
    section_tokens = prompt_cache_pool.shape[2]
    cols_dev = prompt_cache_pool.shape[3]
    adapters, slice_cols, rank = adapter_down.shape
    local_heads = QUERY_HEADS // tp_width
    half_cols = local_heads // 2 * HEAD_DIM
    kvl = max(1, local_heads // PER_KV)
    width = kvl * HEAD_DIM
    rows = steps * slots
    assert sections == 4

    exponents = jnp.arange(HEAD_DIM // 2, dtype=F32) * (2.0 / HEAD_DIM)
    frequency = ROPE_BASE ** (-exponents)
    frequency = jnp.concatenate([frequency, frequency])[None]
    ints = jax.ShapeDtypeStruct((requests,), jnp.int32)
    normed, piece, owners, limits, pick, scale, cosine, sine = pl.pallas_call(
        functools.partial(start_kernel, section_tokens, adapters),
        out_shape=(pltpu.VMEM((rows, model_width), BF16), pltpu.VMEM((rows, slice_cols), BF16), ints, ints)
        + (pltpu.VMEM((requests, rank), F32),) * 2
        + (pltpu.VMEM((sections * rows, HEAD_DIM), F32),) * 2,
        in_specs=[SMEM] + [IN_HBM] * 4 + [VMEM] + [IN_HBM] * 2,
        out_specs=(VMEM, VMEM, SMEM, SMEM) + (VMEM,) * 4,
        scratch_shapes=[
            pltpu.VMEM((rows, model_width), F32),
            pltpu.VMEM((model_width // 128, 128), F32),
            pltpu.VMEM(step_token_states.shape, BF16),
            pltpu.VMEM((model_width // 128, 128), BF16),
            pltpu.SemaphoreType.DMA((6,)),
            *[
                pltpu.SMEM(array.shape, jnp.int32)
                for array in (prompt_slot, prompt_cache_length, slot_adapter, adapter_ranks)
            ],
        ],
        compiler_params=params(8),
        cost_estimate=QUICK,
        name="start",
    )(
        here,
        *[in_hbm(array) for array in (prompt_slot, prompt_cache_length, slot_adapter, adapter_ranks)],
        frequency,
        in_hbm(step_token_states), in_hbm(input_norm_gain.reshape(model_width // 128, 128)),
    )
    normed_beside = swap(normed, "section", 1)
    piece_across = swap(piece, "section", 2)
    piece_beside = swap(piece, "section", 1)
    late_down, late_up, _ = lax.optimization_barrier((adapter_down, adapter_up, normed_beside))
    down_beside = swap(late_down, "section", 1)
    up_beside = swap(late_up, "section", 1)

    packed = tp_width == 4
    chunk = min(512, model_width // 2)
    jobs = [(0, lambda at: (at[0] & 1) * (half_cols // 128), half_cols, chunk)]
    if packed:
        jobs += [(1, lambda at: 0, wkv.shape[1], 2 * chunk)]
    plain_near, *kv_part, held_down = product(
        "query", here, (normed, normed_beside), (wq, wkv), jobs, [F32] * len(jobs), (adapter_down,)
    )
    kv_part = kv_part[0] if packed else jnp.dot(normed, wkv, preferred_element_type=F32)
    plain_far = swap(plain_near, "section", 2)
    late_across = lax.optimization_barrier((piece_across, plain_near))[0]
    piece_beside_across = swap(late_across, "section", 1)
    payload = pltpu.VMEM((sections * rows + kvl * rows, rank), F32)
    own_part = pltpu.VMEM((sections * rows, rank), F32)
    rank_part, *payloads = pl.pallas_call(
        functools.partial(down_kernel, steps, slots),
        out_shape=(own_part,) + ((payload,) * 3 if packed else ()),
        in_specs=[SMEM] + [VMEM] * 8,
        out_specs=(VMEM,) * (4 if packed else 1),
        compiler_params=params(8),
        cost_estimate=QUICK,
        name="down",
    )(
        here,
        *in_vmem(
            piece, piece_beside, piece_across, piece_beside_across, pick, held_down, down_beside, kv_part
        ),
    )
    if packed:
        received = [swap(payloads[bit], "tp", bit + 1) for bit in (2, 1, 0)][::-1]
        parts = [rank_part, *received[::-1]]
        new = (kv_part, *received)
    else:
        parts = [lax.psum(rank_part, "tp")]
        kv_full = lax.all_gather(kv_part[:rows], "tp", axis=1, tiled=True)
        kv_start = here[1] * local_heads // PER_KV * HEAD_DIM
        new = (
            jnp.concatenate(
                [
                    lax.dynamic_slice_in_dim(kv_full, kv_start, width, 1),
                    lax.dynamic_slice_in_dim(kv_full, KVH * HEAD_DIM + kv_start, width, 1),
                ],
                axis=1,
            ),
        )

    cache = prompt_cache_pool
    if cols_dev < HEAD_DIM:
        share = HEAD_DIM // cols_dev
        groups = [list(range(g, g + share)) for g in range(0, tp_width, share)]
        cache = lax.all_gather(cache, "tp", axis=3, tiled=True, axis_index_groups=groups)
    ring = min(8, slots)

    def fetch(places, after, carried, start=None, shape=None):
        count = len(places)
        out = pl.pallas_call(
            functools.partial(fetch_kernel, places, slots, [start] * len(carried)),
            out_shape=(pltpu.VMEM((slots, width, section_tokens), BF16),) * count
            + (pltpu.VMEM((slots, section_tokens, width), BF16),) * count
            + tuple(pltpu.VMEM(shape or c.shape, c.dtype) for c in carried)
            + (pltpu.VMEM((8, 128), F32),),
            in_specs=[SMEM, SMEM, IN_HBM, ANYWHERE] + [IN_HBM] * len(carried),
            out_specs=(VMEM,) * (2 * count + len(carried) + 1),
            scratch_shapes=[
                pltpu.VMEM((ring, section_tokens, width), BF16),
                pltpu.SemaphoreType.DMA((ring,)),
                pltpu.SemaphoreType.DMA((count * slots,)),
                pltpu.SemaphoreType.DMA((1,)),
            ],
            compiler_params=params(12),
            cost_estimate=QUICK,
            name="fetch",
        )(here, owners, in_hbm(cache), after, *[in_hbm(c) for c in carried])
        return dict(zip(places, zip(out[:count], out[count : 2 * count]))), *out[2 * count :]

    caches, held_up, fetch_done = fetch((3, 2, 1), rank_part, (adapter_up,))

    masked = pl.pallas_call(
        functools.partial(query_kernel, steps, slots, len(parts)),
        out_shape=pltpu.VMEM((sections, rows, half_cols), BF16),
        in_specs=[SMEM, ANYWHERE] + [VMEM] * (len(parts) + 8),
        out_specs=VMEM,
        compiler_params=params(8),
        cost_estimate=QUICK,
        name="queries",
    )(here, fetch_done, *in_vmem(*parts, scale, pick, held_up, up_beside, cosine, sine, plain_near, plain_far))
    masked_across = swap(masked, "section", 2)
    quarter = model_width // tp_width
    depth = wo.shape[0]
    columns = [
        functools.partial(lambda bit, at: (at[1] ^ bit) * (quarter // 128), bit)
        for bit in range(tp_width)
    ]
    if packed:
        more, farthest_wo, fetch_done = fetch((0,), masked, (wo,), columns[-1], (depth, quarter))
    else:
        more, fetch_done = fetch((0,), masked, ())
    caches.update(more)

    query_own = pl.pallas_call(
        cross_add_kernel,
        out_shape=pltpu.VMEM(masked.shape, BF16),
        in_specs=[VMEM] * 2 + [ANYWHERE],
        out_specs=VMEM,
        compiler_params=params(8),
        cost_estimate=QUICK,
        name="sum_queries",
    )(*in_vmem(masked, masked_across), fetch_done)
    query_beside = swap(query_own, "section", 1)

    def attend_to(position, after, *new):
        return attend(
            position, steps, slots, kvl, here, limits, after, query_own, query_beside, *caches[position], *new
        )

    part_beside_across = attend_to(3, query_beside)
    part_across = attend_to(2, part_beside_across)
    across = merge(part_across, swap(part_beside_across, "section", 1))
    far = swap(across, "section", 2)
    part_beside = attend_to(1, across)
    part_own = attend_to(0, part_beside, *new, cosine, sine)
    final = in_vmem(part_own, swap(part_beside, "section", 1), far)
    attended_shape = pltpu.VMEM((rows, local_heads * HEAD_DIM), BF16)
    wide_scratch = pltpu.VMEM((local_heads, rows, HEAD_DIM), F32)
    if packed:
        held_wo = pl.pallas_call(
            functools.partial(hold_kernel, columns[-2:-1]),
            out_shape=(pltpu.VMEM((depth, quarter), BF16),),
            in_specs=[SMEM, IN_HBM, ANYWHERE],
            out_specs=(VMEM,),
            scratch_shapes=[pltpu.SemaphoreType.DMA((1,))],
            compiler_params=params(8),
            cost_estimate=QUICK,
            name="hold",
        )(here, in_hbm(wo), part_own)[0]
        block = pltpu.VMEM((rows, quarter), BF16)
        attended, farthest = pl.pallas_call(
            functools.partial(finish_far_kernel, steps),
            out_shape=(attended_shape, block),
            in_specs=[VMEM] * 4,
            out_specs=(VMEM,) * 2,
            scratch_shapes=[wide_scratch],
            compiler_params=params(8),
            cost_estimate=QUICK,
            name="finish",
        )(*final, *in_vmem(farthest_wo))
        farthest = swap(farthest, "tp", tp_width - 1)
        jobs = [(0, columns[1], quarter, depth // CUTS)]
        sent = pl.pallas_call(
            functools.partial(far_kernel, jobs),
            out_shape=(block, block),
            in_specs=[SMEM] + [VMEM] * 2 + [IN_HBM],
            out_specs=(VMEM,) * 2,
            scratch_shapes=stream_scratch([wo], jobs),
            compiler_params=params(16),
            cost_estimate=QUICK,
            name="far_output",
        )(here, *in_vmem(attended, held_wo), in_hbm(wo))
        received = [swap(block, "tp", bit) for block, bit in zip(sent, range(tp_width - 2, 0, -1))]
        jobs = [(0, columns[0], quarter, depth // CUTS)]
        (total,) = product(
            "own_output", here, (attended,), (wo,), jobs, [F32], after=(*sent[:1], farthest)
        )
        total = add(total, farthest, *received)
        blocks = [total] + [swap(total, "tp", bit) for bit in range(1, tp_width)]
        result = pl.pallas_call(
            functools.partial(place_kernel, columns),
            out_shape=jax.ShapeDtypeStruct((rows, model_width), BF16),
            in_specs=[SMEM] + [VMEM] * tp_width,
            out_specs=IN_HBM,
            scratch_shapes=[pltpu.SemaphoreType.DMA((tp_width,))],
            compiler_params=params(8),
            cost_estimate=QUICK,
            name="place",
        )(here, *in_vmem(*blocks))
    else:
        attended = pl.pallas_call(
            functools.partial(finish_kernel, steps),
            out_shape=attended_shape,
            in_specs=[VMEM] * 3,
            out_specs=VMEM,
            scratch_shapes=[wide_scratch],
            compiler_params=params(8),
            cost_estimate=QUICK,
            name="finish",
        )(*final)
        partial_out = jnp.dot(attended, wo, preferred_element_type=F32).astype(BF16)
        result = lax.psum(partial_out, "tp")
    return result.reshape(steps, slots, model_width)


def solution(mesh):
    return jax.shard_map(
        per_device,
        mesh=mesh,
        in_specs=(
            P(None, ("groups", "section"), None),
            P(),
            P(None, "tp"),
            P(None, "tp"),
            P("tp", None),
            P(("groups", "section"), "tp", None),
            P(("groups", "section"), None, "tp"),
            P("groups", None, "section", "tp"),
            P("groups"),
            P("groups"),
            P("groups"),
            P("groups"),
        ),
        out_specs=P(None, ("groups", "section"), None),
        check_vma=False,
    )
```

time: 111 us -> 91.6 us (0.83)
  waiting for transfers between devices: 32.1 us -> 16.9 us
  starting transfers between devices: 25.6 us -> 22 us
  local copies, waits for them, and re-layouts: 1.77 us -> 0 us
    ppermute x23 -> x21, waiting for transfers between devices: 30.1 us -> 16.9 us  [swap(): return jax.tree.map(lambda a: lax.ppermute(a, axis, pairs), value)]
    ppermute x2 -> x0, starting transfers between devices: 4.34 us -> none  [the longest x1 3.68 us: per_device(): second = lax.ppermute(second, 'tp', [(0, 1), (1, 3), (2, 0), (3, 2)])]
    ppermute x2 -> x0, waiting for transfers between devices: 2.05 us -> none  [the longest x1 2.05 us: per_device(): second = lax.ppermute(second, 'tp', [(0, 1), (1, 3), (2, 0), (3, 2)])]
    unnamed x12 -> x0, local copies, waits for them, and re-layouts: 1.77 us -> none
    ppermute x23 -> x21, starting transfers between devices: 21.3 us -> 22 us  [swap(): return jax.tree.map(lambda a: lax.ppermute(a, axis, pairs), value)]
  transfers between devices with their start and end apart: 25 -> 21, of which waited for: 10 -> 10; matrix products, arithmetic and copies ran while one was open for 0% -> 0% of each run, Pallas kernels for 37% -> 46%
where the time goes in v3:
time: 91.6 us; the launch traced here: 91.4 us
  Pallas kernels  52 us (57%)
  starting transfers between devices  22 us (24%)
  waiting for transfers between devices  16.9 us (18%)
    ppermute x21, starting transfers between devices, swap(): return jax.tree.map(lambda a: lax.ppermute(a, axis, pairs), value)  22 us
    ppermute x21, waiting for transfers between devices, swap(): return jax.tree.map(lambda a: lax.ppermute(a, axis, pairs), value)  16.9 us
    pallas_call x2, Pallas kernels, product(): pl.pallas_call(functools.partial(product_kernel, sizes, jobs), out_shape=...  14.6 us
    pallas_call x2, Pallas kernels, fetch(): pl.pallas_call(functools.partial(fetch_kernel, places, slots, [start] * l...  11.7 us
    pallas_call x4, Pallas kernels, attend(): pl.pallas_call(functools.partial(attend_kernel, position, steps, slots, k...  6.97 us
    pallas_call x1, Pallas kernels, per_device(): pl.pallas_call(functools.partial(far_kernel, jobs), out_shape=(block, blo...  5.93 us
    pallas_call x1, Pallas kernels, per_device(): pl.pallas_call(functools.partial(hold_kernel, columns[-2:-1]), out_shape=...  3.94 us
    pallas_call x1, Pallas kernels, per_device(): pl.pallas_call(functools.partial(start_kernel, section_tokens, adapters),...  2.47 us
  transfers between devices with their start and end apart: 21, of which 10 were waited for; matrix products, arithmetic and copies ran while one was open for 0% of the time, Pallas kernels for 46%

profile of v3, /device:TPU:0, one launch (start us, length us, event | category | flops | bytes accessed | tf_op | source)
XLA Modules:
  0.0 91.4 jit_solution(11738136388047596487)
XLA Ops:
  0.2 2.5 %start.1 = (bf16[32,8192]{1,0:T(8,128)(2,1)S(1)}, bf16[32,2048]{1,0:T(8,128)(2,1)S(1)}, s32[32]{0:T(128)S(1)}, s32[32]{0:T(128)S(1)}, f32[32,128]{1,0:T(8,128)S(...) custom-call(s32[2]{0:T(128)S(1)} %pad_add_fusion.here, s32[32]{0:T(128)} %refs_0_.3, ...), custom_call_target="tpu_custom_call" | custom-call | flops 1 | bytes 1 | tf_op jit(solution)/shard_map/start/pallas_call | solution.py:562
  3.2 1.5 %collective-permute-done.2.refs_1_ = bf16[32,8192]{1,0:T(8,128)(2,1)S(1)} collective-permute-done((bf16[32,8192]{1,0:T(8,128)(2,1)S(1)}, bf16[32,8192]{1,0:T(8,128)(2,1)S(1)}, u32[]{:S(2)}, u32[]{:S(2)}) %collective-permute-start.2) | collective-permute-done | bytes 524320 | tf_op jit(solution)/shard_map/ppermute | solution.py:48
  5.2 2.9 %collective-permute-start.1 = (bf16[32,2048]{1,0:T(8,128)(2,1)S(1)}, bf16[32,2048]{1,0:T(8,128)(2,1)S(1)}, u32[]{:S(2)}, u32[]{:S(2)}) collective-permute-start(bf16[32,2048]{1,0:T(8,128)(2,1)S(1)} %get-tuple-element.41.own), channel_id=1, source_target_pairs={{0,8},{4,12},{8,0},{12,4},{1,9},{5,13},{9,1},{13,5},{2,10},{6,14},... | collective-permute-start | bytes 393224 | tf_op jit(solution)/shard_map/ppermute | solution.py:48
  8.1 10.1 %query.1 = (f32[64,1024]{1,0:T(8,128)S(1)}, f32[64,512]{1,0:T(8,128)S(1)}, bf16[4,2048,128]{2,1,0:T(8,128)(2,1)S(1)}) custom-call(s32[2]{0:T(128)S(1)} %pad_add_fusion.here, bf16[32,8192]{1,0:T(8,128)(2,1)S(1)} %get-tuple-element.42.refs_0_, bf16[32,8192]{1,0:T(8,128)(2,1)S(1)} %collective-permute-done.2.refs_1_, bf16[8192,2048]{1,0:T(8,128)(2,1)} %refs_2_.3, ...), custom_call_target="tpu_custom_call" | custom-call | flops 1 | bytes 1 | tf_op jit(solution)/shard_map/query/pallas_call | solution.py:185
  18.8 0.8 collective-permute-done.beside
  19.9 1.8 %down.1 = (f32[128,128]{1,0:T(8,128)S(1)}, f32[192,128]{1,0:T(8,128)S(1)}, f32[192,128]{1,0:T(8,128)S(1)}, f32[192,128]{1,0:T(8,128)S(1)}) custom-call(s32[2]{0:T(128)S(1)} %pad_add_fusion.here, bf16[32,2048]{1,0:T(8,128)(2,1)S(1)} %get-tuple-element.41.own, bf16[32,2048]{1,0:T(8,128)(2,1)S(1)} %collective-permute-done.beside, ...), custom_call_target="tpu_custom_call" | custom-call | flops 1 | bytes 1 | tf_op jit(solution)/shard_map/down/pallas_call | solution.py:610
  21.7 4.1 %collective-permute-start.5 = (f32[192,128]{1,0:T(8,128)S(1)}, f32[192,128]{1,0:T(8,128)S(1)}, u32[]{:S(2)}, u32[]{:S(2)}) collective-permute-start(f32[192,128]{1,0:T(8,128)S(1)} %get-tuple-element.51), channel_id=1, source_target_pairs={{0,3},{1,2},{2,1},{3,0},{4,7},{5,6},{6,5},{7,4},{8,11},{9,10},{10,... | collective-permute-start | bytes 294920 | tf_op jit(solution)/shard_map/ppermute | solution.py:48
  26.5 6.3 %fetch.2 = (bf16[8,256,512]{2,1,0:T(8,128)(2,1)S(1)}, bf16[8,256,512]{2,1,0:T(8,128)(2,1)S(1)}, bf16[8,256,512]{2,1,0:T(8,128)(2,1)S(1)}, bf16[8,512,256]{2,1,0:...) custom-call(s32[2]{0:T(128)S(1)} %pad_add_fusion.here, ...), custom_call_target="tpu_custom_call" | custom-call | flops 1 | bytes 1 | tf_op jit(solution)/shard_map/fetch/pallas_call | solution.py:651
  32.8 1.8 %collective-permute-done.6.refs_2_ = f32[192,128]{1,0:T(8,128)S(1)} collective-permute-done((f32[192,128]{1,0:T(8,128)S(1)}, f32[192,128]{1,0:T(8,128)S(1)}, u32[]{:S(2)}, u32[]{:S(2)}) %collective-permute-start.6) | collective-permute-done | bytes 98336 | tf_op jit(solution)/shard_map/ppermute | solution.py:48
  34.6 1.1 %queries.1.after.own = bf16[4,32,1024]{2,1,0:T(8,128)(2,1)S(1)} custom-call(s32[2]{0:T(128)S(1)} %pad_add_fusion.here, f32[8,128]{1,0:T(8,128)S(1)} %get-tuple-element.50.after, f32[128,128]{1,0:T(8,128)S(1)} %get-tuple-element.49.after.refs_0_, f32[192,128]{1,0:T(8,128)S(1)} %collective-permute-done.5.refs_1_.refs_3_, ...), custom_call_target="tpu_custom_call" | custom-call | flops 1 | bytes 1 | tf_op jit(solution)/shard_map/queries/pallas_call | solution.py:673
  35.7 1.6 %collective-permute-start.10 = (bf16[4,32,1024]{2,1,0:T(8,128)(2,1)S(1)}, bf16[4,32,1024]{2,1,0:T(8,128)(2,1)S(1)}, u32[]{:S(2)}, u32[]{:S(2)}) collective-permute-start(bf16[4,32,1024]{2,1,0:T(8,128)(2,1)S(1)} %queries.1.after.own), channel_id=1, source_target_pairs={{0,8},{4,12},{8,0},{12,4},{1,9},{5,13},{9,1},{13,5},{2,10},{6,14},... | collective-permute-start | bytes 786440 | tf_op jit(solution)/shard_map/ppermute | solution.py:48
  37.3 5.4 %fetch.3 = (bf16[8,256,512]{2,1,0:T(8,128)(2,1)S(1)}, bf16[8,512,256]{2,1,0:T(8,128)(2,1)S(1)}, bf16[2048,2048]{1,0:T(8,128)(2,1)S(1)}, f32[8,128]{1,0:T(8,128)S(1)}) custom-call(s32[2]{0:T(128)S(1)} %pad_add_fusion.here, s32[32]{0:T(128)S(1)} %get-tuple-element.40.owners, bf16[32,2,512,256]{3,2,1,0:T(8,128)(2,1)} %cache.3, ...), custom_call_target="tpu_custom_call" | custom-call | flops 1 | bytes 1 | tf_op jit(solution)/shard_map/fetch/pallas_call | solution.py:651
  42.7 0.9 collective-permute-done.10.across
  43.7 1.5 %collective-permute-done.11.after.other = bf16[4,32,1024]{2,1,0:T(8,128)(2,1)S(1)} collective-permute-done((bf16[4,32,1024]{2,1,0:T(8,128)(2,1)S(1)}, bf16[4,32,1024]{2,1,0:T(8,128)(2,1)S(1)}, u32[]{:S(2)}, u32[]{:S(2)}) %collective-permute-start.11) | collective-permute-done | bytes 262176 | tf_op jit(solution)/shard_map/ppermute | solution.py:48
  45.2 1.6 %attend.4.after = f32[8,72,128]{2,1,0:T(8,128)S(1)} custom-call(s32[2]{0:T(128)S(1)} %pad_add_fusion.here, s32[32]{0:T(128)S(1)} %get-tuple-element.39.limits, bf16[4,32,1024]{2,1,0:T(8,128)(2,1)S(1)} %collective-permute-done.11.after.other, bf16[4,32,1024]{2,1,0:T(8,128)(2,1)S(1)} %sum_queries.1.own, ...), custom_call_target="tpu_custom_call" | custom-call | flops 1 | bytes 1 | tf_op jit(solution)/shard_map/attend/pallas_call | solution.py:505
  47.0 1.6 %attend.5.a = f32[8,72,128]{2,1,0:T(8,128)S(1)} custom-call(s32[2]{0:T(128)S(1)} %pad_add_fusion.here, s32[32]{0:T(128)S(1)} %get-tuple-element.39.limits, f32[8,72,128]{2,1,0:T(8,128)S(1)} %attend.4.after, bf16[4,32,1024]{2,1,0:T(8,128)(2,1)S(1)} %sum_queries.1.own, bf16[4,32,1024]{2,1,0:T(8,128)(2,1)S(1)} %collective-permute-done.11.after.other, ...), custom_call_target="tpu_custom_call" | custom-call | flops 1 | bytes 1 | tf_op jit(solution)/shard_map/attend/pallas_call | solution.py:505
  48.8 1.8 %attend.6.after = f32[8,72,128]{2,1,0:T(8,128)S(1)} custom-call(s32[2]{0:T(128)S(1)} %pad_add_fusion.here, s32[32]{0:T(128)S(1)} %get-tuple-element.39.limits, f32[8,72,128]{2,1,0:T(8,128)S(1)} %merge.1.after, bf16[4,32,1024]{2,1,0:T(8,128)(2,1)S(1)} %sum_queries.1.own, bf16[4,32,1024]{2,1,0:T(8,128)(2,1)S(1)} %collective-permute-done.11.after.other, ...), custom_call_target="tpu_custom_call" | custom-call | flops 1 | bytes 1 | tf_op jit(solution)/shard_map/attend/pallas_call | solution.py:505
  51.0 1.5 %collective-permute-start.14 = (f32[8,72,128]{2,1,0:T(8,128)S(1)}, f32[8,72,128]{2,1,0:T(8,128)S(1)}, u32[]{:S(2)}, u32[]{:S(2)}) collective-permute-start(f32[8,72,128]{2,1,0:T(8,128)S(1)} %merge.1.after), channel_id=1, source_target_pairs={{0,8},{4,12},{8,0},{12,4},{1,9},{5,13},{9,1},{13,5},{2,10},{6,14},... | collective-permute-start | bytes 884744 | tf_op jit(solution)/shard_map/ppermute | solution.py:48
  52.5 2.0 %attend.7.a.after = f32[8,72,128]{2,1,0:T(8,128)S(1)} custom-call(s32[2]{0:T(128)S(1)} %pad_add_fusion.here, s32[32]{0:T(128)S(1)} %get-tuple-element.39.limits, f32[8,72,128]{2,1,0:T(8,128)S(1)} %attend.6.after, bf16[4,32,1024]{2,1,0:T(8,128)(2,1)S(1)} %sum_queries.1.own, bf16[4,32,1024]{2,1,0:T(8,128)(2,1)S(1)} %collective-permute-done.11.after.other, ...), custom_call_target="tpu_custom_call" | custom-call | flops 1 | bytes 1 | tf_op jit(solution)/shard_map/attend/pallas_call | solution.py:505
  54.5 3.9 %hold.1.held_right = bf16[2048,2048]{1,0:T(8,128)(2,1)S(1)} custom-call(s32[2]{0:T(128)S(1)} %pad_add_fusion.here, bf16[2048,8192]{1,0:T(8,128)(2,1)} %refs_1_.3, f32[8,72,128]{2,1,0:T(8,128)S(1)} %attend.7.a.after), custom_call_target="tpu_custom_call" | custom-call | flops 1 | bytes 1 | tf_op jit(solution)/shard_map/hold/pallas_call | solution.py:721
  58.5 1.6 %collective-permute-done.14.c = f32[8,72,128]{2,1,0:T(8,128)S(1)} collective-permute-done((f32[8,72,128]{2,1,0:T(8,128)S(1)}, f32[8,72,128]{2,1,0:T(8,128)S(1)}, u32[]{:S(2)}, u32[]{:S(2)}) %collective-permute-start.14) | collective-permute-done | bytes 294944 | tf_op jit(solution)/shard_map/ppermute | solution.py:48
  60.1 1.7 %finish.1 = (bf16[32,2048]{1,0:T(8,128)(2,1)S(1)}, bf16[32,2048]{1,0:T(8,128)(2,1)S(1)}) custom-call(f32[8,72,128]{2,1,0:T(8,128)S(1)} %attend.7.a.after, f32[8,72,128]{2,1,0:T(8,128)S(1)} %collective-permute-done.13.b, f32[8,72,128]{2,1,0:T(8,128)S(1)} %collective-permute-done.14.c, bf16[2048,2048]{1,0:T(8,128)(2,1)S(1)} %get-tuple-element.68.held_right), custom_call_target="tpu_custom_call" | custom-call | flops 1 | bytes 1 | tf_op jit(solution)/shard_map/finish/pallas_call | solution.py:732
  61.8 2.5 %collective-permute-start.15 = (bf16[32,2048]{1,0:T(8,128)(2,1)S(1)}, bf16[32,2048]{1,0:T(8,128)(2,1)S(1)}, u32[]{:S(2)}, u32[]{:S(2)}) collective-permute-start(bf16[32,2048]{1,0:T(8,128)(2,1)S(1)} %get-tuple-element.71), channel_id=1, source_target_pairs={{0,3},{1,2},{2,1},{3,0},{4,7},{5,6},{6,5},{7,4},{8,11},{9,10},{10,... | collective-permute-start | bytes 393224 | tf_op jit(solution)/shard_map/ppermute | solution.py:48
  64.3 5.9 %far_output.1 = (bf16[32,2048]{1,0:T(8,128)(2,1)S(1)}, bf16[32,2048]{1,0:T(8,128)(2,1)S(1)}) custom-call(s32[2]{0:T(128)S(1)} %pad_add_fusion.here, bf16[32,2048]{1,0:T(8,128)(2,1)S(1)} %get-tuple-element.69.left.refs_0_, bf16[2048,2048]{1,0:T(8,128)(2,1)S(1)} %hold.1.held_right, bf16[2048,8192]{1,0:T(8,128)(2,1)} %refs_1_.3), custom_call_target="tpu_custom_call" | custom-call | flops 1 | bytes 1 | tf_op jit(solution)/shard_map/far_output/pallas_call | solution.py:744
  70.3 1.9 %collective-permute-start.16 = (bf16[32,2048]{1,0:T(8,128)(2,1)S(1)}, bf16[32,2048]{1,0:T(8,128)(2,1)S(1)}, u32[]{:S(2)}, u32[]{:S(2)}) collective-permute-start(bf16[32,2048]{1,0:T(8,128)(2,1)S(1)} %get-tuple-element.70.refs_2_), channel_id=1, source_target_pairs={{0,2},{1,3},{2,0},{3,1},{4,6},{5,7},{6,4},{7,5},{8,10},{9,11},{10,... | collective-permute-start | bytes 393224 | tf_op jit(solution)/shard_map/ppermute | solution.py:48
  72.2 4.5 %own_output.1.refs_0_ = f32[32,2048]{1,0:T(8,128)S(1)} custom-call(s32[2]{0:T(128)S(1)} %pad_add_fusion.here, bf16[32,2048]{1,0:T(8,128)(2,1)S(1)} %get-tuple-element.69.left.refs_0_, bf16[2048,8192]{1,0:T(8,128)(2,1)} %refs_1_.3, bf16[32,2048]{1,0:T(8,128)(2,1)S(1)} %get-tuple-element.70.refs_2_, bf16[32,2048]{1,0:T(8,128)(2,1)S(1)} %collective-permute-done.15.refs_3_.refs_1_), custom_call_target="tpu_custom_call" | custom-call | flops 1 | bytes 1 | tf_op jit(solution)/shard_map/own_output/pallas_call | solution.py:185
  76.8 1.9 %collective-permute-done.16.refs_2_ = bf16[32,2048]{1,0:T(8,128)(2,1)S(1)} collective-permute-done((bf16[32,2048]{1,0:T(8,128)(2,1)S(1)}, bf16[32,2048]{1,0:T(8,128)(2,1)S(1)}, u32[]{:S(2)}, u32[]{:S(2)}) %collective-permute-start.16) | collective-permute-done | bytes 131104 | tf_op jit(solution)/shard_map/ppermute | solution.py:48
  78.7 1.4 %collective-permute-start.20 = (bf16[32,2048]{1,0:T(8,128)(2,1)S(1)}, bf16[32,2048]{1,0:T(8,128)(2,1)S(1)}, u32[]{:S(2)}, u32[]{:S(2)}) collective-permute-start(bf16[32,2048]{1,0:T(8,128)(2,1)S(1)} %add.3.refs_0_), channel_id=1, source_target_pairs={{0,3},{1,2},{2,1},{3,0},{4,7},{5,6},{6,5},{7,4},{8,11},{9,10},{10,... | collective-permute-start | bytes 393224 | tf_op jit(solution)/shard_map/ppermute | solution.py:48
  80.1 3.1 %collective-permute-start.18 = (bf16[32,2048]{1,0:T(8,128)(2,1)S(1)}, bf16[32,2048]{1,0:T(8,128)(2,1)S(1)}, u32[]{:S(2)}, u32[]{:S(2)}) collective-permute-start(bf16[32,2048]{1,0:T(8,128)(2,1)S(1)} %add.3.refs_0_), channel_id=1, source_target_pairs={{0,1},{1,0},{2,3},{3,2},{4,5},{5,4},{6,7},{7,6},{8,9},{9,8},{10,11... | collective-permute-start | bytes 393224 | tf_op jit(solution)/shard_map/ppermute | solution.py:48
  83.2 2.6 %collective-permute-done.20.refs_3_ = bf16[32,2048]{1,0:T(8,128)(2,1)S(1)} collective-permute-done((bf16[32,2048]{1,0:T(8,128)(2,1)S(1)}, bf16[32,2048]{1,0:T(8,128)(2,1)S(1)}, u32[]{:S(2)}, u32[]{:S(2)}) %collective-permute-start.20) | collective-permute-done | bytes 131104 | tf_op jit(solution)/shard_map/ppermute | solution.py:48
  85.7 4.1 %collective-permute-done.19.refs_2_ = bf16[32,2048]{1,0:T(8,128)(2,1)S(1)} collective-permute-done((bf16[32,2048]{1,0:T(8,128)(2,1)S(1)}, bf16[32,2048]{1,0:T(8,128)(2,1)S(1)}, u32[]{:S(2)}, u32[]{:S(2)}) %collective-permute-start.19) | collective-permute-done | bytes 131104 | tf_op jit(solution)/shard_map/ppermute | solution.py:48
  89.9 1.4 %place.1 = bf16[32,8192]{1,0:T(8,128)(2,1)} custom-call(s32[2]{0:T(128)S(1)} %pad_add_fusion.here, bf16[32,2048]{1,0:T(8,128)(2,1)S(1)} %add.3.refs_0_, bf16[32,2048]{1,0:T(8,128)(2,1)S(1)} %collective-permute-done.18.refs_1_, bf16[32,2048]{1,0:T(8,128)(2,1)S(1)} %collective-permute-done.19.refs_2_, bf16[32,2048]{1,0:T(8,128)(2,1)S(1)} %collective-permute-done.20.refs_3_), custom_call_target="tpu_custom_call" | custom-call | flops 1 | bytes 1 | tf_op jit(solution)/shard_map/place/pallas_call | solution.py:761
  (31 shorter events, 3.8 us)
Async XLA Ops:
  2.6 2.1 %collective-permute-start.2 = (bf16[32,8192]{1,0:T(8,128)(2,1)S(1)}, bf16[32,8192]{1,0:T(8,128)(2,1)S(1)}, u32[]{:S(2)}, u32[]{:S(2)}) collective-permute-start(bf16[32,8192]{1,0:T(8,128)(2,1)S(1)} %get-tuple-element.42.refs_0_), channel_id=1, source_target_pairs={{0,4},{4,0},{8,12},{12,8},{1,5},{5,1},{9,13},{13,9},{2,6},{6,2},{1... | collective-permute-start | bytes 1572872 | tf_op jit(solution)/shard_map/ppermute | solution.py:48
  4.7 15.2 %collective-permute-start.4 = (bf16[4,2048,128]{2,1,0:T(8,128)(2,1)}, bf16[4,2048,128]{2,1,0:T(8,128)(2,1)S(1)}, u32[]{:S(2)}, u32[]{:S(2)}) collective-permute-start(bf16[4,2048,128]{2,1,0:T(8,128)(2,1)} %refs_4_.1), channel_id=1, source_target_pairs={{0,4},{4,0},{8,12},{12,8},{1,5},{5,1},{9,13},{13,9},{2,6},{6,2},{1... | collective-permute-start | bytes 6291464 | tf_op jit(solution)/shard_map/ppermute | solution.py:48
  5.1 27.7 %collective-permute-start.8 = (bf16[4,128,2048]{2,1,0:T(8,128)(2,1)}, bf16[4,128,2048]{2,1,0:T(8,128)(2,1)S(1)}, u32[]{:S(2)}, u32[]{:S(2)}) collective-permute-start(bf16[4,128,2048]{2,1,0:T(8,128)(2,1)} %refs_0_.4), channel_id=1, source_target_pairs={{0,4},{4,0},{8,12},{12,8},{1,5},{5,1},{9,13},{13,9},{2,6},{6,2},{1... | collective-permute-start | bytes 6291464 | tf_op jit(solution)/shard_map/ppermute | solution.py:48
  5.2 13.1 %collective-permute-start.1 = (bf16[32,2048]{1,0:T(8,128)(2,1)S(1)}, bf16[32,2048]{1,0:T(8,128)(2,1)S(1)}, u32[]{:S(2)}, u32[]{:S(2)}) collective-permute-start(bf16[32,2048]{1,0:T(8,128)(2,1)S(1)} %get-tuple-element.41.own), channel_id=1, source_target_pairs={{0,8},{4,12},{8,0},{12,4},{1,9},{5,13},{9,1},{13,5},{2,10},{6,14},... | collective-permute-start | bytes 393224 | tf_op jit(solution)/shard_map/ppermute | solution.py:48
  18.2 14.6 %collective-permute-start.9 = (f32[64,1024]{1,0:T(8,128)S(1)}, f32[64,1024]{1,0:T(8,128)S(1)}, u32[]{:S(2)}, u32[]{:S(2)}) collective-permute-start(f32[64,1024]{1,0:T(8,128)S(1)} %get-tuple-element.43.refs_10_), channel_id=1, source_target_pairs={{0,8},{4,12},{8,0},{12,4},{1,9},{5,13},{9,1},{13,5},{2,10},{6,14},... | collective-permute-start | bytes 786440 | tf_op jit(solution)/shard_map/ppermute | solution.py:48
  18.3 1.4 %collective-permute-start = (bf16[32,2048]{1,0:T(8,128)(2,1)S(1)}, bf16[32,2048]{1,0:T(8,128)(2,1)S(1)}, u32[]{:S(2)}, u32[]{:S(2)}) collective-permute-start(bf16[32,2048]{1,0:T(8,128)(2,1)S(1)} %get-tuple-element.41.own), channel_id=1, source_target_pairs={{0,4},{4,0},{8,12},{12,8},{1,5},{5,1},{9,13},{13,9},{2,6},{6,2},{1... | collective-permute-start | bytes 393224 | tf_op jit(solution)/shard_map/ppermute | solution.py:48
  18.3 1.5 %collective-permute-start.3 = (bf16[32,2048]{1,0:T(8,128)(2,1)S(1)}, bf16[32,2048]{1,0:T(8,128)(2,1)S(1)}, u32[]{:S(2)}, u32[]{:S(2)}) collective-permute-start(bf16[32,2048]{1,0:T(8,128)(2,1)S(1)} %collective-permute-done.1.across), channel_id=1, source_target_pairs={{0,4},{4,0},{8,12},{12,8},{1,5},{5,1},{9,13},{13,9},{2,6},{6,2},{1... | collective-permute-start | bytes 393224 | tf_op jit(solution)/shard_map/ppermute | solution.py:48
  21.7 11.1 %collective-permute-start.5 = (f32[192,128]{1,0:T(8,128)S(1)}, f32[192,128]{1,0:T(8,128)S(1)}, u32[]{:S(2)}, u32[]{:S(2)}) collective-permute-start(f32[192,128]{1,0:T(8,128)S(1)} %get-tuple-element.51), channel_id=1, source_target_pairs={{0,3},{1,2},{2,1},{3,0},{4,7},{5,6},{6,5},{7,4},{8,11},{9,10},{10,... | collective-permute-start | bytes 294920 | tf_op jit(solution)/shard_map/ppermute | solution.py:48
  25.8 8.8 %collective-permute-start.6 = (f32[192,128]{1,0:T(8,128)S(1)}, f32[192,128]{1,0:T(8,128)S(1)}, u32[]{:S(2)}, u32[]{:S(2)}) collective-permute-start(f32[192,128]{1,0:T(8,128)S(1)} %get-tuple-element.52), channel_id=1, source_target_pairs={{0,2},{1,3},{2,0},{3,1},{4,6},{5,7},{6,4},{7,5},{8,10},{9,11},{10,... | collective-permute-start | bytes 294920 | tf_op jit(solution)/shard_map/ppermute | solution.py:48
  25.8 8.8 %collective-permute-start.7 = (f32[192,128]{1,0:T(8,128)S(1)}, f32[192,128]{1,0:T(8,128)S(1)}, u32[]{:S(2)}, u32[]{:S(2)}) collective-permute-start(f32[192,128]{1,0:T(8,128)S(1)} %get-tuple-element.53), channel_id=1, source_target_pairs={{0,1},{1,0},{2,3},{3,2},{4,5},{5,4},{6,7},{7,6},{8,9},{9,8},{10,11... | collective-permute-start | bytes 294920 | tf_op jit(solution)/shard_map/ppermute | solution.py:48
  35.7 7.8 %collective-permute-start.10 = (bf16[4,32,1024]{2,1,0:T(8,128)(2,1)S(1)}, bf16[4,32,1024]{2,1,0:T(8,128)(2,1)S(1)}, u32[]{:S(2)}, u32[]{:S(2)}) collective-permute-start(bf16[4,32,1024]{2,1,0:T(8,128)(2,1)S(1)} %queries.1.after.own), channel_id=1, source_target_pairs={{0,8},{4,12},{8,0},{12,4},{1,9},{5,13},{9,1},{13,5},{2,10},{6,14},... | collective-permute-start | bytes 786440 | tf_op jit(solution)/shard_map/ppermute | solution.py:48
  43.6 1.6 %collective-permute-start.11 = (bf16[4,32,1024]{2,1,0:T(8,128)(2,1)S(1)}, bf16[4,32,1024]{2,1,0:T(8,128)(2,1)S(1)}, u32[]{:S(2)}, u32[]{:S(2)}) collective-permute-start(bf16[4,32,1024]{2,1,0:T(8,128)(2,1)S(1)} %sum_queries.1.own), channel_id=1, source_target_pairs={{0,4},{4,0},{8,12},{12,8},{1,5},{5,1},{9,13},{13,9},{2,6},{6,2},{1... | collective-permute-start | bytes 786440 | tf_op jit(solution)/shard_map/ppermute | solution.py:48
  46.8 1.8 %collective-permute-start.12 = (f32[8,72,128]{2,1,0:T(8,128)S(1)}, f32[8,72,128]{2,1,0:T(8,128)S(1)}, u32[]{:S(2)}, u32[]{:S(2)}) collective-permute-start(f32[8,72,128]{2,1,0:T(8,128)S(1)} %attend.4.after), channel_id=1, source_target_pairs={{0,4},{4,0},{8,12},{12,8},{1,5},{5,1},{9,13},{13,9},{2,6},{6,2},{1... | collective-permute-start | bytes 884744 | tf_op jit(solution)/shard_map/ppermute | solution.py:48
  50.6 7.9 %collective-permute-start.13 = (f32[8,72,128]{2,1,0:T(8,128)S(1)}, f32[8,72,128]{2,1,0:T(8,128)S(1)}, u32[]{:S(2)}, u32[]{:S(2)}) collective-permute-start(f32[8,72,128]{2,1,0:T(8,128)S(1)} %attend.6.after), channel_id=1, source_target_pairs={{0,4},{4,0},{8,12},{12,8},{1,5},{5,1},{9,13},{13,9},{2,6},{6,2},{1... | collective-permute-start | bytes 884744 | tf_op jit(solution)/shard_map/ppermute | solution.py:48
  51.0 9.0 %collective-permute-start.14 = (f32[8,72,128]{2,1,0:T(8,128)S(1)}, f32[8,72,128]{2,1,0:T(8,128)S(1)}, u32[]{:S(2)}, u32[]{:S(2)}) collective-permute-start(f32[8,72,128]{2,1,0:T(8,128)S(1)} %merge.1.after), channel_id=1, source_target_pairs={{0,8},{4,12},{8,0},{12,4},{1,9},{5,13},{9,1},{13,5},{2,10},{6,14},... | collective-permute-start | bytes 884744 | tf_op jit(solution)/shard_map/ppermute | solution.py:48
  61.8 10.4 %collective-permute-start.15 = (bf16[32,2048]{1,0:T(8,128)(2,1)S(1)}, bf16[32,2048]{1,0:T(8,128)(2,1)S(1)}, u32[]{:S(2)}, u32[]{:S(2)}) collective-permute-start(bf16[32,2048]{1,0:T(8,128)(2,1)S(1)} %get-tuple-element.71), channel_id=1, source_target_pairs={{0,3},{1,2},{2,1},{3,0},{4,7},{5,6},{6,5},{7,4},{8,11},{9,10},{10,... | collective-permute-start | bytes 393224 | tf_op jit(solution)/shard_map/ppermute | solution.py:48
  70.3 6.5 %collective-permute-start.17 = (bf16[32,2048]{1,0:T(8,128)(2,1)S(1)}, bf16[32,2048]{1,0:T(8,128)(2,1)S(1)}, u32[]{:S(2)}, u32[]{:S(2)}) collective-permute-start(bf16[32,2048]{1,0:T(8,128)(2,1)S(1)} %get-tuple-element.72), channel_id=1, source_target_pairs={{0,1},{1,0},{2,3},{3,2},{4,5},{5,4},{6,7},{7,6},{8,9},{9,8},{10,11... | collective-permute-start | bytes 393224 | tf_op jit(solution)/shard_map/ppermute | solution.py:48
  70.3 8.3 %collective-permute-start.16 = (bf16[32,2048]{1,0:T(8,128)(2,1)S(1)}, bf16[32,2048]{1,0:T(8,128)(2,1)S(1)}, u32[]{:S(2)}, u32[]{:S(2)}) collective-permute-start(bf16[32,2048]{1,0:T(8,128)(2,1)S(1)} %get-tuple-element.70.refs_2_), channel_id=1, source_target_pairs={{0,2},{1,3},{2,0},{3,1},{4,6},{5,7},{6,4},{7,5},{8,10},{9,11},{10,... | collective-permute-start | bytes 393224 | tf_op jit(solution)/shard_map/ppermute | solution.py:48
  78.7 7.0 %collective-permute-start.20 = (bf16[32,2048]{1,0:T(8,128)(2,1)S(1)}, bf16[32,2048]{1,0:T(8,128)(2,1)S(1)}, u32[]{:S(2)}, u32[]{:S(2)}) collective-permute-start(bf16[32,2048]{1,0:T(8,128)(2,1)S(1)} %add.3.refs_0_), channel_id=1, source_target_pairs={{0,3},{1,2},{2,1},{3,0},{4,7},{5,6},{6,5},{7,4},{8,11},{9,10},{10,... | collective-permute-start | bytes 393224 | tf_op jit(solution)/shard_map/ppermute | solution.py:48
  80.1 9.8 %collective-permute-start.19 = (bf16[32,2048]{1,0:T(8,128)(2,1)S(1)}, bf16[32,2048]{1,0:T(8,128)(2,1)S(1)}, u32[]{:S(2)}, u32[]{:S(2)}) collective-permute-start(bf16[32,2048]{1,0:T(8,128)(2,1)S(1)} %add.3.refs_0_), channel_id=1, source_target_pairs={{0,2},{1,3},{2,0},{3,1},{4,6},{5,7},{6,4},{7,5},{8,10},{9,11},{10,... | collective-permute-start | bytes 393224 | tf_op jit(solution)/shard_map/ppermute | solution.py:48
  80.1 9.8 %collective-permute-start.18 = (bf16[32,2048]{1,0:T(8,128)(2,1)S(1)}, bf16[32,2048]{1,0:T(8,128)(2,1)S(1)}, u32[]{:S(2)}, u32[]{:S(2)}) collective-permute-start(bf16[32,2048]{1,0:T(8,128)(2,1)S(1)} %add.3.refs_0_), channel_id=1, source_target_pairs={{0,1},{1,0},{2,3},{3,2},{4,5},{5,4},{6,7},{7,6},{8,9},{9,8},{10,11... | collective-permute-start | bytes 393224 | tf_op jit(solution)/shard_map/ppermute | solution.py:48

commit v4 on v3

--- a/solution.py
+++ b/solution.py
@@ -208,10 +208,10 @@
     out[...] = total.astype(out.dtype)
 
 
-def add(*terms):
+def add(*terms, dtype=BF16):
     return pl.pallas_call(
         add_kernel,
-        out_shape=pltpu.VMEM(terms[0].shape, BF16),
+        out_shape=pltpu.VMEM(terms[0].shape, dtype),
         in_specs=[VMEM] * len(terms),
         out_specs=VMEM,
         compiler_params=params(8),
@@ -330,26 +330,27 @@
         value_copy(n).wait()
 
 
-def hold_kernel(starts, here, source, after, *refs):
-    *outs, sems = refs
-    cols = outs[0].shape[1]
+def attend_and_hold_kernel(starts, operands, attend_body, here, limits, after, right, *refs):
+    inputs, (out, *refs) = refs[:operands], refs[operands:]
+    held, (*scratch, sems) = refs[: len(starts)], refs[len(starts) :]
     copies = []
-    for i, out in enumerate(outs):
-        first = pl.multiple_of(starts[i](here) * 128, 128)
-        copies.append(pltpu.make_async_copy(source.at[:, pl.ds(first, cols)], out, sems.at[i]))
+    for i, (start, target) in enumerate(zip(starts, held)):
+        first = pl.multiple_of(start(here) * 128, 128)
+        source = right.at[:, pl.ds(first, target.shape[1])]
+        copies.append(pltpu.make_async_copy(source, target, sems.at[i]))
     for copy in copies:
         copy.start()
+    attend_body(here, limits, after, *inputs, out, *scratch)
     for copy in copies:
         copy.wait()
 
 
 def place_kernel(starts, here, *refs):
-    *blocks, out, sems = refs
+    blocks, (out, sems) = refs[: len(starts)], refs[-2:]
     copies = []
-    for i, block in enumerate(blocks):
-        cols = block.shape[1]
-        first = pl.multiple_of(starts[i](here) * 128, 128)
-        copies.append(pltpu.make_async_copy(block, out.at[:, pl.ds(first, cols)], sems.at[i]))
+    for i, (start, block) in enumerate(zip(starts, blocks)):
+        first = pl.multiple_of(start(here) * 128, 128)
+        copies.append(pltpu.make_async_copy(block, out.at[:, pl.ds(first, block.shape[1])], sems.at[i]))
     for copy in copies:
         copy.start()
     for copy in copies:
@@ -476,12 +477,10 @@
         out[:, h * HEAD_DIM : (h + 1) * HEAD_DIM] = wide[h].astype(BF16)
 
 
-def far_kernel(jobs, here, left, held_right, right, held_out, *refs):
-    count = len(jobs)
-    outs, held, sems = refs[:count], refs[count:-1], refs[-1]
-    stream = Stream(here, [right], jobs, held, sems)
-    held_out[...] = jnp.dot(left[...], held_right[...], preferred_element_type=F32).astype(BF16)
-    stream.multiply(lambda first, count: left[:, first : first + count], outs)
+def far_kernel(left, *refs):
+    half = len(refs) // 2
+    for right, out in zip(refs[:half], refs[half:]):
+        out[...] = jnp.dot(left[...], right[...], preferred_element_type=F32).astype(out.dtype)
 
 
 def finish_far_kernel(steps, a, b, c, held_right, attended, held_out, wide):
@@ -489,29 +488,43 @@
     held_out[...] = jnp.dot(attended[...], held_right[...], preferred_element_type=F32).astype(BF16)
 
 
-def attend(position, steps, slots, kvl, here, limits, after, own, other, keys, values, *new):
-    heads = 2 * own.shape[2] // HEAD_DIM
-    rows, columns = heads * steps, values.shape[2]
+def attend(position, steps, slots, kvl, here, limits, after, operands, right=None, starts=(), cols=0):
+    heads = 2 * operands[0].shape[2] // HEAD_DIM
+    rows, columns = heads * steps, operands[3].shape[2]
     scratch = [
         pltpu.VMEM((heads, steps * slots, HEAD_DIM), F32),
         pltpu.VMEM((slots, rows, columns), F32),
     ]
-    if new:
+    if position == 0:
         scratch += [
             pltpu.VMEM((2, kvl, steps * slots, HEAD_DIM), F32),
             pltpu.VMEM((slots, FRESH_ROWS, columns), F32),
             pltpu.VMEM((slots, FRESH_ROWS, columns), F32),
         ]
+    body = functools.partial(attend_kernel, position, steps, slots, kvl)
+    out = pltpu.VMEM((slots, rows + STAT_ROWS, HEAD_DIM), F32)
+    if not starts:
+        return pl.pallas_call(
+            body,
+            out_shape=out,
+            in_specs=[SMEM] * 2 + [ANYWHERE] + [VMEM] * len(operands),
+            out_specs=VMEM,
+            scratch_shapes=scratch,
+            compiler_params=params(8),
+            cost_estimate=QUICK,
+            name="attend",
+        )(here, limits, after, *in_vmem(*operands))
+    block = pltpu.VMEM((right.shape[0], cols), right.dtype)
     return pl.pallas_call(
-        functools.partial(attend_kernel, position, steps, slots, kvl),
-        out_shape=pltpu.VMEM((slots, rows + STAT_ROWS, HEAD_DIM), F32),
-        in_specs=[SMEM] * 2 + [ANYWHERE] + [VMEM] * (4 + len(new)),
-        out_specs=VMEM,
-        scratch_shapes=scratch,
+        functools.partial(attend_and_hold_kernel, starts, len(operands), body),
+        out_shape=(out,) + (block,) * len(starts),
+        in_specs=[SMEM] * 2 + [ANYWHERE, IN_HBM] + [VMEM] * len(operands),
+        out_specs=(VMEM,) * (1 + len(starts)),
+        scratch_shapes=scratch + [pltpu.SemaphoreType.DMA((len(starts),))],
         compiler_params=params(8),
         cost_estimate=QUICK,
-        name="attend",
-    )(here, limits, after, *in_vmem(own, other, keys, values, *new))
+        name="attend_hold",
+    )(here, limits, after, in_hbm(right), *in_vmem(*operands))
 
 
 def merge(a, b):
@@ -703,31 +716,23 @@
     )(*in_vmem(masked, masked_across), fetch_done)
     query_beside = swap(query_own, "section", 1)
 
-    def attend_to(position, after, *new):
-        return attend(
-            position, steps, slots, kvl, here, limits, after, query_own, query_beside, *caches[position], *new
-        )
+    def attend_to(position, after, *new, **hold):
+        operands = (query_own, query_beside, *caches[position], *new)
+        return attend(position, steps, slots, kvl, here, limits, after, operands, **hold)
 
     part_beside_across = attend_to(3, query_beside)
-    part_across = attend_to(2, part_beside_across)
+    part_beside = attend_to(1, part_beside_across)
+    part_across = attend_to(2, part_beside)
     across = merge(part_across, swap(part_beside_across, "section", 1))
     far = swap(across, "section", 2)
-    part_beside = attend_to(1, across)
-    part_own = attend_to(0, part_beside, *new, cosine, sine)
+    hold = dict(right=wo, starts=columns[1:-1], cols=quarter) if packed else {}
+    part_own = attend_to(0, across, *new, cosine, sine, **hold)
+    if packed:
+        part_own, *held_wo = part_own
     final = in_vmem(part_own, swap(part_beside, "section", 1), far)
     attended_shape = pltpu.VMEM((rows, local_heads * HEAD_DIM), BF16)
     wide_scratch = pltpu.VMEM((local_heads, rows, HEAD_DIM), F32)
     if packed:
-        held_wo = pl.pallas_call(
-            functools.partial(hold_kernel, columns[-2:-1]),
-            out_shape=(pltpu.VMEM((depth, quarter), BF16),),
-            in_specs=[SMEM, IN_HBM, ANYWHERE],
-            out_specs=(VMEM,),
-            scratch_shapes=[pltpu.SemaphoreType.DMA((1,))],
-            compiler_params=params(8),
-            cost_estimate=QUICK,
-            name="hold",
-        )(here, in_hbm(wo), part_own)[0]
         block = pltpu.VMEM((rows, quarter), BF16)
         attended, farthest = pl.pallas_call(
             functools.partial(finish_far_kernel, steps),
@@ -740,34 +745,38 @@
             name="finish",
         )(*final, *in_vmem(farthest_wo))
         farthest = swap(farthest, "tp", tp_width - 1)
-        jobs = [(0, columns[1], quarter, depth // CUTS)]
+        held_wo = held_wo[::-1]
         sent = pl.pallas_call(
-            functools.partial(far_kernel, jobs),
-            out_shape=(block, block),
-            in_specs=[SMEM] + [VMEM] * 2 + [IN_HBM],
-            out_specs=(VMEM,) * 2,
-            scratch_shapes=stream_scratch([wo], jobs),
-            compiler_params=params(16),
+            far_kernel,
+            out_shape=(block,) * len(held_wo),
+            in_specs=[VMEM] * (1 + len(held_wo)),
+            out_specs=(VMEM,) * len(held_wo),
+            compiler_params=params(8),
             cost_estimate=QUICK,
             name="far_output",
-        )(here, *in_vmem(attended, held_wo), in_hbm(wo))
+        )(*in_vmem(attended, *held_wo))
         received = [swap(block, "tp", bit) for block, bit in zip(sent, range(tp_width - 2, 0, -1))]
         jobs = [(0, columns[0], quarter, depth // CUTS)]
         (total,) = product(
-            "own_output", here, (attended,), (wo,), jobs, [F32], after=(*sent[:1], farthest)
+            "own_output", here, (attended,), (wo,), jobs, [F32], after=sent[:1]
         )
-        total = add(total, farthest, *received)
+        total = add(add(total, farthest, dtype=F32), *received)
         blocks = [total] + [swap(total, "tp", bit) for bit in range(1, tp_width)]
-        result = pl.pallas_call(
-            functools.partial(place_kernel, columns),
-            out_shape=jax.ShapeDtypeStruct((rows, model_width), BF16),
-            in_specs=[SMEM] + [VMEM] * tp_width,
-            out_specs=IN_HBM,
-            scratch_shapes=[pltpu.SemaphoreType.DMA((tp_width,))],
-            compiler_params=params(8),
-            cost_estimate=QUICK,
-            name="place",
-        )(here, *in_vmem(*blocks))
+
+        def place(bits, *earlier):
+            return pl.pallas_call(
+                functools.partial(place_kernel, [columns[bit] for bit in bits]),
+                out_shape=jax.ShapeDtypeStruct((rows, model_width), BF16),
+                in_specs=[SMEM] + [VMEM] * len(bits) + [IN_HBM] * len(earlier),
+                out_specs=IN_HBM,
+                scratch_shapes=[pltpu.SemaphoreType.DMA((len(bits),))],
+                input_output_aliases={1 + len(bits): 0} if earlier else {},
+                compiler_params=params(8),
+                cost_estimate=QUICK,
+                name="place",
+            )(here, *in_vmem(*[blocks[bit] for bit in bits]), *earlier)
+
+        result = place((2, 1), place((0, 3)))
     else:
         attended = pl.pallas_call(
             functools.partial(finish_kernel, steps),

time: 91.6 us -> 89.6 us (0.978)
  waiting for transfers between devices: 16.9 us -> 15.5 us
    ppermute x21, waiting for transfers between devices: 16.9 us -> 15.5 us  [swap(): return jax.tree.map(lambda a: lax.ppermute(a, axis, pairs), value)]
    pallas_call x8 -> x9, Pallas kernels: 18.3 us -> 17.6 us  [the longest x1 7.2 us: attend(): pl.pallas_call(functools.partial(attend_and_hold_kernel, starts, len(oper...]
  transfers between devices with their start and end apart: 21 -> 21, of which waited for: 10 -> 10; matrix products, arithmetic and copies ran while one was open for 0% -> 0% of each run, Pallas kernels for 46% -> 48%
where the time goes in v4:
time: 89.6 us; the launch traced here: 89.4 us
  Pallas kernels  51.4 us (57%)
  starting transfers between devices  22 us (25%)
  waiting for transfers between devices  15.5 us (17%)
    ppermute x21, starting transfers between devices, swap(): return jax.tree.map(lambda a: lax.ppermute(a, axis, pairs), value)  22 us
    ppermute x21, waiting for transfers between devices, swap(): return jax.tree.map(lambda a: lax.ppermute(a, axis, pairs), value)  15.5 us
    pallas_call x2, Pallas kernels, product(): pl.pallas_call(functools.partial(product_kernel, sizes, jobs), out_shape=...  14.6 us
    pallas_call x2, Pallas kernels, fetch(): pl.pallas_call(functools.partial(fetch_kernel, places, slots, [start] * l...  11.7 us
    pallas_call x1, Pallas kernels, attend(): pl.pallas_call(functools.partial(attend_and_hold_kernel, starts, len(oper...  7.2 us
    pallas_call x3, Pallas kernels, attend(): pl.pallas_call(body, out_shape=out, in_specs=[SMEM] * 2 + [ANYWHERE] + [V...  4.88 us
    pallas_call x1, Pallas kernels, per_device(): pl.pallas_call(far_kernel, out_shape=(block,) * len(held_wo), in_specs=[V...  2.97 us
    pallas_call x2, Pallas kernels, place(): pl.pallas_call(functools.partial(place_kernel, [columns[bit] for bit in b...  2.52 us
  transfers between devices with their start and end apart: 21, of which 10 were waited for; matrix products, arithmetic and copies ran while one was open for 0% of the time, Pallas kernels for 48%

profile of v4, /device:TPU:0, one launch (start us, length us, event | category | flops | bytes accessed | tf_op | source)
XLA Modules:
  0.0 89.4 jit_solution(752544559192068538)
XLA Ops:
  0.2 2.5 %start.1 = (bf16[32,8192]{1,0:T(8,128)(2,1)S(1)}, bf16[32,2048]{1,0:T(8,128)(2,1)S(1)}, s32[32]{0:T(128)S(1)}, s32[32]{0:T(128)S(1)}, f32[32,128]{1,0:T(8,128)S(...) custom-call(s32[2]{0:T(128)S(1)} %pad_add_fusion.here, s32[32]{0:T(128)} %refs_0_.3, ...), custom_call_target="tpu_custom_call" | custom-call | flops 1 | bytes 1 | tf_op jit(solution)/shard_map/start/pallas_call | solution.py:575
  3.2 1.5 %collective-permute-done.2.refs_1_ = bf16[32,8192]{1,0:T(8,128)(2,1)S(1)} collective-permute-done((bf16[32,8192]{1,0:T(8,128)(2,1)S(1)}, bf16[32,8192]{1,0:T(8,128)(2,1)S(1)}, u32[]{:S(2)}, u32[]{:S(2)}) %collective-permute-start.2) | collective-permute-done | bytes 524320 | tf_op jit(solution)/shard_map/ppermute | solution.py:48
  5.2 2.9 %collective-permute-start.1 = (bf16[32,2048]{1,0:T(8,128)(2,1)S(1)}, bf16[32,2048]{1,0:T(8,128)(2,1)S(1)}, u32[]{:S(2)}, u32[]{:S(2)}) collective-permute-start(bf16[32,2048]{1,0:T(8,128)(2,1)S(1)} %get-tuple-element.44.own), channel_id=1, source_target_pairs={{0,8},{4,12},{8,0},{12,4},{1,9},{5,13},{9,1},{13,5},{2,10},{6,14},... | collective-permute-start | bytes 393224 | tf_op jit(solution)/shard_map/ppermute | solution.py:48
  8.1 10.1 %query.1 = (f32[64,1024]{1,0:T(8,128)S(1)}, f32[64,512]{1,0:T(8,128)S(1)}, bf16[4,2048,128]{2,1,0:T(8,128)(2,1)S(1)}) custom-call(s32[2]{0:T(128)S(1)} %pad_add_fusion.here, bf16[32,8192]{1,0:T(8,128)(2,1)S(1)} %get-tuple-element.45.refs_0_, bf16[32,8192]{1,0:T(8,128)(2,1)S(1)} %collective-permute-done.2.refs_1_, bf16[8192,2048]{1,0:T(8,128)(2,1)} %refs_2_.3, ...), custom_call_target="tpu_custom_call" | custom-call | flops 1 | bytes 1 | tf_op jit(solution)/shard_map/query/pallas_call | solution.py:185
  18.8 0.8 collective-permute-done.beside
  19.9 1.8 %down.1 = (f32[128,128]{1,0:T(8,128)S(1)}, f32[192,128]{1,0:T(8,128)S(1)}, f32[192,128]{1,0:T(8,128)S(1)}, f32[192,128]{1,0:T(8,128)S(1)}) custom-call(s32[2]{0:T(128)S(1)} %pad_add_fusion.here, bf16[32,2048]{1,0:T(8,128)(2,1)S(1)} %get-tuple-element.44.own, bf16[32,2048]{1,0:T(8,128)(2,1)S(1)} %collective-permute-done.beside, ...), custom_call_target="tpu_custom_call" | custom-call | flops 1 | bytes 1 | tf_op jit(solution)/shard_map/down/pallas_call | solution.py:623
  21.7 4.1 %collective-permute-start.5 = (f32[192,128]{1,0:T(8,128)S(1)}, f32[192,128]{1,0:T(8,128)S(1)}, u32[]{:S(2)}, u32[]{:S(2)}) collective-permute-start(f32[192,128]{1,0:T(8,128)S(1)} %get-tuple-element.54), channel_id=1, source_target_pairs={{0,3},{1,2},{2,1},{3,0},{4,7},{5,6},{6,5},{7,4},{8,11},{9,10},{10,... | collective-permute-start | bytes 294920 | tf_op jit(solution)/shard_map/ppermute | solution.py:48
  25.8 0.6 collective-permute-start.7
  26.5 6.3 %fetch.2 = (bf16[8,256,512]{2,1,0:T(8,128)(2,1)S(1)}, bf16[8,256,512]{2,1,0:T(8,128)(2,1)S(1)}, bf16[8,256,512]{2,1,0:T(8,128)(2,1)S(1)}, bf16[8,512,256]{2,1,0:...) custom-call(s32[2]{0:T(128)S(1)} %pad_add_fusion.here, ...), custom_call_target="tpu_custom_call" | custom-call | flops 1 | bytes 1 | tf_op jit(solution)/shard_map/fetch/pallas_call | solution.py:664
  32.8 1.8 %collective-permute-done.6.refs_2_.refs_6_ = f32[192,128]{1,0:T(8,128)S(1)} collective-permute-done((f32[192,128]{1,0:T(8,128)S(1)}, f32[192,128]{1,0:T(8,128)S(1)}, u32[]{:S(2)}, u32[]{:S(2)}) %collective-permute-start.6) | collective-permute-done | bytes 98336 | tf_op jit(solution)/shard_map/ppermute | solution.py:48
  34.6 1.1 %queries.1.after.own = bf16[4,32,1024]{2,1,0:T(8,128)(2,1)S(1)} custom-call(s32[2]{0:T(128)S(1)} %pad_add_fusion.here, f32[8,128]{1,0:T(8,128)S(1)} %get-tuple-element.53.after, f32[128,128]{1,0:T(8,128)S(1)} %get-tuple-element.52.after.refs_0_, f32[192,128]{1,0:T(8,128)S(1)} %collective-permute-done.5.refs_1_.refs_7_, ...), custom_call_target="tpu_custom_call" | custom-call | flops 1 | bytes 1 | tf_op jit(solution)/shard_map/queries/pallas_call | solution.py:686
  35.7 1.6 %collective-permute-start.10 = (bf16[4,32,1024]{2,1,0:T(8,128)(2,1)S(1)}, bf16[4,32,1024]{2,1,0:T(8,128)(2,1)S(1)}, u32[]{:S(2)}, u32[]{:S(2)}) collective-permute-start(bf16[4,32,1024]{2,1,0:T(8,128)(2,1)S(1)} %queries.1.after.own), channel_id=1, source_target_pairs={{0,8},{4,12},{8,0},{12,4},{1,9},{5,13},{9,1},{13,5},{2,10},{6,14},... | collective-permute-start | bytes 786440 | tf_op jit(solution)/shard_map/ppermute | solution.py:48
  37.3 5.4 %fetch.3 = (bf16[8,256,512]{2,1,0:T(8,128)(2,1)S(1)}, bf16[8,512,256]{2,1,0:T(8,128)(2,1)S(1)}, bf16[2048,2048]{1,0:T(8,128)(2,1)S(1)}, f32[8,128]{1,0:T(8,128)S(1)}) custom-call(s32[2]{0:T(128)S(1)} %pad_add_fusion.here, s32[32]{0:T(128)S(1)} %get-tuple-element.43.owners, bf16[32,2,512,256]{3,2,1,0:T(8,128)(2,1)} %cache.3, ...), custom_call_target="tpu_custom_call" | custom-call | flops 1 | bytes 1 | tf_op jit(solution)/shard_map/fetch/pallas_call | solution.py:664
  42.7 0.9 collective-permute-done.10.across
  43.7 1.5 %collective-permute-done.11.after.other.refs_1_ = bf16[4,32,1024]{2,1,0:T(8,128)(2,1)S(1)} collective-permute-done((bf16[4,32,1024]{2,1,0:T(8,128)(2,1)S(1)}, bf16[4,32,1024]{2,1,0:T(8,128)(2,1)S(1)}, u32[]{:S(2)}, u32[]{:S(2)}) %collective-permute-start.11) | collective-permute-done | bytes 262176 | tf_op jit(solution)/shard_map/ppermute | solution.py:48
  45.2 1.6 %attend.3.after = f32[8,72,128]{2,1,0:T(8,128)S(1)} custom-call(s32[2]{0:T(128)S(1)} %pad_add_fusion.here, s32[32]{0:T(128)S(1)} %get-tuple-element.42.limits, bf16[4,32,1024]{2,1,0:T(8,128)(2,1)S(1)} %collective-permute-done.11.after.other.refs_1_, bf16[4,32,1024]{2,1,0:T(8,128)(2,1)S(1)} %sum_queries.1.own.refs_0_, ...), custom_call_target="tpu_custom_call" | custom-call | flops 1 | bytes 1 | tf_op jit(solution)/shard_map/attend/pallas_call | solution.py:507
  47.0 1.6 %attend.4.after = f32[8,72,128]{2,1,0:T(8,128)S(1)} custom-call(s32[2]{0:T(128)S(1)} %pad_add_fusion.here, s32[32]{0:T(128)S(1)} %get-tuple-element.42.limits, f32[8,72,128]{2,1,0:T(8,128)S(1)} %attend.3.after, bf16[4,32,1024]{2,1,0:T(8,128)(2,1)S(1)} %sum_queries.1.own.refs_0_, bf16[4,32,1024]{2,1,0:T(8,128)(2,1)S(1)} %collective-permute-done.11.after.other.refs_1_, ...), custom_call_target="tpu_custom_call" | custom-call | flops 1 | bytes 1 | tf_op jit(solution)/shard_map/attend/pallas_call | solution.py:507
  49.0 1.7 %attend.5.a = f32[8,72,128]{2,1,0:T(8,128)S(1)} custom-call(s32[2]{0:T(128)S(1)} %pad_add_fusion.here, s32[32]{0:T(128)S(1)} %get-tuple-element.42.limits, f32[8,72,128]{2,1,0:T(8,128)S(1)} %attend.4.after, bf16[4,32,1024]{2,1,0:T(8,128)(2,1)S(1)} %sum_queries.1.own.refs_0_, bf16[4,32,1024]{2,1,0:T(8,128)(2,1)S(1)} %collective-permute-done.11.after.other.refs_1_, ...), custom_call_target="tpu_custom_call" | custom-call | flops 1 | bytes 1 | tf_op jit(solution)/shard_map/attend/pallas_call | solution.py:507
  51.0 1.6 %collective-permute-start.14 = (f32[8,72,128]{2,1,0:T(8,128)S(1)}, f32[8,72,128]{2,1,0:T(8,128)S(1)}, u32[]{:S(2)}, u32[]{:S(2)}) collective-permute-start(f32[8,72,128]{2,1,0:T(8,128)S(1)} %merge.1.after), channel_id=1, source_target_pairs={{0,8},{4,12},{8,0},{12,4},{1,9},{5,13},{9,1},{13,5},{2,10},{6,14},... | collective-permute-start | bytes 884744 | tf_op jit(solution)/shard_map/ppermute | solution.py:48
  52.5 7.2 %attend_hold.1 = (f32[8,72,128]{2,1,0:T(8,128)S(1)}, bf16[2048,2048]{1,0:T(8,128)(2,1)S(1)}, bf16[2048,2048]{1,0:T(8,128)(2,1)S(1)}) custom-call(s32[2]{0:T(128)S(1)} %pad_add_fusion.here, s32[32]{0:T(128)S(1)} %get-tuple-element.42.limits, f32[8,72,128]{2,1,0:T(8,128)S(1)} %merge.1.after, bf16[2048,8192]{1,0:T(8,128)(2,1)} %refs_1_.3, ...), custom_call_target="tpu_custom_call" | custom-call | flops 1 | bytes 1 | tf_op jit(solution)/shard_map/attend_hold/pallas_call | solution.py:518
  60.1 1.7 %finish.1 = (bf16[32,2048]{1,0:T(8,128)(2,1)S(1)}, bf16[32,2048]{1,0:T(8,128)(2,1)S(1)}) custom-call(f32[8,72,128]{2,1,0:T(8,128)S(1)} %get-tuple-element.71.a, f32[8,72,128]{2,1,0:T(8,128)S(1)} %collective-permute-done.13.b, f32[8,72,128]{2,1,0:T(8,128)S(1)} %collective-permute-done.14.c, bf16[2048,2048]{1,0:T(8,128)(2,1)S(1)} %get-tuple-element.72.held_right), custom_call_target="tpu_custom_call" | custom-call | flops 1 | bytes 1 | tf_op jit(solution)/shard_map/finish/pallas_call | solution.py:737
  61.8 2.5 %collective-permute-start.15 = (bf16[32,2048]{1,0:T(8,128)(2,1)S(1)}, bf16[32,2048]{1,0:T(8,128)(2,1)S(1)}, u32[]{:S(2)}, u32[]{:S(2)}) collective-permute-start(bf16[32,2048]{1,0:T(8,128)(2,1)S(1)} %get-tuple-element.77), channel_id=1, source_target_pairs={{0,3},{1,2},{2,1},{3,0},{4,7},{5,6},{6,5},{7,4},{8,11},{9,10},{10,... | collective-permute-start | bytes 393224 | tf_op jit(solution)/shard_map/ppermute | solution.py:48
  64.3 3.0 %far_output.1 = (bf16[32,2048]{1,0:T(8,128)(2,1)S(1)}, bf16[32,2048]{1,0:T(8,128)(2,1)S(1)}) custom-call(bf16[32,2048]{1,0:T(8,128)(2,1)S(1)} %get-tuple-element.73.left.refs_0_, bf16[2048,2048]{1,0:T(8,128)(2,1)S(1)} %get-tuple-element.74.refs_0_, bf16[2048,2048]{1,0:T(8,128)(2,1)S(1)} %get-tuple-element.75.refs_1_), custom_call_target="tpu_custom_call" | custom-call | flops 1 | bytes 1 | tf_op jit(solution)/shard_map/far_output/pallas_call | solution.py:749
  67.3 1.9 %collective-permute-start.17 = (bf16[32,2048]{1,0:T(8,128)(2,1)S(1)}, bf16[32,2048]{1,0:T(8,128)(2,1)S(1)}, u32[]{:S(2)}, u32[]{:S(2)}) collective-permute-start(bf16[32,2048]{1,0:T(8,128)(2,1)S(1)} %get-tuple-element.78), channel_id=1, source_target_pairs={{0,1},{1,0},{2,3},{3,2},{4,5},{5,4},{6,7},{7,6},{8,9},{9,8},{10,11... | collective-permute-start | bytes 393224 | tf_op jit(solution)/shard_map/ppermute | solution.py:48
  69.2 4.5 %own_output.1.refs_0_ = f32[32,2048]{1,0:T(8,128)S(1)} custom-call(s32[2]{0:T(128)S(1)} %pad_add_fusion.here, bf16[32,2048]{1,0:T(8,128)(2,1)S(1)} %get-tuple-element.73.left.refs_0_, bf16[2048,8192]{1,0:T(8,128)(2,1)} %refs_1_.3, bf16[32,2048]{1,0:T(8,128)(2,1)S(1)} %get-tuple-element.76.refs_2_), custom_call_target="tpu_custom_call" | custom-call | flops 1 | bytes 1 | tf_op jit(solution)/shard_map/own_output/pallas_call | solution.py:185
  73.8 1.4 %collective-permute-done.16.refs_1_ = bf16[32,2048]{1,0:T(8,128)(2,1)S(1)} collective-permute-done((bf16[32,2048]{1,0:T(8,128)(2,1)S(1)}, bf16[32,2048]{1,0:T(8,128)(2,1)S(1)}, u32[]{:S(2)}, u32[]{:S(2)}) %collective-permute-start.16) | collective-permute-done | bytes 131104 | tf_op jit(solution)/shard_map/ppermute | solution.py:48
  75.2 2.0 %collective-permute-start.20 = (bf16[32,2048]{1,0:T(8,128)(2,1)S(1)}, bf16[32,2048]{1,0:T(8,128)(2,1)S(1)}, u32[]{:S(2)}, u32[]{:S(2)}) collective-permute-start(bf16[32,2048]{1,0:T(8,128)(2,1)S(1)} %add.5.refs_0_), channel_id=1, source_target_pairs={{0,3},{1,2},{2,1},{3,0},{4,7},{5,6},{6,5},{7,4},{8,11},{9,10},{10,... | collective-permute-start | bytes 393224 | tf_op jit(solution)/shard_map/ppermute | solution.py:48
  77.3 2.4 %collective-permute-start.19 = (bf16[32,2048]{1,0:T(8,128)(2,1)S(1)}, bf16[32,2048]{1,0:T(8,128)(2,1)S(1)}, u32[]{:S(2)}, u32[]{:S(2)}) collective-permute-start(bf16[32,2048]{1,0:T(8,128)(2,1)S(1)} %add.5.refs_0_), channel_id=1, source_target_pairs={{0,1},{1,0},{2,3},{3,2},{4,5},{5,4},{6,7},{7,6},{8,9},{9,8},{10,11... | collective-permute-start | bytes 393224 | tf_op jit(solution)/shard_map/ppermute | solution.py:48
  79.7 3.8 %collective-permute-done.20.refs_1_ = bf16[32,2048]{1,0:T(8,128)(2,1)S(1)} collective-permute-done((bf16[32,2048]{1,0:T(8,128)(2,1)S(1)}, bf16[32,2048]{1,0:T(8,128)(2,1)S(1)}, u32[]{:S(2)}, u32[]{:S(2)}) %collective-permute-start.20) | collective-permute-done | bytes 131104 | tf_op jit(solution)/shard_map/ppermute | solution.py:48
  83.5 1.3 %place.2.refs_2_ = bf16[32,8192]{1,0:T(8,128)(2,1)} custom-call(s32[2]{0:T(128)S(1)} %pad_add_fusion.here, bf16[32,2048]{1,0:T(8,128)(2,1)S(1)} %add.5.refs_0_, bf16[32,2048]{1,0:T(8,128)(2,1)S(1)} %collective-permute-done.20.refs_1_), custom_call_target="tpu_custom_call" | custom-call | flops 1 | bytes 1 | tf_op jit(solution)/shard_map/place/pallas_call | solution.py:767
  84.8 3.2 %collective-permute-done.18.refs_0_ = bf16[32,2048]{1,0:T(8,128)(2,1)S(1)} collective-permute-done((bf16[32,2048]{1,0:T(8,128)(2,1)S(1)}, bf16[32,2048]{1,0:T(8,128)(2,1)S(1)}, u32[]{:S(2)}, u32[]{:S(2)}) %collective-permute-start.18) | collective-permute-done | bytes 131104 | tf_op jit(solution)/shard_map/ppermute | solution.py:48
  88.0 1.3 %place.3 = bf16[32,8192]{1,0:T(8,128)(2,1)} custom-call(s32[2]{0:T(128)S(1)} %pad_add_fusion.here, bf16[32,2048]{1,0:T(8,128)(2,1)S(1)} %collective-permute-done.18.refs_0_, bf16[32,2048]{1,0:T(8,128)(2,1)S(1)} %collective-permute-done.19.refs_1_, bf16[32,8192]{1,0:T(8,128)(2,1)} %place.2.refs_2_), custom_call_target="tpu_custom_call", output_to_operand_aliasing={{}: (3, {})} | custom-call | flops 1 | bytes 1 | tf_op jit(solution)/shard_map/place/pallas_call | solution.py:767
  (32 shorter events, 3.5 us)
Async XLA Ops:
  2.6 2.1 %collective-permute-start.2 = (bf16[32,8192]{1,0:T(8,128)(2,1)S(1)}, bf16[32,8192]{1,0:T(8,128)(2,1)S(1)}, u32[]{:S(2)}, u32[]{:S(2)}) collective-permute-start(bf16[32,8192]{1,0:T(8,128)(2,1)S(1)} %get-tuple-element.45.refs_0_), channel_id=1, source_target_pairs={{0,4},{4,0},{8,12},{12,8},{1,5},{5,1},{9,13},{13,9},{2,6},{6,2},{1... | collective-permute-start | bytes 1572872 | tf_op jit(solution)/shard_map/ppermute | solution.py:48
  4.7 15.2 %collective-permute-start.4 = (bf16[4,2048,128]{2,1,0:T(8,128)(2,1)}, bf16[4,2048,128]{2,1,0:T(8,128)(2,1)S(1)}, u32[]{:S(2)}, u32[]{:S(2)}) collective-permute-start(bf16[4,2048,128]{2,1,0:T(8,128)(2,1)} %refs_4_.1), channel_id=1, source_target_pairs={{0,4},{4,0},{8,12},{12,8},{1,5},{5,1},{9,13},{13,9},{2,6},{6,2},{1... | collective-permute-start | bytes 6291464 | tf_op jit(solution)/shard_map/ppermute | solution.py:48
  5.1 27.7 %collective-permute-start.8 = (bf16[4,128,2048]{2,1,0:T(8,128)(2,1)}, bf16[4,128,2048]{2,1,0:T(8,128)(2,1)S(1)}, u32[]{:S(2)}, u32[]{:S(2)}) collective-permute-start(bf16[4,128,2048]{2,1,0:T(8,128)(2,1)} %refs_0_.4), channel_id=1, source_target_pairs={{0,4},{4,0},{8,12},{12,8},{1,5},{5,1},{9,13},{13,9},{2,6},{6,2},{1... | collective-permute-start | bytes 6291464 | tf_op jit(solution)/shard_map/ppermute | solution.py:48
  5.2 13.1 %collective-permute-start.1 = (bf16[32,2048]{1,0:T(8,128)(2,1)S(1)}, bf16[32,2048]{1,0:T(8,128)(2,1)S(1)}, u32[]{:S(2)}, u32[]{:S(2)}) collective-permute-start(bf16[32,2048]{1,0:T(8,128)(2,1)S(1)} %get-tuple-element.44.own), channel_id=1, source_target_pairs={{0,8},{4,12},{8,0},{12,4},{1,9},{5,13},{9,1},{13,5},{2,10},{6,14},... | collective-permute-start | bytes 393224 | tf_op jit(solution)/shard_map/ppermute | solution.py:48
  18.2 14.6 %collective-permute-start.9 = (f32[64,1024]{1,0:T(8,128)S(1)}, f32[64,1024]{1,0:T(8,128)S(1)}, u32[]{:S(2)}, u32[]{:S(2)}) collective-permute-start(f32[64,1024]{1,0:T(8,128)S(1)} %get-tuple-element.46.refs_10_), channel_id=1, source_target_pairs={{0,8},{4,12},{8,0},{12,4},{1,9},{5,13},{9,1},{13,5},{2,10},{6,14},... | collective-permute-start | bytes 786440 | tf_op jit(solution)/shard_map/ppermute | solution.py:48
  18.3 1.4 %collective-permute-start = (bf16[32,2048]{1,0:T(8,128)(2,1)S(1)}, bf16[32,2048]{1,0:T(8,128)(2,1)S(1)}, u32[]{:S(2)}, u32[]{:S(2)}) collective-permute-start(bf16[32,2048]{1,0:T(8,128)(2,1)S(1)} %get-tuple-element.44.own), channel_id=1, source_target_pairs={{0,4},{4,0},{8,12},{12,8},{1,5},{5,1},{9,13},{13,9},{2,6},{6,2},{1... | collective-permute-start | bytes 393224 | tf_op jit(solution)/shard_map/ppermute | solution.py:48
  18.3 1.5 %collective-permute-start.3 = (bf16[32,2048]{1,0:T(8,128)(2,1)S(1)}, bf16[32,2048]{1,0:T(8,128)(2,1)S(1)}, u32[]{:S(2)}, u32[]{:S(2)}) collective-permute-start(bf16[32,2048]{1,0:T(8,128)(2,1)S(1)} %collective-permute-done.1.across), channel_id=1, source_target_pairs={{0,4},{4,0},{8,12},{12,8},{1,5},{5,1},{9,13},{13,9},{2,6},{6,2},{1... | collective-permute-start | bytes 393224 | tf_op jit(solution)/shard_map/ppermute | solution.py:48
  21.7 11.1 %collective-permute-start.5 = (f32[192,128]{1,0:T(8,128)S(1)}, f32[192,128]{1,0:T(8,128)S(1)}, u32[]{:S(2)}, u32[]{:S(2)}) collective-permute-start(f32[192,128]{1,0:T(8,128)S(1)} %get-tuple-element.54), channel_id=1, source_target_pairs={{0,3},{1,2},{2,1},{3,0},{4,7},{5,6},{6,5},{7,4},{8,11},{9,10},{10,... | collective-permute-start | bytes 294920 | tf_op jit(solution)/shard_map/ppermute | solution.py:48
  25.8 8.8 %collective-permute-start.6 = (f32[192,128]{1,0:T(8,128)S(1)}, f32[192,128]{1,0:T(8,128)S(1)}, u32[]{:S(2)}, u32[]{:S(2)}) collective-permute-start(f32[192,128]{1,0:T(8,128)S(1)} %get-tuple-element.55), channel_id=1, source_target_pairs={{0,2},{1,3},{2,0},{3,1},{4,6},{5,7},{6,4},{7,5},{8,10},{9,11},{10,... | collective-permute-start | bytes 294920 | tf_op jit(solution)/shard_map/ppermute | solution.py:48
  25.8 8.8 %collective-permute-start.7 = (f32[192,128]{1,0:T(8,128)S(1)}, f32[192,128]{1,0:T(8,128)S(1)}, u32[]{:S(2)}, u32[]{:S(2)}) collective-permute-start(f32[192,128]{1,0:T(8,128)S(1)} %get-tuple-element.56), channel_id=1, source_target_pairs={{0,1},{1,0},{2,3},{3,2},{4,5},{5,4},{6,7},{7,6},{8,9},{9,8},{10,11... | collective-permute-start | bytes 294920 | tf_op jit(solution)/shard_map/ppermute | solution.py:48
  35.7 7.8 %collective-permute-start.10 = (bf16[4,32,1024]{2,1,0:T(8,128)(2,1)S(1)}, bf16[4,32,1024]{2,1,0:T(8,128)(2,1)S(1)}, u32[]{:S(2)}, u32[]{:S(2)}) collective-permute-start(bf16[4,32,1024]{2,1,0:T(8,128)(2,1)S(1)} %queries.1.after.own), channel_id=1, source_target_pairs={{0,8},{4,12},{8,0},{12,4},{1,9},{5,13},{9,1},{13,5},{2,10},{6,14},... | collective-permute-start | bytes 786440 | tf_op jit(solution)/shard_map/ppermute | solution.py:48
  43.6 1.6 %collective-permute-start.11 = (bf16[4,32,1024]{2,1,0:T(8,128)(2,1)S(1)}, bf16[4,32,1024]{2,1,0:T(8,128)(2,1)S(1)}, u32[]{:S(2)}, u32[]{:S(2)}) collective-permute-start(bf16[4,32,1024]{2,1,0:T(8,128)(2,1)S(1)} %sum_queries.1.own.refs_0_), channel_id=1, source_target_pairs={{0,4},{4,0},{8,12},{12,8},{1,5},{5,1},{9,13},{13,9},{2,6},{6,2},{1... | collective-permute-start | bytes 786440 | tf_op jit(solution)/shard_map/ppermute | solution.py:48
  46.8 3.9 %collective-permute-start.12 = (f32[8,72,128]{2,1,0:T(8,128)S(1)}, f32[8,72,128]{2,1,0:T(8,128)S(1)}, u32[]{:S(2)}, u32[]{:S(2)}) collective-permute-start(f32[8,72,128]{2,1,0:T(8,128)S(1)} %attend.3.after), channel_id=1, source_target_pairs={{0,4},{4,0},{8,12},{12,8},{1,5},{5,1},{9,13},{13,9},{2,6},{6,2},{1... | collective-permute-start | bytes 884744 | tf_op jit(solution)/shard_map/ppermute | solution.py:48
  48.6 11.1 %collective-permute-start.13 = (f32[8,72,128]{2,1,0:T(8,128)S(1)}, f32[8,72,128]{2,1,0:T(8,128)S(1)}, u32[]{:S(2)}, u32[]{:S(2)}) collective-permute-start(f32[8,72,128]{2,1,0:T(8,128)S(1)} %attend.4.after), channel_id=1, source_target_pairs={{0,4},{4,0},{8,12},{12,8},{1,5},{5,1},{9,13},{13,9},{2,6},{6,2},{1... | collective-permute-start | bytes 884744 | tf_op jit(solution)/shard_map/ppermute | solution.py:48
  51.0 9.1 %collective-permute-start.14 = (f32[8,72,128]{2,1,0:T(8,128)S(1)}, f32[8,72,128]{2,1,0:T(8,128)S(1)}, u32[]{:S(2)}, u32[]{:S(2)}) collective-permute-start(f32[8,72,128]{2,1,0:T(8,128)S(1)} %merge.1.after), channel_id=1, source_target_pairs={{0,8},{4,12},{8,0},{12,4},{1,9},{5,13},{9,1},{13,5},{2,10},{6,14},... | collective-permute-start | bytes 884744 | tf_op jit(solution)/shard_map/ppermute | solution.py:48
  61.8 11.9 %collective-permute-start.15 = (bf16[32,2048]{1,0:T(8,128)(2,1)S(1)}, bf16[32,2048]{1,0:T(8,128)(2,1)S(1)}, u32[]{:S(2)}, u32[]{:S(2)}) collective-permute-start(bf16[32,2048]{1,0:T(8,128)(2,1)S(1)} %get-tuple-element.77), channel_id=1, source_target_pairs={{0,3},{1,2},{2,1},{3,0},{4,7},{5,6},{6,5},{7,4},{8,11},{9,10},{10,... | collective-permute-start | bytes 393224 | tf_op jit(solution)/shard_map/ppermute | solution.py:48
  67.3 7.9 %collective-permute-start.16 = (bf16[32,2048]{1,0:T(8,128)(2,1)S(1)}, bf16[32,2048]{1,0:T(8,128)(2,1)S(1)}, u32[]{:S(2)}, u32[]{:S(2)}) collective-permute-start(bf16[32,2048]{1,0:T(8,128)(2,1)S(1)} %get-tuple-element.76.refs_2_), channel_id=1, source_target_pairs={{0,2},{1,3},{2,0},{3,1},{4,6},{5,7},{6,4},{7,5},{8,10},{9,11},{10,... | collective-permute-start | bytes 393224 | tf_op jit(solution)/shard_map/ppermute | solution.py:48
  67.3 7.9 %collective-permute-start.17 = (bf16[32,2048]{1,0:T(8,128)(2,1)S(1)}, bf16[32,2048]{1,0:T(8,128)(2,1)S(1)}, u32[]{:S(2)}, u32[]{:S(2)}) collective-permute-start(bf16[32,2048]{1,0:T(8,128)(2,1)S(1)} %get-tuple-element.78), channel_id=1, source_target_pairs={{0,1},{1,0},{2,3},{3,2},{4,5},{5,4},{6,7},{7,6},{8,9},{9,8},{10,11... | collective-permute-start | bytes 393224 | tf_op jit(solution)/shard_map/ppermute | solution.py:48
  75.2 8.3 %collective-permute-start.20 = (bf16[32,2048]{1,0:T(8,128)(2,1)S(1)}, bf16[32,2048]{1,0:T(8,128)(2,1)S(1)}, u32[]{:S(2)}, u32[]{:S(2)}) collective-permute-start(bf16[32,2048]{1,0:T(8,128)(2,1)S(1)} %add.5.refs_0_), channel_id=1, source_target_pairs={{0,3},{1,2},{2,1},{3,0},{4,7},{5,6},{6,5},{7,4},{8,11},{9,10},{10,... | collective-permute-start | bytes 393224 | tf_op jit(solution)/shard_map/ppermute | solution.py:48
  77.3 10.7 %collective-permute-start.18 = (bf16[32,2048]{1,0:T(8,128)(2,1)S(1)}, bf16[32,2048]{1,0:T(8,128)(2,1)S(1)}, u32[]{:S(2)}, u32[]{:S(2)}) collective-permute-start(bf16[32,2048]{1,0:T(8,128)(2,1)S(1)} %add.5.refs_0_), channel_id=1, source_target_pairs={{0,2},{1,3},{2,0},{3,1},{4,6},{5,7},{6,4},{7,5},{8,10},{9,11},{10,... | collective-permute-start | bytes 393224 | tf_op jit(solution)/shard_map/ppermute | solution.py:48
  77.3 10.7 %collective-permute-start.19 = (bf16[32,2048]{1,0:T(8,128)(2,1)S(1)}, bf16[32,2048]{1,0:T(8,128)(2,1)S(1)}, u32[]{:S(2)}, u32[]{:S(2)}) collective-permute-start(bf16[32,2048]{1,0:T(8,128)(2,1)S(1)} %add.5.refs_0_), channel_id=1, source_target_pairs={{0,1},{1,0},{2,3},{3,2},{4,5},{5,4},{6,7},{7,6},{8,9},{9,8},{10,11... | collective-permute-start | bytes 393224 | tf_op jit(solution)/shard_map/ppermute | solution.py:48

commit v5 on v4

--- a/solution.py
+++ b/solution.py
@@ -611,8 +611,8 @@
     jobs = [(0, lambda at: (at[0] & 1) * (half_cols // 128), half_cols, chunk)]
     if packed:
         jobs += [(1, lambda at: 0, wkv.shape[1], 2 * chunk)]
-    plain_near, *kv_part, held_down = product(
-        "query", here, (normed, normed_beside), (wq, wkv), jobs, [F32] * len(jobs), (adapter_down,)
+    plain_near, *kv_part = product(
+        "query", here, (normed, normed_beside), (wq, wkv), jobs, [F32] * len(jobs)
     )
     kv_part = kv_part[0] if packed else jnp.dot(normed, wkv, preferred_element_type=F32)
     plain_far = swap(plain_near, "section", 2)
@@ -631,7 +631,7 @@
     )(
         here,
         *in_vmem(
-            piece, piece_beside, piece_across, piece_beside_across, pick, held_down, down_beside, kv_part
+            piece, piece_beside, piece_across, piece_beside_across, pick, adapter_down, down_beside, kv_part
         ),
     )
     if packed:

time: 89.6 us -> 89 us (level)
  no operation moved by 1% of the time
where the time goes in v5:
time: 89 us; the launch traced here: 88.9 us
  Pallas kernels  50.8 us (57%)
  starting transfers between devices  22 us (25%)
  waiting for transfers between devices  15.5 us (17%)
    ppermute x21, starting transfers between devices, swap(): return jax.tree.map(lambda a: lax.ppermute(a, axis, pairs), value)  22 us
    ppermute x21, waiting for transfers between devices, swap(): return jax.tree.map(lambda a: lax.ppermute(a, axis, pairs), value)  15.5 us
    pallas_call x2, Pallas kernels, product(): pl.pallas_call(functools.partial(product_kernel, sizes, jobs), out_shape=...  14.1 us
    pallas_call x2, Pallas kernels, fetch(): pl.pallas_call(functools.partial(fetch_kernel, places, slots, [start] * l...  11.7 us
    pallas_call x1, Pallas kernels, attend(): pl.pallas_call(functools.partial(attend_and_hold_kernel, starts, len(oper...  7.2 us
    pallas_call x3, Pallas kernels, attend(): pl.pallas_call(body, out_shape=out, in_specs=[SMEM] * 2 + [ANYWHERE] + [V...  4.87 us
    pallas_call x1, Pallas kernels, per_device(): pl.pallas_call(far_kernel, out_shape=(block,) * len(held_wo), in_specs=[V...  2.97 us
    pallas_call x2, Pallas kernels, place(): pl.pallas_call(functools.partial(place_kernel, [columns[bit] for bit in b...  2.52 us
  transfers between devices with their start and end apart: 21, of which 10 were waited for; matrix products, arithmetic and copies ran while one was open for 0% of the time, Pallas kernels for 48%

profile of v5, /device:TPU:0, one launch (start us, length us, event | category | flops | bytes accessed | tf_op | source)
XLA Modules:
  0.0 88.9 jit_solution(15056123477597768547)
XLA Ops:
  0.2 2.5 %start.1 = (bf16[32,8192]{1,0:T(8,128)(2,1)S(1)}, bf16[32,2048]{1,0:T(8,128)(2,1)S(1)}, s32[32]{0:T(128)S(1)}, s32[32]{0:T(128)S(1)}, f32[32,128]{1,0:T(8,128)S(...) custom-call(s32[2]{0:T(128)S(1)} %pad_add_fusion.here, s32[32]{0:T(128)} %refs_0_.3, ...), custom_call_target="tpu_custom_call" | custom-call | flops 1 | bytes 1 | tf_op jit(solution)/shard_map/start/pallas_call | solution.py:575
  3.2 1.5 %collective-permute-done.2.refs_1_ = bf16[32,8192]{1,0:T(8,128)(2,1)S(1)} collective-permute-done((bf16[32,8192]{1,0:T(8,128)(2,1)S(1)}, bf16[32,8192]{1,0:T(8,128)(2,1)S(1)}, u32[]{:S(2)}, u32[]{:S(2)}) %collective-permute-start.2) | collective-permute-done | bytes 524320 | tf_op jit(solution)/shard_map/ppermute | solution.py:48
  5.2 2.9 %collective-permute-start.1 = (bf16[32,2048]{1,0:T(8,128)(2,1)S(1)}, bf16[32,2048]{1,0:T(8,128)(2,1)S(1)}, u32[]{:S(2)}, u32[]{:S(2)}) collective-permute-start(bf16[32,2048]{1,0:T(8,128)(2,1)S(1)} %get-tuple-element.43.own), channel_id=1, source_target_pairs={{0,8},{4,12},{8,0},{12,4},{1,9},{5,13},{9,1},{13,5},{2,10},{6,14},... | collective-permute-start | bytes 393224 | tf_op jit(solution)/shard_map/ppermute | solution.py:48
  8.1 9.5 %query.1 = (f32[64,1024]{1,0:T(8,128)S(1)}, f32[64,512]{1,0:T(8,128)S(1)}) custom-call(s32[2]{0:T(128)S(1)} %pad_add_fusion.here, bf16[32,8192]{1,0:T(8,128)(2,1)S(1)} %get-tuple-element.44.refs_0_, bf16[32,8192]{1,0:T(8,128)(2,1)S(1)} %collective-permute-done.2.refs_1_, bf16[8192,2048]{1,0:T(8,128)(2,1)} %refs_2_.3, bf16[8192,512]{1,0:T(8,128)(2,1)} %refs_3_.3), custom_call_target="tpu_custom_call" | custom-call | flops 1 | bytes 1 | tf_op jit(solution)/shard_map/query/pallas_call | solution.py:185
  18.3 0.8 collective-permute-done.beside
  19.3 1.8 %down.2 = (f32[128,128]{1,0:T(8,128)S(1)}, f32[192,128]{1,0:T(8,128)S(1)}, f32[192,128]{1,0:T(8,128)S(1)}, f32[192,128]{1,0:T(8,128)S(1)}) custom-call(s32[2]{0:T(128)S(1)} %pad_add_fusion.here, bf16[32,2048]{1,0:T(8,128)(2,1)S(1)} %get-tuple-element.43.own, bf16[32,2048]{1,0:T(8,128)(2,1)S(1)} %collective-permute-done.beside, ...), custom_call_target="tpu_custom_call" | custom-call | flops 1 | bytes 1 | tf_op jit(solution)/shard_map/down/pallas_call | solution.py:623
  21.1 4.1 %collective-permute-start.5 = (f32[192,128]{1,0:T(8,128)S(1)}, f32[192,128]{1,0:T(8,128)S(1)}, u32[]{:S(2)}, u32[]{:S(2)}) collective-permute-start(f32[192,128]{1,0:T(8,128)S(1)} %get-tuple-element.52), channel_id=1, source_target_pairs={{0,3},{1,2},{2,1},{3,0},{4,7},{5,6},{6,5},{7,4},{8,11},{9,10},{10,... | collective-permute-start | bytes 294920 | tf_op jit(solution)/shard_map/ppermute | solution.py:48
  25.2 0.6 collective-permute-start.7
  25.9 6.3 %fetch.2 = (bf16[8,256,512]{2,1,0:T(8,128)(2,1)S(1)}, bf16[8,256,512]{2,1,0:T(8,128)(2,1)S(1)}, bf16[8,256,512]{2,1,0:T(8,128)(2,1)S(1)}, bf16[8,512,256]{2,1,0:...) custom-call(s32[2]{0:T(128)S(1)} %pad_add_fusion.here, ...), custom_call_target="tpu_custom_call" | custom-call | flops 1 | bytes 1 | tf_op jit(solution)/shard_map/fetch/pallas_call | solution.py:664
  32.2 1.8 %collective-permute-done.6.refs_2_.refs_6_ = f32[192,128]{1,0:T(8,128)S(1)} collective-permute-done((f32[192,128]{1,0:T(8,128)S(1)}, f32[192,128]{1,0:T(8,128)S(1)}, u32[]{:S(2)}, u32[]{:S(2)}) %collective-permute-start.6) | collective-permute-done | bytes 98336 | tf_op jit(solution)/shard_map/ppermute | solution.py:48
  34.0 1.1 %queries.1.after.own = bf16[4,32,1024]{2,1,0:T(8,128)(2,1)S(1)} custom-call(s32[2]{0:T(128)S(1)} %pad_add_fusion.here, f32[8,128]{1,0:T(8,128)S(1)} %get-tuple-element.51.after, f32[128,128]{1,0:T(8,128)S(1)} %get-tuple-element.50.after.refs_0_, f32[192,128]{1,0:T(8,128)S(1)} %collective-permute-done.5.refs_1_.refs_7_, ...), custom_call_target="tpu_custom_call" | custom-call | flops 1 | bytes 1 | tf_op jit(solution)/shard_map/queries/pallas_call | solution.py:686
  35.1 1.6 %collective-permute-start.10 = (bf16[4,32,1024]{2,1,0:T(8,128)(2,1)S(1)}, bf16[4,32,1024]{2,1,0:T(8,128)(2,1)S(1)}, u32[]{:S(2)}, u32[]{:S(2)}) collective-permute-start(bf16[4,32,1024]{2,1,0:T(8,128)(2,1)S(1)} %queries.1.after.own), channel_id=1, source_target_pairs={{0,8},{4,12},{8,0},{12,4},{1,9},{5,13},{9,1},{13,5},{2,10},{6,14},... | collective-permute-start | bytes 786440 | tf_op jit(solution)/shard_map/ppermute | solution.py:48
  36.7 5.4 %fetch.3 = (bf16[8,256,512]{2,1,0:T(8,128)(2,1)S(1)}, bf16[8,512,256]{2,1,0:T(8,128)(2,1)S(1)}, bf16[2048,2048]{1,0:T(8,128)(2,1)S(1)}, f32[8,128]{1,0:T(8,128)S(1)}) custom-call(s32[2]{0:T(128)S(1)} %pad_add_fusion.here, s32[32]{0:T(128)S(1)} %get-tuple-element.42.owners, bf16[32,2,512,256]{3,2,1,0:T(8,128)(2,1)} %cache.3, ...), custom_call_target="tpu_custom_call" | custom-call | flops 1 | bytes 1 | tf_op jit(solution)/shard_map/fetch/pallas_call | solution.py:664
  42.1 0.9 collective-permute-done.10.across
  43.1 1.5 %collective-permute-done.11.after.other.refs_1_ = bf16[4,32,1024]{2,1,0:T(8,128)(2,1)S(1)} collective-permute-done((bf16[4,32,1024]{2,1,0:T(8,128)(2,1)S(1)}, bf16[4,32,1024]{2,1,0:T(8,128)(2,1)S(1)}, u32[]{:S(2)}, u32[]{:S(2)}) %collective-permute-start.11) | collective-permute-done | bytes 262176 | tf_op jit(solution)/shard_map/ppermute | solution.py:48
  44.6 1.6 %attend.3.after = f32[8,72,128]{2,1,0:T(8,128)S(1)} custom-call(s32[2]{0:T(128)S(1)} %pad_add_fusion.here, s32[32]{0:T(128)S(1)} %get-tuple-element.41.limits, bf16[4,32,1024]{2,1,0:T(8,128)(2,1)S(1)} %collective-permute-done.11.after.other.refs_1_, bf16[4,32,1024]{2,1,0:T(8,128)(2,1)S(1)} %sum_queries.1.own.refs_0_, ...), custom_call_target="tpu_custom_call" | custom-call | flops 1 | bytes 1 | tf_op jit(solution)/shard_map/attend/pallas_call | solution.py:507
  46.4 1.6 %attend.4.after = f32[8,72,128]{2,1,0:T(8,128)S(1)} custom-call(s32[2]{0:T(128)S(1)} %pad_add_fusion.here, s32[32]{0:T(128)S(1)} %get-tuple-element.41.limits, f32[8,72,128]{2,1,0:T(8,128)S(1)} %attend.3.after, bf16[4,32,1024]{2,1,0:T(8,128)(2,1)S(1)} %sum_queries.1.own.refs_0_, bf16[4,32,1024]{2,1,0:T(8,128)(2,1)S(1)} %collective-permute-done.11.after.other.refs_1_, ...), custom_call_target="tpu_custom_call" | custom-call | flops 1 | bytes 1 | tf_op jit(solution)/shard_map/attend/pallas_call | solution.py:507
  48.4 1.7 %attend.5.a = f32[8,72,128]{2,1,0:T(8,128)S(1)} custom-call(s32[2]{0:T(128)S(1)} %pad_add_fusion.here, s32[32]{0:T(128)S(1)} %get-tuple-element.41.limits, f32[8,72,128]{2,1,0:T(8,128)S(1)} %attend.4.after, bf16[4,32,1024]{2,1,0:T(8,128)(2,1)S(1)} %sum_queries.1.own.refs_0_, bf16[4,32,1024]{2,1,0:T(8,128)(2,1)S(1)} %collective-permute-done.11.after.other.refs_1_, ...), custom_call_target="tpu_custom_call" | custom-call | flops 1 | bytes 1 | tf_op jit(solution)/shard_map/attend/pallas_call | solution.py:507
  50.4 1.6 %collective-permute-start.14 = (f32[8,72,128]{2,1,0:T(8,128)S(1)}, f32[8,72,128]{2,1,0:T(8,128)S(1)}, u32[]{:S(2)}, u32[]{:S(2)}) collective-permute-start(f32[8,72,128]{2,1,0:T(8,128)S(1)} %merge.1.after), channel_id=1, source_target_pairs={{0,8},{4,12},{8,0},{12,4},{1,9},{5,13},{9,1},{13,5},{2,10},{6,14},... | collective-permute-start | bytes 884744 | tf_op jit(solution)/shard_map/ppermute | solution.py:48
  52.0 7.2 %attend_hold.1 = (f32[8,72,128]{2,1,0:T(8,128)S(1)}, bf16[2048,2048]{1,0:T(8,128)(2,1)S(1)}, bf16[2048,2048]{1,0:T(8,128)(2,1)S(1)}) custom-call(s32[2]{0:T(128)S(1)} %pad_add_fusion.here, s32[32]{0:T(128)S(1)} %get-tuple-element.41.limits, f32[8,72,128]{2,1,0:T(8,128)S(1)} %merge.1.after, bf16[2048,8192]{1,0:T(8,128)(2,1)} %refs_1_.3, ...), custom_call_target="tpu_custom_call" | custom-call | flops 1 | bytes 1 | tf_op jit(solution)/shard_map/attend_hold/pallas_call | solution.py:518
  59.6 1.7 %finish.1 = (bf16[32,2048]{1,0:T(8,128)(2,1)S(1)}, bf16[32,2048]{1,0:T(8,128)(2,1)S(1)}) custom-call(f32[8,72,128]{2,1,0:T(8,128)S(1)} %get-tuple-element.69.a, f32[8,72,128]{2,1,0:T(8,128)S(1)} %collective-permute-done.13.b, f32[8,72,128]{2,1,0:T(8,128)S(1)} %collective-permute-done.14.c, bf16[2048,2048]{1,0:T(8,128)(2,1)S(1)} %get-tuple-element.70.held_right), custom_call_target="tpu_custom_call" | custom-call | flops 1 | bytes 1 | tf_op jit(solution)/shard_map/finish/pallas_call | solution.py:737
  61.3 2.5 %collective-permute-start.15 = (bf16[32,2048]{1,0:T(8,128)(2,1)S(1)}, bf16[32,2048]{1,0:T(8,128)(2,1)S(1)}, u32[]{:S(2)}, u32[]{:S(2)}) collective-permute-start(bf16[32,2048]{1,0:T(8,128)(2,1)S(1)} %get-tuple-element.75), channel_id=1, source_target_pairs={{0,3},{1,2},{2,1},{3,0},{4,7},{5,6},{6,5},{7,4},{8,11},{9,10},{10,... | collective-permute-start | bytes 393224 | tf_op jit(solution)/shard_map/ppermute | solution.py:48
  63.8 3.0 %far_output.1 = (bf16[32,2048]{1,0:T(8,128)(2,1)S(1)}, bf16[32,2048]{1,0:T(8,128)(2,1)S(1)}) custom-call(bf16[32,2048]{1,0:T(8,128)(2,1)S(1)} %get-tuple-element.71.left.refs_0_, bf16[2048,2048]{1,0:T(8,128)(2,1)S(1)} %get-tuple-element.72.refs_0_, bf16[2048,2048]{1,0:T(8,128)(2,1)S(1)} %get-tuple-element.73.refs_1_), custom_call_target="tpu_custom_call" | custom-call | flops 1 | bytes 1 | tf_op jit(solution)/shard_map/far_output/pallas_call | solution.py:749
  66.8 1.9 %collective-permute-start.17 = (bf16[32,2048]{1,0:T(8,128)(2,1)S(1)}, bf16[32,2048]{1,0:T(8,128)(2,1)S(1)}, u32[]{:S(2)}, u32[]{:S(2)}) collective-permute-start(bf16[32,2048]{1,0:T(8,128)(2,1)S(1)} %get-tuple-element.76), channel_id=1, source_target_pairs={{0,1},{1,0},{2,3},{3,2},{4,5},{5,4},{6,7},{7,6},{8,9},{9,8},{10,11... | collective-permute-start | bytes 393224 | tf_op jit(solution)/shard_map/ppermute | solution.py:48
  68.7 4.5 %own_output.1.refs_0_ = f32[32,2048]{1,0:T(8,128)S(1)} custom-call(s32[2]{0:T(128)S(1)} %pad_add_fusion.here, bf16[32,2048]{1,0:T(8,128)(2,1)S(1)} %get-tuple-element.71.left.refs_0_, bf16[2048,8192]{1,0:T(8,128)(2,1)} %refs_1_.3, bf16[32,2048]{1,0:T(8,128)(2,1)S(1)} %get-tuple-element.74.refs_2_), custom_call_target="tpu_custom_call" | custom-call | flops 1 | bytes 1 | tf_op jit(solution)/shard_map/own_output/pallas_call | solution.py:185
  73.3 1.4 %collective-permute-done.16.refs_1_ = bf16[32,2048]{1,0:T(8,128)(2,1)S(1)} collective-permute-done((bf16[32,2048]{1,0:T(8,128)(2,1)S(1)}, bf16[32,2048]{1,0:T(8,128)(2,1)S(1)}, u32[]{:S(2)}, u32[]{:S(2)}) %collective-permute-start.16) | collective-permute-done | bytes 131104 | tf_op jit(solution)/shard_map/ppermute | solution.py:48
  74.7 2.0 %collective-permute-start.20 = (bf16[32,2048]{1,0:T(8,128)(2,1)S(1)}, bf16[32,2048]{1,0:T(8,128)(2,1)S(1)}, u32[]{:S(2)}, u32[]{:S(2)}) collective-permute-start(bf16[32,2048]{1,0:T(8,128)(2,1)S(1)} %add.5.refs_0_), channel_id=1, source_target_pairs={{0,3},{1,2},{2,1},{3,0},{4,7},{5,6},{6,5},{7,4},{8,11},{9,10},{10,... | collective-permute-start | bytes 393224 | tf_op jit(solution)/shard_map/ppermute | solution.py:48
  76.8 2.4 %collective-permute-start.19 = (bf16[32,2048]{1,0:T(8,128)(2,1)S(1)}, bf16[32,2048]{1,0:T(8,128)(2,1)S(1)}, u32[]{:S(2)}, u32[]{:S(2)}) collective-permute-start(bf16[32,2048]{1,0:T(8,128)(2,1)S(1)} %add.5.refs_0_), channel_id=1, source_target_pairs={{0,1},{1,0},{2,3},{3,2},{4,5},{5,4},{6,7},{7,6},{8,9},{9,8},{10,11... | collective-permute-start | bytes 393224 | tf_op jit(solution)/shard_map/ppermute | solution.py:48
  79.2 3.8 %collective-permute-done.20.refs_1_ = bf16[32,2048]{1,0:T(8,128)(2,1)S(1)} collective-permute-done((bf16[32,2048]{1,0:T(8,128)(2,1)S(1)}, bf16[32,2048]{1,0:T(8,128)(2,1)S(1)}, u32[]{:S(2)}, u32[]{:S(2)}) %collective-permute-start.20) | collective-permute-done | bytes 131104 | tf_op jit(solution)/shard_map/ppermute | solution.py:48
  83.0 1.3 %place.2.refs_2_ = bf16[32,8192]{1,0:T(8,128)(2,1)} custom-call(s32[2]{0:T(128)S(1)} %pad_add_fusion.here, bf16[32,2048]{1,0:T(8,128)(2,1)S(1)} %add.5.refs_0_, bf16[32,2048]{1,0:T(8,128)(2,1)S(1)} %collective-permute-done.20.refs_1_), custom_call_target="tpu_custom_call" | custom-call | flops 1 | bytes 1 | tf_op jit(solution)/shard_map/place/pallas_call | solution.py:767
  84.3 3.2 %collective-permute-done.18.refs_0_ = bf16[32,2048]{1,0:T(8,128)(2,1)S(1)} collective-permute-done((bf16[32,2048]{1,0:T(8,128)(2,1)S(1)}, bf16[32,2048]{1,0:T(8,128)(2,1)S(1)}, u32[]{:S(2)}, u32[]{:S(2)}) %collective-permute-start.18) | collective-permute-done | bytes 131104 | tf_op jit(solution)/shard_map/ppermute | solution.py:48
  87.5 1.3 %place.3 = bf16[32,8192]{1,0:T(8,128)(2,1)} custom-call(s32[2]{0:T(128)S(1)} %pad_add_fusion.here, bf16[32,2048]{1,0:T(8,128)(2,1)S(1)} %collective-permute-done.18.refs_0_, bf16[32,2048]{1,0:T(8,128)(2,1)S(1)} %collective-permute-done.19.refs_1_, bf16[32,8192]{1,0:T(8,128)(2,1)} %place.2.refs_2_), custom_call_target="tpu_custom_call", output_to_operand_aliasing={{}: (3, {})} | custom-call | flops 1 | bytes 1 | tf_op jit(solution)/shard_map/place/pallas_call | solution.py:767
  (34 shorter events, 3.5 us)
Async XLA Ops:
  2.6 2.1 %collective-permute-start.2 = (bf16[32,8192]{1,0:T(8,128)(2,1)S(1)}, bf16[32,8192]{1,0:T(8,128)(2,1)S(1)}, u32[]{:S(2)}, u32[]{:S(2)}) collective-permute-start(bf16[32,8192]{1,0:T(8,128)(2,1)S(1)} %get-tuple-element.44.refs_0_), channel_id=1, source_target_pairs={{0,4},{4,0},{8,12},{12,8},{1,5},{5,1},{9,13},{13,9},{2,6},{6,2},{1... | collective-permute-start | bytes 1572872 | tf_op jit(solution)/shard_map/ppermute | solution.py:48
  4.7 14.6 %collective-permute-start.4 = (bf16[4,2048,128]{2,1,0:T(8,128)(2,1)}, bf16[4,2048,128]{2,1,0:T(8,128)(2,1)S(1)}, u32[]{:S(2)}, u32[]{:S(2)}) collective-permute-start(bf16[4,2048,128]{2,1,0:T(8,128)(2,1)} %down.3), channel_id=1, source_target_pairs={{0,4},{4,0},{8,12},{12,8},{1,5},{5,1},{9,13},{13,9},{2,6},{6,2},{1... | collective-permute-start | bytes 6291464 | tf_op jit(solution)/shard_map/ppermute | solution.py:48
  5.1 27.2 %collective-permute-start.8 = (bf16[4,128,2048]{2,1,0:T(8,128)(2,1)}, bf16[4,128,2048]{2,1,0:T(8,128)(2,1)S(1)}, u32[]{:S(2)}, u32[]{:S(2)}) collective-permute-start(bf16[4,128,2048]{2,1,0:T(8,128)(2,1)} %refs_0_.4), channel_id=1, source_target_pairs={{0,4},{4,0},{8,12},{12,8},{1,5},{5,1},{9,13},{13,9},{2,6},{6,2},{1... | collective-permute-start | bytes 6291464 | tf_op jit(solution)/shard_map/ppermute | solution.py:48
  5.2 14.1 %copy-start = (bf16[4,2048,128]{2,1,0:T(8,128)(2,1)S(1)}, bf16[4,2048,128]{2,1,0:T(8,128)(2,1)}, u32[]{:S(2)}) copy-start(bf16[4,2048,128]{2,1,0:T(8,128)(2,1)} %down.3) | copy-start | bytes 6291460
  5.2 12.6 %collective-permute-start.1 = (bf16[32,2048]{1,0:T(8,128)(2,1)S(1)}, bf16[32,2048]{1,0:T(8,128)(2,1)S(1)}, u32[]{:S(2)}, u32[]{:S(2)}) collective-permute-start(bf16[32,2048]{1,0:T(8,128)(2,1)S(1)} %get-tuple-element.43.own), channel_id=1, source_target_pairs={{0,8},{4,12},{8,0},{12,4},{1,9},{5,13},{9,1},{13,5},{2,10},{6,14},... | collective-permute-start | bytes 393224 | tf_op jit(solution)/shard_map/ppermute | solution.py:48
  17.6 14.6 %collective-permute-start.9 = (f32[64,1024]{1,0:T(8,128)S(1)}, f32[64,1024]{1,0:T(8,128)S(1)}, u32[]{:S(2)}, u32[]{:S(2)}) collective-permute-start(f32[64,1024]{1,0:T(8,128)S(1)} %get-tuple-element.45.refs_10_), channel_id=1, source_target_pairs={{0,8},{4,12},{8,0},{12,4},{1,9},{5,13},{9,1},{13,5},{2,10},{6,14},... | collective-permute-start | bytes 786440 | tf_op jit(solution)/shard_map/ppermute | solution.py:48
  17.8 1.3 %collective-permute-start = (bf16[32,2048]{1,0:T(8,128)(2,1)S(1)}, bf16[32,2048]{1,0:T(8,128)(2,1)S(1)}, u32[]{:S(2)}, u32[]{:S(2)}) collective-permute-start(bf16[32,2048]{1,0:T(8,128)(2,1)S(1)} %get-tuple-element.43.own), channel_id=1, source_target_pairs={{0,4},{4,0},{8,12},{12,8},{1,5},{5,1},{9,13},{13,9},{2,6},{6,2},{1... | collective-permute-start | bytes 393224 | tf_op jit(solution)/shard_map/ppermute | solution.py:48
  17.8 1.5 %collective-permute-start.3 = (bf16[32,2048]{1,0:T(8,128)(2,1)S(1)}, bf16[32,2048]{1,0:T(8,128)(2,1)S(1)}, u32[]{:S(2)}, u32[]{:S(2)}) collective-permute-start(bf16[32,2048]{1,0:T(8,128)(2,1)S(1)} %collective-permute-done.1.across), channel_id=1, source_target_pairs={{0,4},{4,0},{8,12},{12,8},{1,5},{5,1},{9,13},{13,9},{2,6},{6,2},{1... | collective-permute-start | bytes 393224 | tf_op jit(solution)/shard_map/ppermute | solution.py:48
  21.1 11.1 %collective-permute-start.5 = (f32[192,128]{1,0:T(8,128)S(1)}, f32[192,128]{1,0:T(8,128)S(1)}, u32[]{:S(2)}, u32[]{:S(2)}) collective-permute-start(f32[192,128]{1,0:T(8,128)S(1)} %get-tuple-element.52), channel_id=1, source_target_pairs={{0,3},{1,2},{2,1},{3,0},{4,7},{5,6},{6,5},{7,4},{8,11},{9,10},{10,... | collective-permute-start | bytes 294920 | tf_op jit(solution)/shard_map/ppermute | solution.py:48
  25.2 8.8 %collective-permute-start.6 = (f32[192,128]{1,0:T(8,128)S(1)}, f32[192,128]{1,0:T(8,128)S(1)}, u32[]{:S(2)}, u32[]{:S(2)}) collective-permute-start(f32[192,128]{1,0:T(8,128)S(1)} %get-tuple-element.53), channel_id=1, source_target_pairs={{0,2},{1,3},{2,0},{3,1},{4,6},{5,7},{6,4},{7,5},{8,10},{9,11},{10,... | collective-permute-start | bytes 294920 | tf_op jit(solution)/shard_map/ppermute | solution.py:48
  25.2 8.8 %collective-permute-start.7 = (f32[192,128]{1,0:T(8,128)S(1)}, f32[192,128]{1,0:T(8,128)S(1)}, u32[]{:S(2)}, u32[]{:S(2)}) collective-permute-start(f32[192,128]{1,0:T(8,128)S(1)} %get-tuple-element.54), channel_id=1, source_target_pairs={{0,1},{1,0},{2,3},{3,2},{4,5},{5,4},{6,7},{7,6},{8,9},{9,8},{10,11... | collective-permute-start | bytes 294920 | tf_op jit(solution)/shard_map/ppermute | solution.py:48
  35.1 7.8 %collective-permute-start.10 = (bf16[4,32,1024]{2,1,0:T(8,128)(2,1)S(1)}, bf16[4,32,1024]{2,1,0:T(8,128)(2,1)S(1)}, u32[]{:S(2)}, u32[]{:S(2)}) collective-permute-start(bf16[4,32,1024]{2,1,0:T(8,128)(2,1)S(1)} %queries.1.after.own), channel_id=1, source_target_pairs={{0,8},{4,12},{8,0},{12,4},{1,9},{5,13},{9,1},{13,5},{2,10},{6,14},... | collective-permute-start | bytes 786440 | tf_op jit(solution)/shard_map/ppermute | solution.py:48
  43.0 1.6 %collective-permute-start.11 = (bf16[4,32,1024]{2,1,0:T(8,128)(2,1)S(1)}, bf16[4,32,1024]{2,1,0:T(8,128)(2,1)S(1)}, u32[]{:S(2)}, u32[]{:S(2)}) collective-permute-start(bf16[4,32,1024]{2,1,0:T(8,128)(2,1)S(1)} %sum_queries.1.own.refs_0_), channel_id=1, source_target_pairs={{0,4},{4,0},{8,12},{12,8},{1,5},{5,1},{9,13},{13,9},{2,6},{6,2},{1... | collective-permute-start | bytes 786440 | tf_op jit(solution)/shard_map/ppermute | solution.py:48
  46.2 3.9 %collective-permute-start.12 = (f32[8,72,128]{2,1,0:T(8,128)S(1)}, f32[8,72,128]{2,1,0:T(8,128)S(1)}, u32[]{:S(2)}, u32[]{:S(2)}) collective-permute-start(f32[8,72,128]{2,1,0:T(8,128)S(1)} %attend.3.after), channel_id=1, source_target_pairs={{0,4},{4,0},{8,12},{12,8},{1,5},{5,1},{9,13},{13,9},{2,6},{6,2},{1... | collective-permute-start | bytes 884744 | tf_op jit(solution)/shard_map/ppermute | solution.py:48
  48.0 11.2 %collective-permute-start.13 = (f32[8,72,128]{2,1,0:T(8,128)S(1)}, f32[8,72,128]{2,1,0:T(8,128)S(1)}, u32[]{:S(2)}, u32[]{:S(2)}) collective-permute-start(f32[8,72,128]{2,1,0:T(8,128)S(1)} %attend.4.after), channel_id=1, source_target_pairs={{0,4},{4,0},{8,12},{12,8},{1,5},{5,1},{9,13},{13,9},{2,6},{6,2},{1... | collective-permute-start | bytes 884744 | tf_op jit(solution)/shard_map/ppermute | solution.py:48
  50.4 9.1 %collective-permute-start.14 = (f32[8,72,128]{2,1,0:T(8,128)S(1)}, f32[8,72,128]{2,1,0:T(8,128)S(1)}, u32[]{:S(2)}, u32[]{:S(2)}) collective-permute-start(f32[8,72,128]{2,1,0:T(8,128)S(1)} %merge.1.after), channel_id=1, source_target_pairs={{0,8},{4,12},{8,0},{12,4},{1,9},{5,13},{9,1},{13,5},{2,10},{6,14},... | collective-permute-start | bytes 884744 | tf_op jit(solution)/shard_map/ppermute | solution.py:48
  61.3 11.9 %collective-permute-start.15 = (bf16[32,2048]{1,0:T(8,128)(2,1)S(1)}, bf16[32,2048]{1,0:T(8,128)(2,1)S(1)}, u32[]{:S(2)}, u32[]{:S(2)}) collective-permute-start(bf16[32,2048]{1,0:T(8,128)(2,1)S(1)} %get-tuple-element.75), channel_id=1, source_target_pairs={{0,3},{1,2},{2,1},{3,0},{4,7},{5,6},{6,5},{7,4},{8,11},{9,10},{10,... | collective-permute-start | bytes 393224 | tf_op jit(solution)/shard_map/ppermute | solution.py:48
  66.8 7.9 %collective-permute-start.16 = (bf16[32,2048]{1,0:T(8,128)(2,1)S(1)}, bf16[32,2048]{1,0:T(8,128)(2,1)S(1)}, u32[]{:S(2)}, u32[]{:S(2)}) collective-permute-start(bf16[32,2048]{1,0:T(8,128)(2,1)S(1)} %get-tuple-element.74.refs_2_), channel_id=1, source_target_pairs={{0,2},{1,3},{2,0},{3,1},{4,6},{5,7},{6,4},{7,5},{8,10},{9,11},{10,... | collective-permute-start | bytes 393224 | tf_op jit(solution)/shard_map/ppermute | solution.py:48
  66.8 7.9 %collective-permute-start.17 = (bf16[32,2048]{1,0:T(8,128)(2,1)S(1)}, bf16[32,2048]{1,0:T(8,128)(2,1)S(1)}, u32[]{:S(2)}, u32[]{:S(2)}) collective-permute-start(bf16[32,2048]{1,0:T(8,128)(2,1)S(1)} %get-tuple-element.76), channel_id=1, source_target_pairs={{0,1},{1,0},{2,3},{3,2},{4,5},{5,4},{6,7},{7,6},{8,9},{9,8},{10,11... | collective-permute-start | bytes 393224 | tf_op jit(solution)/shard_map/ppermute | solution.py:48
  74.7 8.3 %collective-permute-start.20 = (bf16[32,2048]{1,0:T(8,128)(2,1)S(1)}, bf16[32,2048]{1,0:T(8,128)(2,1)S(1)}, u32[]{:S(2)}, u32[]{:S(2)}) collective-permute-start(bf16[32,2048]{1,0:T(8,128)(2,1)S(1)} %add.5.refs_0_), channel_id=1, source_target_pairs={{0,3},{1,2},{2,1},{3,0},{4,7},{5,6},{6,5},{7,4},{8,11},{9,10},{10,... | collective-permute-start | bytes 393224 | tf_op jit(solution)/shard_map/ppermute | solution.py:48
  76.8 10.7 %collective-permute-start.18 = (bf16[32,2048]{1,0:T(8,128)(2,1)S(1)}, bf16[32,2048]{1,0:T(8,128)(2,1)S(1)}, u32[]{:S(2)}, u32[]{:S(2)}) collective-permute-start(bf16[32,2048]{1,0:T(8,128)(2,1)S(1)} %add.5.refs_0_), channel_id=1, source_target_pairs={{0,2},{1,3},{2,0},{3,1},{4,6},{5,7},{6,4},{7,5},{8,10},{9,11},{10,... | collective-permute-start | bytes 393224 | tf_op jit(solution)/shard_map/ppermute | solution.py:48
  76.8 10.7 %collective-permute-start.19 = (bf16[32,2048]{1,0:T(8,128)(2,1)S(1)}, bf16[32,2048]{1,0:T(8,128)(2,1)S(1)}, u32[]{:S(2)}, u32[]{:S(2)}) collective-permute-start(bf16[32,2048]{1,0:T(8,128)(2,1)S(1)} %add.5.refs_0_), channel_id=1, source_target_pairs={{0,1},{1,0},{2,3},{3,2},{4,5},{5,4},{6,7},{7,6},{8,9},{9,8},{10,11... | collective-permute-start | bytes 393224 | tf_op jit(solution)/shard_map/ppermute | solution.py:48

commit v6 on v5

--- a/solution.py
+++ b/solution.py
@@ -700,7 +700,7 @@
         for bit in range(tp_width)
     ]
     if packed:
-        more, farthest_wo, fetch_done = fetch((0,), masked, (wo,), columns[-1], (depth, quarter))
+        more, farthest_wo, fetch_done = fetch((0,), masked, (wo,), columns[2], (depth, quarter))
     else:
         more, fetch_done = fetch((0,), masked, ())
     caches.update(more)
@@ -725,7 +725,7 @@
     part_across = attend_to(2, part_beside)
     across = merge(part_across, swap(part_beside_across, "section", 1))
     far = swap(across, "section", 2)
-    hold = dict(right=wo, starts=columns[1:-1], cols=quarter) if packed else {}
+    hold = dict(right=wo, starts=columns[1::2], cols=quarter) if packed else {}
     part_own = attend_to(0, across, *new, cosine, sine, **hold)
     if packed:
         part_own, *held_wo = part_own
@@ -744,7 +744,7 @@
             cost_estimate=QUICK,
             name="finish",
         )(*final, *in_vmem(farthest_wo))
-        farthest = swap(farthest, "tp", tp_width - 1)
+        farthest = swap(farthest, "tp", 2)
         held_wo = held_wo[::-1]
         sent = pl.pallas_call(
             far_kernel,
@@ -755,7 +755,7 @@
             cost_estimate=QUICK,
             name="far_output",
         )(*in_vmem(attended, *held_wo))
-        received = [swap(block, "tp", bit) for block, bit in zip(sent, range(tp_width - 2, 0, -1))]
+        received = [swap(block, "tp", bit) for block, bit in zip(sent, (3, 1))]
         jobs = [(0, columns[0], quarter, depth // CUTS)]
         (total,) = product(
             "own_output", here, (attended,), (wo,), jobs, [F32], after=sent[:1]

time: 89 us -> 91.1 us (1.024)
  waiting for transfers between devices: 15.5 us -> 18.5 us
    ppermute x21, waiting for transfers between devices: 15.5 us -> 18.5 us  [swap(): return jax.tree.map(lambda a: lax.ppermute(a, axis, pairs), value)]
  transfers between devices with their start and end apart: 21 -> 21, of which waited for: 10 -> 12; matrix products, arithmetic and copies ran while one was open for 0% -> 0% of each run, Pallas kernels for 48% -> 47%
where the time goes in v6:
time: 91.1 us; the launch traced here: 91 us
  Pallas kernels  50.8 us (56%)
  starting transfers between devices  21.1 us (23%)
  waiting for transfers between devices  18.5 us (20%)
    ppermute x21, starting transfers between devices, swap(): return jax.tree.map(lambda a: lax.ppermute(a, axis, pairs), value)  21.1 us
    ppermute x21, waiting for transfers between devices, swap(): return jax.tree.map(lambda a: lax.ppermute(a, axis, pairs), value)  18.5 us
    pallas_call x2, Pallas kernels, product(): pl.pallas_call(functools.partial(product_kernel, sizes, jobs), out_shape=...  14.1 us
    pallas_call x2, Pallas kernels, fetch(): pl.pallas_call(functools.partial(fetch_kernel, places, slots, [start] * l...  11.7 us
    pallas_call x1, Pallas kernels, attend(): pl.pallas_call(functools.partial(attend_and_hold_kernel, starts, len(oper...  7.2 us
    pallas_call x3, Pallas kernels, attend(): pl.pallas_call(body, out_shape=out, in_specs=[SMEM] * 2 + [ANYWHERE] + [V...  4.87 us
    pallas_call x1, Pallas kernels, per_device(): pl.pallas_call(far_kernel, out_shape=(block,) * len(held_wo), in_specs=[V...  2.97 us
    pallas_call x2, Pallas kernels, place(): pl.pallas_call(functools.partial(place_kernel, [columns[bit] for bit in b...  2.52 us
  transfers between devices with their start and end apart: 21, of which 12 were waited for; matrix products, arithmetic and copies ran while one was open for 0% of the time, Pallas kernels for 47%

profile of v6, /device:TPU:0, one launch (start us, length us, event | category | flops | bytes accessed | tf_op | source)
XLA Modules:
  0.0 91.0 jit_solution(9105957464837365241)
XLA Ops:
  0.2 2.5 %start.1 = (bf16[32,8192]{1,0:T(8,128)(2,1)S(1)}, bf16[32,2048]{1,0:T(8,128)(2,1)S(1)}, s32[32]{0:T(128)S(1)}, s32[32]{0:T(128)S(1)}, f32[32,128]{1,0:T(8,128)S(...) custom-call(s32[2]{0:T(128)S(1)} %pad_add_fusion.here, s32[32]{0:T(128)} %refs_0_.3, ...), custom_call_target="tpu_custom_call" | custom-call | flops 1 | bytes 1 | tf_op jit(solution)/shard_map/start/pallas_call | solution.py:575
  3.2 1.5 %collective-permute-done.2.refs_1_ = bf16[32,8192]{1,0:T(8,128)(2,1)S(1)} collective-permute-done((bf16[32,8192]{1,0:T(8,128)(2,1)S(1)}, bf16[32,8192]{1,0:T(8,128)(2,1)S(1)}, u32[]{:S(2)}, u32[]{:S(2)}) %collective-permute-start.2) | collective-permute-done | bytes 524320 | tf_op jit(solution)/shard_map/ppermute | solution.py:48
  5.2 2.9 %collective-permute-start.1 = (bf16[32,2048]{1,0:T(8,128)(2,1)S(1)}, bf16[32,2048]{1,0:T(8,128)(2,1)S(1)}, u32[]{:S(2)}, u32[]{:S(2)}) collective-permute-start(bf16[32,2048]{1,0:T(8,128)(2,1)S(1)} %get-tuple-element.43.own), channel_id=1, source_target_pairs={{0,8},{4,12},{8,0},{12,4},{1,9},{5,13},{9,1},{13,5},{2,10},{6,14},... | collective-permute-start | bytes 393224 | tf_op jit(solution)/shard_map/ppermute | solution.py:48
  8.1 9.5 %query.1 = (f32[64,1024]{1,0:T(8,128)S(1)}, f32[64,512]{1,0:T(8,128)S(1)}) custom-call(s32[2]{0:T(128)S(1)} %pad_add_fusion.here, bf16[32,8192]{1,0:T(8,128)(2,1)S(1)} %get-tuple-element.44.refs_0_, bf16[32,8192]{1,0:T(8,128)(2,1)S(1)} %collective-permute-done.2.refs_1_, bf16[8192,2048]{1,0:T(8,128)(2,1)} %refs_2_.3, bf16[8192,512]{1,0:T(8,128)(2,1)} %refs_3_.3), custom_call_target="tpu_custom_call" | custom-call | flops 1 | bytes 1 | tf_op jit(solution)/shard_map/query/pallas_call | solution.py:185
  18.3 0.8 collective-permute-done.beside
  19.3 1.8 %down.2 = (f32[128,128]{1,0:T(8,128)S(1)}, f32[192,128]{1,0:T(8,128)S(1)}, f32[192,128]{1,0:T(8,128)S(1)}, f32[192,128]{1,0:T(8,128)S(1)}) custom-call(s32[2]{0:T(128)S(1)} %pad_add_fusion.here, bf16[32,2048]{1,0:T(8,128)(2,1)S(1)} %get-tuple-element.43.own, bf16[32,2048]{1,0:T(8,128)(2,1)S(1)} %collective-permute-done.beside, ...), custom_call_target="tpu_custom_call" | custom-call | flops 1 | bytes 1 | tf_op jit(solution)/shard_map/down/pallas_call | solution.py:623
  21.1 4.1 %collective-permute-start.5 = (f32[192,128]{1,0:T(8,128)S(1)}, f32[192,128]{1,0:T(8,128)S(1)}, u32[]{:S(2)}, u32[]{:S(2)}) collective-permute-start(f32[192,128]{1,0:T(8,128)S(1)} %get-tuple-element.52), channel_id=1, source_target_pairs={{0,3},{1,2},{2,1},{3,0},{4,7},{5,6},{6,5},{7,4},{8,11},{9,10},{10,... | collective-permute-start | bytes 294920 | tf_op jit(solution)/shard_map/ppermute | solution.py:48
  25.2 0.6 collective-permute-start.7
  25.9 6.3 %fetch.2 = (bf16[8,256,512]{2,1,0:T(8,128)(2,1)S(1)}, bf16[8,256,512]{2,1,0:T(8,128)(2,1)S(1)}, bf16[8,256,512]{2,1,0:T(8,128)(2,1)S(1)}, bf16[8,512,256]{2,1,0:...) custom-call(s32[2]{0:T(128)S(1)} %pad_add_fusion.here, ...), custom_call_target="tpu_custom_call" | custom-call | flops 1 | bytes 1 | tf_op jit(solution)/shard_map/fetch/pallas_call | solution.py:664
  32.2 1.8 %collective-permute-done.6.refs_2_.refs_6_ = f32[192,128]{1,0:T(8,128)S(1)} collective-permute-done((f32[192,128]{1,0:T(8,128)S(1)}, f32[192,128]{1,0:T(8,128)S(1)}, u32[]{:S(2)}, u32[]{:S(2)}) %collective-permute-start.6) | collective-permute-done | bytes 98336 | tf_op jit(solution)/shard_map/ppermute | solution.py:48
  34.0 1.1 %queries.1.after.own = bf16[4,32,1024]{2,1,0:T(8,128)(2,1)S(1)} custom-call(s32[2]{0:T(128)S(1)} %pad_add_fusion.here, f32[8,128]{1,0:T(8,128)S(1)} %get-tuple-element.51.after, f32[128,128]{1,0:T(8,128)S(1)} %get-tuple-element.50.after.refs_0_, f32[192,128]{1,0:T(8,128)S(1)} %collective-permute-done.5.refs_1_.refs_7_, ...), custom_call_target="tpu_custom_call" | custom-call | flops 1 | bytes 1 | tf_op jit(solution)/shard_map/queries/pallas_call | solution.py:686
  35.1 1.6 %collective-permute-start.10 = (bf16[4,32,1024]{2,1,0:T(8,128)(2,1)S(1)}, bf16[4,32,1024]{2,1,0:T(8,128)(2,1)S(1)}, u32[]{:S(2)}, u32[]{:S(2)}) collective-permute-start(bf16[4,32,1024]{2,1,0:T(8,128)(2,1)S(1)} %queries.1.after.own), channel_id=1, source_target_pairs={{0,8},{4,12},{8,0},{12,4},{1,9},{5,13},{9,1},{13,5},{2,10},{6,14},... | collective-permute-start | bytes 786440 | tf_op jit(solution)/shard_map/ppermute | solution.py:48
  36.7 5.4 %fetch.3 = (bf16[8,256,512]{2,1,0:T(8,128)(2,1)S(1)}, bf16[8,512,256]{2,1,0:T(8,128)(2,1)S(1)}, bf16[2048,2048]{1,0:T(8,128)(2,1)S(1)}, f32[8,128]{1,0:T(8,128)S(1)}) custom-call(s32[2]{0:T(128)S(1)} %pad_add_fusion.here, s32[32]{0:T(128)S(1)} %get-tuple-element.42.owners, bf16[32,2,512,256]{3,2,1,0:T(8,128)(2,1)} %cache.3, ...), custom_call_target="tpu_custom_call" | custom-call | flops 1 | bytes 1 | tf_op jit(solution)/shard_map/fetch/pallas_call | solution.py:664
  42.1 0.9 collective-permute-done.10.across
  43.1 1.5 %collective-permute-done.11.after.other.refs_1_ = bf16[4,32,1024]{2,1,0:T(8,128)(2,1)S(1)} collective-permute-done((bf16[4,32,1024]{2,1,0:T(8,128)(2,1)S(1)}, bf16[4,32,1024]{2,1,0:T(8,128)(2,1)S(1)}, u32[]{:S(2)}, u32[]{:S(2)}) %collective-permute-start.11) | collective-permute-done | bytes 262176 | tf_op jit(solution)/shard_map/ppermute | solution.py:48
  44.6 1.6 %attend.3.after = f32[8,72,128]{2,1,0:T(8,128)S(1)} custom-call(s32[2]{0:T(128)S(1)} %pad_add_fusion.here, s32[32]{0:T(128)S(1)} %get-tuple-element.41.limits, bf16[4,32,1024]{2,1,0:T(8,128)(2,1)S(1)} %collective-permute-done.11.after.other.refs_1_, bf16[4,32,1024]{2,1,0:T(8,128)(2,1)S(1)} %sum_queries.1.own.refs_0_, ...), custom_call_target="tpu_custom_call" | custom-call | flops 1 | bytes 1 | tf_op jit(solution)/shard_map/attend/pallas_call | solution.py:507
  46.4 1.6 %attend.4.after = f32[8,72,128]{2,1,0:T(8,128)S(1)} custom-call(s32[2]{0:T(128)S(1)} %pad_add_fusion.here, s32[32]{0:T(128)S(1)} %get-tuple-element.41.limits, f32[8,72,128]{2,1,0:T(8,128)S(1)} %attend.3.after, bf16[4,32,1024]{2,1,0:T(8,128)(2,1)S(1)} %sum_queries.1.own.refs_0_, bf16[4,32,1024]{2,1,0:T(8,128)(2,1)S(1)} %collective-permute-done.11.after.other.refs_1_, ...), custom_call_target="tpu_custom_call" | custom-call | flops 1 | bytes 1 | tf_op jit(solution)/shard_map/attend/pallas_call | solution.py:507
  48.4 1.7 %attend.5.a = f32[8,72,128]{2,1,0:T(8,128)S(1)} custom-call(s32[2]{0:T(128)S(1)} %pad_add_fusion.here, s32[32]{0:T(128)S(1)} %get-tuple-element.41.limits, f32[8,72,128]{2,1,0:T(8,128)S(1)} %attend.4.after, bf16[4,32,1024]{2,1,0:T(8,128)(2,1)S(1)} %sum_queries.1.own.refs_0_, bf16[4,32,1024]{2,1,0:T(8,128)(2,1)S(1)} %collective-permute-done.11.after.other.refs_1_, ...), custom_call_target="tpu_custom_call" | custom-call | flops 1 | bytes 1 | tf_op jit(solution)/shard_map/attend/pallas_call | solution.py:507
  50.4 1.6 %collective-permute-start.14 = (f32[8,72,128]{2,1,0:T(8,128)S(1)}, f32[8,72,128]{2,1,0:T(8,128)S(1)}, u32[]{:S(2)}, u32[]{:S(2)}) collective-permute-start(f32[8,72,128]{2,1,0:T(8,128)S(1)} %merge.1.after), channel_id=1, source_target_pairs={{0,8},{4,12},{8,0},{12,4},{1,9},{5,13},{9,1},{13,5},{2,10},{6,14},... | collective-permute-start | bytes 884744 | tf_op jit(solution)/shard_map/ppermute | solution.py:48
  52.0 7.2 %attend_hold.1 = (f32[8,72,128]{2,1,0:T(8,128)S(1)}, bf16[2048,2048]{1,0:T(8,128)(2,1)S(1)}, bf16[2048,2048]{1,0:T(8,128)(2,1)S(1)}) custom-call(s32[2]{0:T(128)S(1)} %pad_add_fusion.here, s32[32]{0:T(128)S(1)} %get-tuple-element.41.limits, f32[8,72,128]{2,1,0:T(8,128)S(1)} %merge.1.after, bf16[2048,8192]{1,0:T(8,128)(2,1)} %refs_1_.3, ...), custom_call_target="tpu_custom_call" | custom-call | flops 1 | bytes 1 | tf_op jit(solution)/shard_map/attend_hold/pallas_call | solution.py:518
  59.6 1.7 %finish.1 = (bf16[32,2048]{1,0:T(8,128)(2,1)S(1)}, bf16[32,2048]{1,0:T(8,128)(2,1)S(1)}) custom-call(f32[8,72,128]{2,1,0:T(8,128)S(1)} %get-tuple-element.69.a, f32[8,72,128]{2,1,0:T(8,128)S(1)} %collective-permute-done.13.b, f32[8,72,128]{2,1,0:T(8,128)S(1)} %collective-permute-done.14.c, bf16[2048,2048]{1,0:T(8,128)(2,1)S(1)} %get-tuple-element.70.held_right), custom_call_target="tpu_custom_call" | custom-call | flops 1 | bytes 1 | tf_op jit(solution)/shard_map/finish/pallas_call | solution.py:737
  61.3 0.8 collective-permute-start.15
  62.1 3.0 %far_output.1 = (bf16[32,2048]{1,0:T(8,128)(2,1)S(1)}, bf16[32,2048]{1,0:T(8,128)(2,1)S(1)}) custom-call(bf16[32,2048]{1,0:T(8,128)(2,1)S(1)} %get-tuple-element.71.left.refs_0_, bf16[2048,2048]{1,0:T(8,128)(2,1)S(1)} %get-tuple-element.72.refs_0_, bf16[2048,2048]{1,0:T(8,128)(2,1)S(1)} %get-tuple-element.73.refs_1_), custom_call_target="tpu_custom_call" | custom-call | flops 1 | bytes 1 | tf_op jit(solution)/shard_map/far_output/pallas_call | solution.py:749
  65.1 2.1 %collective-permute-start.16 = (bf16[32,2048]{1,0:T(8,128)(2,1)S(1)}, bf16[32,2048]{1,0:T(8,128)(2,1)S(1)}, u32[]{:S(2)}, u32[]{:S(2)}) collective-permute-start(bf16[32,2048]{1,0:T(8,128)(2,1)S(1)} %get-tuple-element.74.refs_2_), channel_id=1, source_target_pairs={{0,3},{1,2},{2,1},{3,0},{4,7},{5,6},{6,5},{7,4},{8,11},{9,10},{10,... | collective-permute-start | bytes 393224 | tf_op jit(solution)/shard_map/ppermute | solution.py:48
  67.8 4.5 %own_output.1.refs_0_ = f32[32,2048]{1,0:T(8,128)S(1)} custom-call(s32[2]{0:T(128)S(1)} %pad_add_fusion.here, bf16[32,2048]{1,0:T(8,128)(2,1)S(1)} %get-tuple-element.71.left.refs_0_, bf16[2048,8192]{1,0:T(8,128)(2,1)} %refs_1_.3, bf16[32,2048]{1,0:T(8,128)(2,1)S(1)} %get-tuple-element.74.refs_2_), custom_call_target="tpu_custom_call" | custom-call | flops 1 | bytes 1 | tf_op jit(solution)/shard_map/own_output/pallas_call | solution.py:185
  73.0 2.5 %collective-permute-done.17.refs_2_ = bf16[32,2048]{1,0:T(8,128)(2,1)S(1)} collective-permute-done((bf16[32,2048]{1,0:T(8,128)(2,1)S(1)}, bf16[32,2048]{1,0:T(8,128)(2,1)S(1)}, u32[]{:S(2)}, u32[]{:S(2)}) %collective-permute-start.17) | collective-permute-done | bytes 131104 | tf_op jit(solution)/shard_map/ppermute | solution.py:48
  75.6 1.8 %collective-permute-start.20 = (bf16[32,2048]{1,0:T(8,128)(2,1)S(1)}, bf16[32,2048]{1,0:T(8,128)(2,1)S(1)}, u32[]{:S(2)}, u32[]{:S(2)}) collective-permute-start(bf16[32,2048]{1,0:T(8,128)(2,1)S(1)} %add.5.refs_0_), channel_id=1, source_target_pairs={{0,3},{1,2},{2,1},{3,0},{4,7},{5,6},{6,5},{7,4},{8,11},{9,10},{10,... | collective-permute-start | bytes 393224 | tf_op jit(solution)/shard_map/ppermute | solution.py:48
  77.7 2.3 %collective-permute-start.19 = (bf16[32,2048]{1,0:T(8,128)(2,1)S(1)}, bf16[32,2048]{1,0:T(8,128)(2,1)S(1)}, u32[]{:S(2)}, u32[]{:S(2)}) collective-permute-start(bf16[32,2048]{1,0:T(8,128)(2,1)S(1)} %add.5.refs_0_), channel_id=1, source_target_pairs={{0,1},{1,0},{2,3},{3,2},{4,5},{5,4},{6,7},{7,6},{8,9},{9,8},{10,11... | collective-permute-start | bytes 393224 | tf_op jit(solution)/shard_map/ppermute | solution.py:48
  80.0 3.9 %collective-permute-done.20.refs_1_ = bf16[32,2048]{1,0:T(8,128)(2,1)S(1)} collective-permute-done((bf16[32,2048]{1,0:T(8,128)(2,1)S(1)}, bf16[32,2048]{1,0:T(8,128)(2,1)S(1)}, u32[]{:S(2)}, u32[]{:S(2)}) %collective-permute-start.20) | collective-permute-done | bytes 131104 | tf_op jit(solution)/shard_map/ppermute | solution.py:48
  83.9 1.3 %place.2.refs_2_ = bf16[32,8192]{1,0:T(8,128)(2,1)} custom-call(s32[2]{0:T(128)S(1)} %pad_add_fusion.here, bf16[32,2048]{1,0:T(8,128)(2,1)S(1)} %add.5.refs_0_, bf16[32,2048]{1,0:T(8,128)(2,1)S(1)} %collective-permute-done.20.refs_1_), custom_call_target="tpu_custom_call" | custom-call | flops 1 | bytes 1 | tf_op jit(solution)/shard_map/place/pallas_call | solution.py:767
  85.2 4.3 %collective-permute-done.18.refs_0_ = bf16[32,2048]{1,0:T(8,128)(2,1)S(1)} collective-permute-done((bf16[32,2048]{1,0:T(8,128)(2,1)S(1)}, bf16[32,2048]{1,0:T(8,128)(2,1)S(1)}, u32[]{:S(2)}, u32[]{:S(2)}) %collective-permute-start.18) | collective-permute-done | bytes 131104 | tf_op jit(solution)/shard_map/ppermute | solution.py:48
  89.5 1.3 %place.3 = bf16[32,8192]{1,0:T(8,128)(2,1)} custom-call(s32[2]{0:T(128)S(1)} %pad_add_fusion.here, bf16[32,2048]{1,0:T(8,128)(2,1)S(1)} %collective-permute-done.18.refs_0_, bf16[32,2048]{1,0:T(8,128)(2,1)S(1)} %collective-permute-done.19.refs_1_, bf16[32,8192]{1,0:T(8,128)(2,1)} %place.2.refs_2_), custom_call_target="tpu_custom_call", output_to_operand_aliasing={{}: (3, {})} | custom-call | flops 1 | bytes 1 | tf_op jit(solution)/shard_map/place/pallas_call | solution.py:767
  (34 shorter events, 5.1 us)
Async XLA Ops:
  2.6 2.1 %collective-permute-start.2 = (bf16[32,8192]{1,0:T(8,128)(2,1)S(1)}, bf16[32,8192]{1,0:T(8,128)(2,1)S(1)}, u32[]{:S(2)}, u32[]{:S(2)}) collective-permute-start(bf16[32,8192]{1,0:T(8,128)(2,1)S(1)} %get-tuple-element.44.refs_0_), channel_id=1, source_target_pairs={{0,4},{4,0},{8,12},{12,8},{1,5},{5,1},{9,13},{13,9},{2,6},{6,2},{1... | collective-permute-start | bytes 1572872 | tf_op jit(solution)/shard_map/ppermute | solution.py:48
  4.7 14.6 %collective-permute-start.4 = (bf16[4,2048,128]{2,1,0:T(8,128)(2,1)}, bf16[4,2048,128]{2,1,0:T(8,128)(2,1)S(1)}, u32[]{:S(2)}, u32[]{:S(2)}) collective-permute-start(bf16[4,2048,128]{2,1,0:T(8,128)(2,1)} %down.3), channel_id=1, source_target_pairs={{0,4},{4,0},{8,12},{12,8},{1,5},{5,1},{9,13},{13,9},{2,6},{6,2},{1... | collective-permute-start | bytes 6291464 | tf_op jit(solution)/shard_map/ppermute | solution.py:48
  5.1 27.2 %collective-permute-start.8 = (bf16[4,128,2048]{2,1,0:T(8,128)(2,1)}, bf16[4,128,2048]{2,1,0:T(8,128)(2,1)S(1)}, u32[]{:S(2)}, u32[]{:S(2)}) collective-permute-start(bf16[4,128,2048]{2,1,0:T(8,128)(2,1)} %refs_0_.4), channel_id=1, source_target_pairs={{0,4},{4,0},{8,12},{12,8},{1,5},{5,1},{9,13},{13,9},{2,6},{6,2},{1... | collective-permute-start | bytes 6291464 | tf_op jit(solution)/shard_map/ppermute | solution.py:48
  5.2 14.1 %copy-start = (bf16[4,2048,128]{2,1,0:T(8,128)(2,1)S(1)}, bf16[4,2048,128]{2,1,0:T(8,128)(2,1)}, u32[]{:S(2)}) copy-start(bf16[4,2048,128]{2,1,0:T(8,128)(2,1)} %down.3) | copy-start | bytes 6291460
  5.2 12.6 %collective-permute-start.1 = (bf16[32,2048]{1,0:T(8,128)(2,1)S(1)}, bf16[32,2048]{1,0:T(8,128)(2,1)S(1)}, u32[]{:S(2)}, u32[]{:S(2)}) collective-permute-start(bf16[32,2048]{1,0:T(8,128)(2,1)S(1)} %get-tuple-element.43.own), channel_id=1, source_target_pairs={{0,8},{4,12},{8,0},{12,4},{1,9},{5,13},{9,1},{13,5},{2,10},{6,14},... | collective-permute-start | bytes 393224 | tf_op jit(solution)/shard_map/ppermute | solution.py:48
  17.6 14.6 %collective-permute-start.9 = (f32[64,1024]{1,0:T(8,128)S(1)}, f32[64,1024]{1,0:T(8,128)S(1)}, u32[]{:S(2)}, u32[]{:S(2)}) collective-permute-start(f32[64,1024]{1,0:T(8,128)S(1)} %get-tuple-element.45.refs_10_), channel_id=1, source_target_pairs={{0,8},{4,12},{8,0},{12,4},{1,9},{5,13},{9,1},{13,5},{2,10},{6,14},... | collective-permute-start | bytes 786440 | tf_op jit(solution)/shard_map/ppermute | solution.py:48
  17.8 1.3 %collective-permute-start = (bf16[32,2048]{1,0:T(8,128)(2,1)S(1)}, bf16[32,2048]{1,0:T(8,128)(2,1)S(1)}, u32[]{:S(2)}, u32[]{:S(2)}) collective-permute-start(bf16[32,2048]{1,0:T(8,128)(2,1)S(1)} %get-tuple-element.43.own), channel_id=1, source_target_pairs={{0,4},{4,0},{8,12},{12,8},{1,5},{5,1},{9,13},{13,9},{2,6},{6,2},{1... | collective-permute-start | bytes 393224 | tf_op jit(solution)/shard_map/ppermute | solution.py:48
  17.8 1.5 %collective-permute-start.3 = (bf16[32,2048]{1,0:T(8,128)(2,1)S(1)}, bf16[32,2048]{1,0:T(8,128)(2,1)S(1)}, u32[]{:S(2)}, u32[]{:S(2)}) collective-permute-start(bf16[32,2048]{1,0:T(8,128)(2,1)S(1)} %collective-permute-done.1.across), channel_id=1, source_target_pairs={{0,4},{4,0},{8,12},{12,8},{1,5},{5,1},{9,13},{13,9},{2,6},{6,2},{1... | collective-permute-start | bytes 393224 | tf_op jit(solution)/shard_map/ppermute | solution.py:48
  21.1 11.1 %collective-permute-start.5 = (f32[192,128]{1,0:T(8,128)S(1)}, f32[192,128]{1,0:T(8,128)S(1)}, u32[]{:S(2)}, u32[]{:S(2)}) collective-permute-start(f32[192,128]{1,0:T(8,128)S(1)} %get-tuple-element.52), channel_id=1, source_target_pairs={{0,3},{1,2},{2,1},{3,0},{4,7},{5,6},{6,5},{7,4},{8,11},{9,10},{10,... | collective-permute-start | bytes 294920 | tf_op jit(solution)/shard_map/ppermute | solution.py:48
  25.2 8.8 %collective-permute-start.6 = (f32[192,128]{1,0:T(8,128)S(1)}, f32[192,128]{1,0:T(8,128)S(1)}, u32[]{:S(2)}, u32[]{:S(2)}) collective-permute-start(f32[192,128]{1,0:T(8,128)S(1)} %get-tuple-element.53), channel_id=1, source_target_pairs={{0,2},{1,3},{2,0},{3,1},{4,6},{5,7},{6,4},{7,5},{8,10},{9,11},{10,... | collective-permute-start | bytes 294920 | tf_op jit(solution)/shard_map/ppermute | solution.py:48
  25.2 8.8 %collective-permute-start.7 = (f32[192,128]{1,0:T(8,128)S(1)}, f32[192,128]{1,0:T(8,128)S(1)}, u32[]{:S(2)}, u32[]{:S(2)}) collective-permute-start(f32[192,128]{1,0:T(8,128)S(1)} %get-tuple-element.54), channel_id=1, source_target_pairs={{0,1},{1,0},{2,3},{3,2},{4,5},{5,4},{6,7},{7,6},{8,9},{9,8},{10,11... | collective-permute-start | bytes 294920 | tf_op jit(solution)/shard_map/ppermute | solution.py:48
  35.1 7.8 %collective-permute-start.10 = (bf16[4,32,1024]{2,1,0:T(8,128)(2,1)S(1)}, bf16[4,32,1024]{2,1,0:T(8,128)(2,1)S(1)}, u32[]{:S(2)}, u32[]{:S(2)}) collective-permute-start(bf16[4,32,1024]{2,1,0:T(8,128)(2,1)S(1)} %queries.1.after.own), channel_id=1, source_target_pairs={{0,8},{4,12},{8,0},{12,4},{1,9},{5,13},{9,1},{13,5},{2,10},{6,14},... | collective-permute-start | bytes 786440 | tf_op jit(solution)/shard_map/ppermute | solution.py:48
  43.0 1.6 %collective-permute-start.11 = (bf16[4,32,1024]{2,1,0:T(8,128)(2,1)S(1)}, bf16[4,32,1024]{2,1,0:T(8,128)(2,1)S(1)}, u32[]{:S(2)}, u32[]{:S(2)}) collective-permute-start(bf16[4,32,1024]{2,1,0:T(8,128)(2,1)S(1)} %sum_queries.1.own.refs_0_), channel_id=1, source_target_pairs={{0,4},{4,0},{8,12},{12,8},{1,5},{5,1},{9,13},{13,9},{2,6},{6,2},{1... | collective-permute-start | bytes 786440 | tf_op jit(solution)/shard_map/ppermute | solution.py:48
  46.2 3.9 %collective-permute-start.12 = (f32[8,72,128]{2,1,0:T(8,128)S(1)}, f32[8,72,128]{2,1,0:T(8,128)S(1)}, u32[]{:S(2)}, u32[]{:S(2)}) collective-permute-start(f32[8,72,128]{2,1,0:T(8,128)S(1)} %attend.3.after), channel_id=1, source_target_pairs={{0,4},{4,0},{8,12},{12,8},{1,5},{5,1},{9,13},{13,9},{2,6},{6,2},{1... | collective-permute-start | bytes 884744 | tf_op jit(solution)/shard_map/ppermute | solution.py:48
  48.0 11.2 %collective-permute-start.13 = (f32[8,72,128]{2,1,0:T(8,128)S(1)}, f32[8,72,128]{2,1,0:T(8,128)S(1)}, u32[]{:S(2)}, u32[]{:S(2)}) collective-permute-start(f32[8,72,128]{2,1,0:T(8,128)S(1)} %attend.4.after), channel_id=1, source_target_pairs={{0,4},{4,0},{8,12},{12,8},{1,5},{5,1},{9,13},{13,9},{2,6},{6,2},{1... | collective-permute-start | bytes 884744 | tf_op jit(solution)/shard_map/ppermute | solution.py:48
  50.4 9.1 %collective-permute-start.14 = (f32[8,72,128]{2,1,0:T(8,128)S(1)}, f32[8,72,128]{2,1,0:T(8,128)S(1)}, u32[]{:S(2)}, u32[]{:S(2)}) collective-permute-start(f32[8,72,128]{2,1,0:T(8,128)S(1)} %merge.1.after), channel_id=1, source_target_pairs={{0,8},{4,12},{8,0},{12,4},{1,9},{5,13},{9,1},{13,5},{2,10},{6,14},... | collective-permute-start | bytes 884744 | tf_op jit(solution)/shard_map/ppermute | solution.py:48
  61.3 11.1 %collective-permute-start.15 = (bf16[32,2048]{1,0:T(8,128)(2,1)S(1)}, bf16[32,2048]{1,0:T(8,128)(2,1)S(1)}, u32[]{:S(2)}, u32[]{:S(2)}) collective-permute-start(bf16[32,2048]{1,0:T(8,128)(2,1)S(1)} %get-tuple-element.75), channel_id=1, source_target_pairs={{0,2},{1,3},{2,0},{3,1},{4,6},{5,7},{6,4},{7,5},{8,10},{9,11},{10,... | collective-permute-start | bytes 393224 | tf_op jit(solution)/shard_map/ppermute | solution.py:48
  65.1 7.9 %collective-permute-start.16 = (bf16[32,2048]{1,0:T(8,128)(2,1)S(1)}, bf16[32,2048]{1,0:T(8,128)(2,1)S(1)}, u32[]{:S(2)}, u32[]{:S(2)}) collective-permute-start(bf16[32,2048]{1,0:T(8,128)(2,1)S(1)} %get-tuple-element.74.refs_2_), channel_id=1, source_target_pairs={{0,3},{1,2},{2,1},{3,0},{4,7},{5,6},{6,5},{7,4},{8,11},{9,10},{10,... | collective-permute-start | bytes 393224 | tf_op jit(solution)/shard_map/ppermute | solution.py:48
  67.2 8.3 %collective-permute-start.17 = (bf16[32,2048]{1,0:T(8,128)(2,1)S(1)}, bf16[32,2048]{1,0:T(8,128)(2,1)S(1)}, u32[]{:S(2)}, u32[]{:S(2)}) collective-permute-start(bf16[32,2048]{1,0:T(8,128)(2,1)S(1)} %get-tuple-element.76), channel_id=1, source_target_pairs={{0,1},{1,0},{2,3},{3,2},{4,5},{5,4},{6,7},{7,6},{8,9},{9,8},{10,11... | collective-permute-start | bytes 393224 | tf_op jit(solution)/shard_map/ppermute | solution.py:48
  75.6 8.3 %collective-permute-start.20 = (bf16[32,2048]{1,0:T(8,128)(2,1)S(1)}, bf16[32,2048]{1,0:T(8,128)(2,1)S(1)}, u32[]{:S(2)}, u32[]{:S(2)}) collective-permute-start(bf16[32,2048]{1,0:T(8,128)(2,1)S(1)} %add.5.refs_0_), channel_id=1, source_target_pairs={{0,3},{1,2},{2,1},{3,0},{4,7},{5,6},{6,5},{7,4},{8,11},{9,10},{10,... | collective-permute-start | bytes 393224 | tf_op jit(solution)/shard_map/ppermute | solution.py:48
  77.4 12.2 %collective-permute-start.18 = (bf16[32,2048]{1,0:T(8,128)(2,1)S(1)}, bf16[32,2048]{1,0:T(8,128)(2,1)S(1)}, u32[]{:S(2)}, u32[]{:S(2)}) collective-permute-start(bf16[32,2048]{1,0:T(8,128)(2,1)S(1)} %add.5.refs_0_), channel_id=1, source_target_pairs={{0,2},{1,3},{2,0},{3,1},{4,6},{5,7},{6,4},{7,5},{8,10},{9,11},{10,... | collective-permute-start | bytes 393224 | tf_op jit(solution)/shard_map/ppermute | solution.py:48
  77.7 11.8 %collective-permute-start.19 = (bf16[32,2048]{1,0:T(8,128)(2,1)S(1)}, bf16[32,2048]{1,0:T(8,128)(2,1)S(1)}, u32[]{:S(2)}, u32[]{:S(2)}) collective-permute-start(bf16[32,2048]{1,0:T(8,128)(2,1)S(1)} %add.5.refs_0_), channel_id=1, source_target_pairs={{0,1},{1,0},{2,3},{3,2},{4,5},{5,4},{6,7},{7,6},{8,9},{9,8},{10,11... | collective-permute-start | bytes 393224 | tf_op jit(solution)/shard_map/ppermute | solution.py:48
